TPU v7x, 512 devices: a whole 4x4x16 slice. The times are simulated.
512 devices in a mesh: tok: 2 (over core), head: 16 (over y, x), exp: 16 (over z).
Axes of the slice: x: 4, y: 4, z: 16, core: 2. Of those that a mesh axis runs over, the one named last changes fastest.
Arguments:
- context: bfloat16 [16, 64, 4096], P('exp', 'tok', 'head'), may hold values from -6 to 6
- out_proj: bfloat16 [4096, 4096], P('head', 'exp'), may hold values from -0.125 to 0.125
- stream: float32 [16, 64, 4096], P('exp', 'tok', 'head'), may hold values from -75 to 75
- norm_gain: float32 [4096], replicated, may hold values from 0.1 to 1.9
- expert_ids: int32 [16, 64, 8], P('exp', 'tok'), may hold values from 0 to 31, as said below
- slot_ids: int32 [16, 64, 8], P('exp', 'tok'), may hold values from -1 to 11, as said below
- gate_probs: float32 [16, 64, 8], P('exp', 'tok'), may hold values from 0.02 to 0.3
- w_gate: bfloat16 [32, 3072, 4096], P(('tok', 'exp'), 'head'), may hold values from -0.09375 to 0.09375
- w_up: bfloat16 [32, 3072, 4096], P(('tok', 'exp'), 'head'), may hold values from -0.09375 to 0.09375
- w_down: bfloat16 [32, 3072, 4096], P(('tok', 'exp'), 'head'), may hold values from -0.15625 to 0.15625
Outputs:
- mixed: float32 [16, 64, 4096], P('exp', 'tok', 'head')
Inputs may be any that keep to these rules, and one draw needn't show every extreme that they name: `expert_ids`: each token names 8 different experts. `slot_ids`: within a block of 32 consecutive tokens of one image, the choices of one expert take slots 0, 1, 2, ... in token order until its 12 slots are full, later ones get -1; in every block some expert fills all 12 slots.
All inputs are finite; a program needn't handle non-finite values.
Results may differ from a plain program's by a relative error of at most 0.0034.
Values may be sent and summed in bfloat16 or wider, within the bound.
No kernel may reach another device: no remote copies, remote signals or barrier semaphores. Data moves between devices by JAX's collectives and lax.ppermute only.
A program may use at most 64 MiB of HBM per device.

v0:
```python
import jax
import jax.numpy as jnp
from jax import lax
from jax.sharding import Mesh
from jax.sharding import PartitionSpec as P

EXPERTS = 32
TOP = 8
CAP = 12
HEAD = ("head_0", "head_1")


eps_value = 1e-05


def cut_along(x, dim, count):
    shape = x.shape
    pieces = x.reshape(*shape[:dim], count, shape[dim] // count, *shape[dim + 1 :])
    return jnp.moveaxis(pieces, dim, 0)


def sum_at_owner(x, axis, dim):
    pieces = cut_along(x, dim, lax.axis_size(axis))
    arrived = lax.all_to_all(pieces, axis, split_axis=0, concat_axis=0, tiled=True)
    return arrived.astype(jnp.float32).sum(axis=0)


def over_axes(x, axes):
    for axis in axes:
        x = lax.psum(x, axis)
    return x


def gather_axes(x, axes, dim):
    result = x
    for number in range(len(axes) - 1, -1, -1):
        result = lax.all_gather(result, axes[number], axis=dim, tiled=True)
    return result


def on_device(
    context, out_proj, stream, norm_gain, expert_ids, slot_ids, gate_probs, w_gate, w_up, w_down
):
    local_context = context[0]
    own_stream = stream[0]
    col_width = own_stream.shape[1]
    full_width = col_width * lax.axis_size(HEAD)
    col_start = lax.axis_index(HEAD) * col_width
    partial_value = jnp.dot(
        local_context,
        lax.all_gather(out_proj, "exp", axis=1, tiled=True),
        preferred_element_type=jnp.float32,
    )
    resid_own = sum_at_owner(partial_value.astype(jnp.bfloat16), HEAD, 1) + own_stream
    total_sq = over_axes(jnp.sum(resid_own * resid_own, axis=1, keepdims=True), HEAD)
    gain_own = lax.dynamic_slice_in_dim(norm_gain, col_start, col_width, 0)
    normed_own = (resid_own * lax.rsqrt(total_sq / full_width + eps_value) * gain_own).astype(
        jnp.bfloat16
    )
    choice_ids = expert_ids[0]
    choice_slots = slot_ids[0]
    weights = gate_probs[0]
    spill_slot = EXPERTS * CAP
    target = jnp.where(choice_slots >= 0, choice_ids * CAP + choice_slots, spill_slot)
    outgoing = (
        jnp.zeros((spill_slot + 1, col_width), jnp.bfloat16)
        .at[target.reshape(-1)]
        .set(jnp.repeat(normed_own, TOP, axis=0))
    )
    outgoing = outgoing[:spill_slot].reshape(EXPERTS, CAP, col_width)
    tok_count = lax.axis_size("tok")
    groups = tok_count * lax.axis_size("exp")
    local_experts = w_gate.shape[0]
    arrived = lax.all_to_all(outgoing, ("tok", "exp"), split_axis=0, concat_axis=0, tiled=True)
    arrived = arrived.reshape(groups, local_experts, CAP, col_width)
    piece = gather_axes(arrived, HEAD, 3)
    gate_more = jnp.einsum("slcd,lhd->slch", piece, w_gate, preferred_element_type=jnp.float32)
    up_more = jnp.einsum("slcd,lhd->slch", piece, w_up, preferred_element_type=jnp.float32)
    hidden = (jax.nn.silu(gate_more) * up_more).astype(jnp.bfloat16)
    produced = jnp.einsum(
        "slch,lhd->slcd", hidden, w_down, preferred_element_type=jnp.float32
    ).astype(jnp.bfloat16)
    widened = lax.optimization_barrier(produced).astype(jnp.float32)
    summed = sum_at_owner(widened.astype(jnp.bfloat16), HEAD, 3)
    returned_share = lax.all_to_all(
        summed.reshape(EXPERTS, CAP, col_width).astype(jnp.bfloat16),
        ("tok", "exp"),
        split_axis=0,
        concat_axis=0,
        tiled=True,
    ).astype(jnp.float32)
    lookup_share = jnp.concatenate(
        [returned_share.reshape(spill_slot, col_width), jnp.zeros((1, col_width), jnp.float32)],
        axis=0,
    )
    picked_share = lookup_share[target]
    expert_own = jnp.sum(picked_share * weights[:, :, None], axis=1)
    return (resid_own + expert_own)[None]


def solution(mesh):
    split = Mesh(
        mesh.devices.reshape(mesh.shape["tok"], 4, 4, mesh.shape["exp"]),
        ("tok", "head_0", "head_1", "exp"),
    )
    in_specs = (
        P("exp", "tok", HEAD),
        P(HEAD, "exp"),
        P("exp", "tok", HEAD),
        P(),
        P("exp", "tok", None),
        P("exp", "tok", None),
        P("exp", "tok", None),
        P(("tok", "exp"), HEAD, None),
        P(("tok", "exp"), HEAD, None),
        P(("tok", "exp"), HEAD, None),
    )
    out_specs = P("exp", "tok", HEAD)
    return jax.shard_map(
        on_device, mesh=split, in_specs=in_specs, out_specs=out_specs, check_vma=False
    )
```

profile of v0, /device:TPU:1, one launch (start us, length us, event | category | flops | bytes accessed | tf_op | source)
XLA Modules:
  0.0 316.5 jit_solution(14243525346558986769)
XLA Ops:
  6.5 0.0 copy-start
  6.5 0.0 copy-start.4
  6.5 0.0 copy-start.3
  6.5 0.0 copy-start.1
  6.5 0.0 all-gather.5.cloned.1.call-start
  6.6 0.7 all-gather.5.cloned.1.call-update
  7.3 76.2 %all-gather.5.cloned.1.call-done = bf16[256,4096]{1,0:T(8,128)(2,1)} async-done(((bf16[256,256]{1,0:T(8,128)(2,1)}), bf16[256,4096]{1,0:T(8,128)(2,1)}) %all-gather.5.cloned.1.call-update) | async-done | bytes 2097168 | tf_op jit(solution)/shard_map/all_gather | solution.py:51
  83.5 2.1 convolution_convert_fusion.1
  85.6 0.7 copy.38
  86.3 6.5 %all-to-all-start = ((bf16[16,32,256]{2,1,0:T(8,128)(2,1)}), bf16[16,32,256]{2,1,0:T(8,128)(2,1)S(1)}, u32[]{:S(2)}, u32[]{:S(2)}) async-start(bf16[16,32,256]{2,1,0:T(8,128)(2,1)} %bitcast.101), calls=%async_computation | async-start | bytes 524288 | tf_op jit(solution)/shard_map/all_to_all | solution.py:24
  92.8 0.0 all-gather.7.cloned.1.call-start
  92.9 0.0 copy-done.4
  92.9 0.0 copy-done.3
  92.9 0.1 copy.25
  93.0 0.1 select_n.49
  93.1 0.8 dynamic_slice.3
  93.9 6.5 %all-to-all-done = bf16[16,32,256]{2,1,0:T(8,128)(2,1)S(1)} async-done(((bf16[16,32,256]{2,1,0:T(8,128)(2,1)}), bf16[16,32,256]{2,1,0:T(8,128)(2,1)S(1)}, u32[]{:S(2)}, u32[]{:S(2)}) %all-to-all-start) | async-done | bytes 262176 | tf_op jit(solution)/shard_map/all_to_all | solution.py:24
  100.4 0.0 copy-done.1
  100.4 0.1 multiply_reduce_fusion
  100.5 6.6 %psum.14 = f32[32,1]{0,1:T(1,128)S(1)} all-reduce(f32[32,1]{0,1:T(1,128)S(1)} %bitcast.107), channel_id=1, replica_groups=mesh['tok'=2,'head_0'=4,'head_1'=4,'exp'=16] {'head_0'}, use_global_device_ids=true, to_apply=%region_2.0 | all-reduce | flops 32 | bytes 256 | tf_op jit(solution)/shard_map/psum | solution.py:30
  107.1 7.0 %psum.15 = f32[32,1]{0,1:T(1,128)S(1)} all-reduce(f32[32,1]{0,1:T(1,128)S(1)} %psum.14), channel_id=1, replica_groups=mesh['tok'=2,'head_0'=4,'head_1'=4,'exp'=16] {'head_1'}, use_global_device_ids=true, to_apply=%region_3.0 | all-reduce | flops 32 | bytes 256 | tf_op jit(solution)/shard_map/psum | solution.py:30
  114.1 0.1 multiply_convert_fusion
  114.2 1.5 scatter_custom_fusion
  115.8 0.0 copy-start.5
  115.8 44.8 %all_to_all.20 = bf16[32,12,256]{2,1,0:T(8,128)(2,1)S(1)} all-to-all(bf16[32,12,256]{2,1,0:T(8,128)(2,1)S(1)} %reshape.147), channel_id=1, replica_groups=mesh['tok'=2,'head_0'=4,'head_1'=4,'exp'=16] {'tok','exp'}, dimensions={0} | all-to-all | bytes 393216 | tf_op jit(solution)/shard_map/all_to_all | solution.py:74
  160.6 0.1 copy.26
  160.6 13.4 %all-gather = bf16[32,12,1024]{2,0,1:T(8,128)(2,1)} all-gather(bf16[32,12,256]{2,0,1:T(8,128)(2,1)S(1)} %copy.26), channel_id=2, replica_groups=mesh['tok'=2,'head_0'=4,'head_1'=4,'exp'=16] {'head_1'}, dimensions={2}, use_global_device_ids=true | all-gather | bytes 983040 | tf_op jit(solution)/shard_map/all_gather | solution.py:37
  174.0 0.0 all-gather.7.cloned.1.call-update
  174.0 36.9 %all-gather.7.cloned.1.call-done = bf16[32,12,4096]{2,0,1:T(8,128)(2,1)} async-done(((bf16[32,12,1024]{2,0,1:T(8,128)(2,1)}), bf16[32,12,4096]{2,0,1:T(8,128)(2,1)}) %all-gather.7.cloned.1.call-update) | async-done | bytes 3145744 | tf_op jit(solution)/shard_map/all_gather | solution.py:37
  210.9 0.0 copy-done.5
  210.9 3.7 %fusion.6 = f32[32,1,12,192]{3,0,2,1:T(8,128)} fusion(bf16[32,12,4096]{2,0,1:T(8,128)(2,1)} %all-gather.7.cloned.1.call-done, bf16[1,192,4096]{2,1,0:T(8,128)(2,1)S(1)} %copy-done.5), kind=kOutput, calls=%fused_computation.11 | convolution fusion | flops 603979776 | bytes 5013504 | tf_op jit(solution)/shard_map/slcd,lhd->slch/dot_general | solution.py:77
  214.6 0.0 copy-done
  214.6 7.6 %fusion = bf16[32,1,12,4096]{3,0,2,1:T(8,128)(2,1)} fusion(bf16[1,192,4096]{2,1,0:T(8,128)(2,1)S(1)} %copy-done, bf16[32,12,4096]{2,0,1:T(8,128)(2,1)} %all-gather.7.cloned.1.call-done, bf16[1,192,4096]{2,1,0:T(8,128)(2,1)} %param.18, f32[32,1,12,192]{3,0,2,1:T(8,128)} %fusion.6), kind=kOutput, calls=%fused_computation.3 | convolution fusion | flops 1209974784 | bytes 9732096 | tf_op jit(solution)/shard_map/slch,lhd->slcd/dot_general | solution.py:80
  222.2 2.3 copy.37
  224.5 44.0 %all_to_all.21 = bf16[16,32,1,12,256]{4,1,3,2,0:T(8,128)(2,1)} all-to-all(bf16[16,32,1,12,256]{4,1,3,2,0:T(8,128)(2,1)S(1)} %bitcast.102), channel_id=1, replica_groups=mesh['tok'=2,'head_0'=4,'head_1'=4,'exp'=16] {'head_0','head_1'}, dimensions={0} | all-to-all | bytes 6291456 | tf_op jit(solution)/shard_map/all_to_all | solution.py:24
  268.5 0.0 copy-start.2
  268.5 2.6 reduce_sum.46
  271.0 0.8 copy.29
  271.8 14.3 %all-to-all-start.3 = ((bf16[32,12,256]{2,1,0:T(8,128)(2,1)}), bf16[32,12,256]{2,1,0:T(8,128)(2,1)S(1)}, u32[]{:S(2)}, u32[]{:S(2)}) async-start(bf16[32,12,256]{2,1,0:T(8,128)(2,1)} %copy.29), calls=%async_computation.3 | async-start | bytes 524288 | tf_op jit(solution)/shard_map/all_to_all | solution.py:85
  286.2 0.1 copy.30
  286.2 0.1 reshape.158
  286.3 0.0 copy-done.2
  286.3 0.1 copy.31
  286.4 21.4 %all-to-all-done.3 = bf16[32,12,256]{2,1,0:T(8,128)(2,1)S(1)} async-done(((bf16[32,12,256]{2,1,0:T(8,128)(2,1)}), bf16[32,12,256]{2,1,0:T(8,128)(2,1)S(1)}, u32[]{:S(2)}, u32[]{:S(2)}) %all-to-all-start.3) | async-done | bytes 196640 | tf_op jit(solution)/shard_map/all_to_all | solution.py:85
  307.9 1.0 gather_fusion
  308.9 0.1 fusion.28
  309.0 0.6 bitcast_add_fusion
  (9 shorter events, 0.2 us)
Async XLA Ops:
  6.5 208.1 %copy-start = (bf16[1,192,4096]{2,1,0:T(8,128)(2,1)S(1)}, bf16[1,192,4096]{2,1,0:T(8,128)(2,1)}, u32[]{:S(2)}) copy-start(bf16[1,192,4096]{2,1,0:T(8,128)(2,1)} %param.19) | copy-start | bytes 4718596
  6.5 86.4 %copy-start.4 = (s32[1,32,8]{1,2,0:T(8,128)S(1)}, s32[1,32,8]{1,2,0:T(8,128)}, u32[]{:S(2)}) copy-start(s32[1,32,8]{1,2,0:T(8,128)} %param.14) | copy-start | bytes 3076
  6.5 86.4 %copy-start.3 = (s32[1,32,8]{1,2,0:T(8,128)S(1)}, s32[1,32,8]{1,2,0:T(8,128)}, u32[]{:S(2)}) copy-start(s32[1,32,8]{1,2,0:T(8,128)} %param.15) | copy-start | bytes 3076
  6.5 93.9 %copy-start.1 = (f32[1,32,256]{2,1,0:T(8,128)S(1)}, f32[1,32,256]{2,1,0:T(8,128)}, u32[]{:S(2)}) copy-start(f32[1,32,256]{2,1,0:T(8,128)} %param.12) | copy-start | bytes 98308
  6.5 77.0 %all-gather.5.cloned.1.call-start = ((), (), s32[]{:S(2)}) async-start(), calls=%async_computation.4 | async-start | bytes 2228224 | tf_op jit(solution)/shard_map/all_gather | solution.py:51
  86.3 14.1 %all-to-all-start = ((bf16[16,32,256]{2,1,0:T(8,128)(2,1)}), bf16[16,32,256]{2,1,0:T(8,128)(2,1)S(1)}, u32[]{:S(2)}, u32[]{:S(2)}) async-start(bf16[16,32,256]{2,1,0:T(8,128)(2,1)} %bitcast.101), calls=%async_computation | async-start | bytes 524288 | tf_op jit(solution)/shard_map/all_to_all | solution.py:24
  92.8 118.1 %all-gather.7.cloned.1.call-start = ((), (), s32[]{:S(2)}) async-start(), calls=%async_computation.5 | async-start | bytes 3932160 | tf_op jit(solution)/shard_map/all_gather | solution.py:37
  115.8 95.2 %copy-start.5 = (bf16[1,192,4096]{2,1,0:T(8,128)(2,1)S(1)}, bf16[1,192,4096]{2,1,0:T(8,128)(2,1)}, u32[]{:S(2)}) copy-start(bf16[1,192,4096]{2,1,0:T(8,128)(2,1)} %param.17) | copy-start | bytes 4718596
  268.5 17.9 %copy-start.2 = (f32[1,32,8]{1,2,0:T(8,128)S(1)}, f32[1,32,8]{1,2,0:T(8,128)}, u32[]{:S(2)}) copy-start(f32[1,32,8]{1,2,0:T(8,128)} %param.16) | copy-start | bytes 3076
  271.8 36.0 %all-to-all-start.3 = ((bf16[32,12,256]{2,1,0:T(8,128)(2,1)}), bf16[32,12,256]{2,1,0:T(8,128)(2,1)S(1)}, u32[]{:S(2)}, u32[]{:S(2)}) async-start(bf16[32,12,256]{2,1,0:T(8,128)(2,1)} %copy.29), calls=%async_computation.3 | async-start | bytes 524288 | tf_op jit(solution)/shard_map/all_to_all | solution.py:85
Sparse Core Ops, SparseCore 0:
  9.4 74.0 all-gather.4
  174.2 36.7 all-gather.6
where the time goes:
time: 317 us; the launch traced here: 316 us
  waiting for transfers between devices  142 us (45%)
  blocking collectives  116 us (37%)
  starting transfers between devices  20.9 us (7%)
  between operations  13.6 us (4%)
  matrix products  13.3 us (4%)
  local copies, waits for them, and re-layouts  7.68 us (2%)
  other arithmetic  3.61 us (1%)
    all_gather x1, waiting for transfers between devices, on_device(): lax.all_gather(out_proj, 'exp', axis=1, tiled=True)  76.2 us
    all_to_all x1, blocking collectives, on_device(): lax.all_to_all(outgoing, ('tok', 'exp'), split_axis=0, concat_axis=0, til...  44.8 us
    all_to_all x1, blocking collectives, sum_at_owner(): lax.all_to_all(pieces, axis, split_axis=0, concat_axis=0, tiled=True)  44 us
    all_gather x1, waiting for transfers between devices, gather_axes(): result = lax.all_gather(result, axes[number], axis=dim, tiled=True)  36.9 us
    all_to_all x1, waiting for transfers between devices, on_device(): lax.all_to_all(summed.reshape(EXPERTS, CAP, col_width).astype(jnp.bfloat1...  21.4 us
    all_to_all x1, starting transfers between devices, on_device(): lax.all_to_all(summed.reshape(EXPERTS, CAP, col_width).astype(jnp.bfloat1...  14.3 us
    psum x2, blocking collectives, over_axes(): x = lax.psum(x, axis)  13.5 us
    all_gather x1, blocking collectives, gather_axes(): result = lax.all_gather(result, axes[number], axis=dim, tiled=True)  13.4 us
  transfers between devices with their start and end apart: 4, of which 4 were waited for; matrix products, arithmetic and copies ran while one was open for 0% of the time, Pallas kernels for 0%

commit v1 on v0

v1 whole, which is shorter than its diff:
```python
import functools

import jax
import jax.numpy as jnp
import numpy as np
from jax import lax
from jax.experimental import pallas as pl
from jax.experimental.pallas import tpu as pltpu
from jax.sharding import Mesh
from jax.sharding import PartitionSpec as P

CAP = 12
TOK = 32
COLS = 256
GRID_Y = 4
GRID_X = 4
HEADS = 16
EXPS = 16
WIDTH = HEADS * COLS
HALF = WIDTH // 2
ROWS = 2 * EXPS * CAP
HEAD = ("head_0", "head_1")
EPS = 1e-05
BF16 = jnp.bfloat16
F32 = jnp.float32

VMEM = pl.BlockSpec(memory_space=pltpu.VMEM)
SMEM = pl.BlockSpec(memory_space=pltpu.SMEM)


def call(kernel, out_shape, scalars, arrays, flops=0, moved=0):
    return pl.pallas_call(
        kernel,
        out_shape=out_shape,
        in_specs=[SMEM] * len(scalars) + [VMEM] * len(arrays),
        out_specs=jax.tree.map(lambda _: VMEM, out_shape),
        compiler_params=pltpu.CompilerParams(vmem_limit_bytes=48 * 1024 * 1024),
        cost_estimate=pl.CostEstimate(flops=flops, bytes_accessed=moved, transcendentals=0),
    )(*scalars, *arrays)


def shape_of(*dims, dtype=BF16):
    return jax.ShapeDtypeStruct(dims, dtype)


def exchange(x, axes):
    return lax.all_to_all(x, axes, split_axis=0, concat_axis=0, tiled=True)


def project_kernel(head_ref, got_ref, weight_ref, partial_ref, routes_ref):
    rows = got_ref[:, 0:TOK, :].reshape(EXPS * TOK, COLS)
    product = jnp.dot(rows, weight_ref[...], preferred_element_type=F32)
    partial_ref[...] = product.astype(BF16).reshape(EXPS, TOK, COLS)
    routes_ref[...] = got_ref[head_ref[0], TOK : TOK + 16, :].astype(F32)


def residual_kernel(parts_ref, stream_ref, resid_ref, copies_ref):
    total = parts_ref[0].astype(F32)
    for index in range(1, HEADS):
        total = total + parts_ref[index].astype(F32)
    total = total + stream_ref[...]
    resid_ref[...] = total
    rounded = total.astype(BF16)
    for index in range(EXPS):
        copies_ref[index] = rounded


def dispatch_kernel(exp_ref, rows_ref, routes_ref, gain_ref, out_ref):
    squares = jnp.zeros((TOK, COLS), F32)
    for block in range(EXPS):
        value = rows_ref[block].astype(F32)
        squares = squares + value * value
    scale = lax.rsqrt(jnp.sum(squares, axis=1, keepdims=True) / WIDTH + EPS)
    ids = routes_ref[0:8, 0 : 2 * TOK]
    slots = routes_ref[8:16, 0 : 2 * TOK]
    here = exp_ref[0].astype(F32)
    taken = []
    for core in range(2):
        match = ids == here + float(core * EXPS)
        taken.append(jnp.sum(jnp.where(match, slots + 1.0, 0.0), axis=0, keepdims=True) - 1.0)
    row = lax.broadcasted_iota(jnp.int32, (4 * CAP, 2 * TOK), 0)
    col = lax.broadcasted_iota(jnp.int32, (4 * CAP, 2 * TOK), 1)
    second = row >= 2 * CAP
    row_in = jnp.where(second, row - 2 * CAP, row)
    upper = row_in >= CAP
    slot = jnp.where(upper, row_in - CAP, row_in).astype(F32)
    same_half = upper == (col >= TOK)
    wanted = jnp.where(second, taken[1], taken[0])
    select = jnp.where((wanted == slot) & same_half, 1.0, 0.0).astype(BF16)
    for block in range(EXPS // 2):
        pair = []
        for piece in (block, block + EXPS // 2):
            gain = gain_ref[0:1, piece * COLS : (piece + 1) * COLS]
            pair.append((rows_ref[piece].astype(F32) * scale * gain).astype(BF16))
        picked = jnp.dot(select, jnp.concatenate(pair, axis=0), preferred_element_type=F32)
        picked = picked.astype(BF16)
        for head in range(HEADS):
            out_ref[head, :, block * COLS : (block + 1) * COLS] = picked


def hidden_kernel(rows_ref, gate_ref, up_ref, order_ref, out_ref):
    contract = (((1,), (1,)), ((), ()))

    def both_halves(weight_ref):
        low = lax.dot_general(
            weight_ref[:, :HALF], rows_ref[...], contract, preferred_element_type=F32
        )
        high = lax.dot_general(
            weight_ref[:, HALF:], rows_ref[...], contract, preferred_element_type=F32
        )
        return low + pltpu.roll(high, high.shape[1] - CAP, 1)

    gate = both_halves(gate_ref)
    up = both_halves(up_ref)
    hidden = (gate / (1.0 + jnp.exp(-gate)) * up).astype(BF16)
    ordered = jnp.dot(hidden, order_ref[...], preferred_element_type=F32).astype(BF16)
    for index in range(GRID_X):
        out_ref[index] = ordered


def pieces_kernel(x_ref, weight_ref, *out_refs):
    for step, out_ref in enumerate(out_refs):
        column = lax.rem(x_ref[0] + step, GRID_X)
        for row in range(GRID_Y):
            start = pl.multiple_of((row * GRID_X + column) * COLS, COLS)
            out_ref[:, row * COLS : (row + 1) * COLS] = weight_ref[:, pl.ds(start, COLS)]


def down_kernel(x_ref, hidden_ref, *refs):
    weights, out_ref = refs[:-1], refs[-1]
    contract = (((0,), (0,)), ((), ()))
    total = jnp.zeros((ROWS, GRID_Y * COLS), F32)
    for step, weight_ref in enumerate(weights):
        source = lax.rem(x_ref[0] + GRID_X - step, GRID_X)
        total = total + lax.dot_general(
            hidden_ref[source], weight_ref[...], contract, preferred_element_type=F32
        )
    rounded = total.astype(BF16)
    for half in range(2):
        for row in range(GRID_Y):
            out_ref[half * GRID_Y + row] = rounded[
                half * EXPS * CAP : (half + 1) * EXPS * CAP, row * COLS : (row + 1) * COLS
            ]


def collect_kernel(parts_ref, order_ref, out_ref):
    halves = []
    for core in range(2):
        total = parts_ref[core * GRID_Y].astype(F32)
        for row in range(1, GRID_Y):
            total = total + parts_ref[core * GRID_Y + row].astype(F32)
        halves.append(total.astype(BF16))
    stacked = jnp.concatenate(halves, axis=0)
    out_ref[...] = jnp.dot(order_ref[...], stacked, preferred_element_type=F32).astype(BF16)


def mix_kernel(results_ref, target_ref, probs_ref, resid_ref, out_ref):
    place = lax.broadcasted_iota(jnp.int32, (TOK, ROWS), 1)
    weights = jnp.zeros((TOK, ROWS), F32)
    for choice in range(8):
        hit = place == target_ref[:, choice : choice + 1]
        weights = weights + jnp.where(hit, probs_ref[:, choice : choice + 1], 0.0)
    coarse = weights.astype(BF16)
    fine = (weights - coarse.astype(F32)).astype(BF16)
    results = results_ref[...]
    mixed = jnp.dot(coarse, results, preferred_element_type=F32)
    mixed = mixed + jnp.dot(fine, results, preferred_element_type=F32)
    out_ref[...] = resid_ref[...] + mixed


def slot_order():
    order = np.zeros((2 * ROWS, ROWS), np.float32)
    for image in range(EXPS):
        for half in range(2):
            for slot in range(CAP):
                order[(image * 2 + half) * 2 * CAP + slot, (half * EXPS + image) * CAP + slot] = 1
    return order


def return_order():
    order = np.zeros((ROWS, ROWS), np.float32)
    for image in range(EXPS):
        for core in range(2):
            for slot in range(CAP):
                order[(image * 2 + core) * CAP + slot, (core * EXPS + image) * CAP + slot] = 1
    return order


def on_device(
    context, out_proj, stream, norm_gain, expert_ids, slot_ids, gate_probs, w_gate, w_up, w_down
):
    head = lax.axis_index(HEAD).astype(jnp.int32)[None]
    exp = lax.axis_index("exp").astype(jnp.int32)[None]
    x_at = lax.axis_index("head_1").astype(jnp.int32)[None]
    turn = [(a * EXPS + b, b * EXPS + a) for a in range(HEADS) for b in range(EXPS)]
    turned = HEAD + ("exp",)

    ids, slots = expert_ids[0], slot_ids[0]
    routes = jnp.concatenate([ids.T, slots.T], axis=0).astype(BF16)
    routes = jnp.pad(jnp.concatenate([routes, routes], axis=1), ((0, 0), (0, COLS - 2 * TOK)))
    payload = jnp.concatenate([context[0], routes], axis=0)
    got = exchange(jnp.broadcast_to(payload, (EXPS, *payload.shape)), "exp")

    stream_turned = lax.ppermute(stream[0], turned, turn)
    downs = call(
        pieces_kernel, [shape_of(192, GRID_Y * COLS)] * GRID_X, [x_at], [w_down[0]], moved=3 << 20
    )
    down_parts = [downs[0]]
    for step in range(1, GRID_X):
        ring = [(a, (a + step) % GRID_X) for a in range(GRID_X)]
        down_parts.append(lax.ppermute(downs[step], "head_1", ring))

    partial, routed = call(
        project_kernel,
        (shape_of(EXPS, TOK, COLS), shape_of(16, COLS, dtype=F32)),
        [head],
        [got, out_proj],
    )
    parts = exchange(partial, HEAD)
    resid_turned, copies = call(
        residual_kernel,
        (shape_of(TOK, COLS, dtype=F32), shape_of(EXPS, TOK, COLS)),
        [],
        [parts, stream_turned],
    )
    resid = lax.ppermute(resid_turned, turned, turn)
    rows = exchange(copies, "exp")
    rows, *down_parts = lax.optimization_barrier((rows, *down_parts))
    outgoing = call(
        dispatch_kernel,
        shape_of(HEADS, 4 * CAP, HALF),
        [exp],
        [rows, routed, norm_gain.reshape(1, WIDTH)],
    )
    arrived = exchange(outgoing.reshape(2 * HEADS, 2 * CAP, HALF), HEAD + ("tok",))
    hidden = call(
        hidden_kernel,
        shape_of(GRID_X, 192, ROWS),
        [],
        [arrived.reshape(2 * ROWS, HALF), w_gate[0], w_up[0], jnp.asarray(slot_order(), BF16)],
    )
    hidden_row = exchange(hidden, "head_1")
    produced = call(
        down_kernel, shape_of(2 * GRID_Y, ROWS // 2, COLS), [x_at], [hidden_row, *down_parts]
    )
    gathered = exchange(produced, ("tok", "head_0"))
    summed = call(
        collect_kernel,
        shape_of(ROWS, COLS),
        [],
        [gathered, jnp.asarray(return_order(), BF16)],
    )
    results = exchange(summed.reshape(EXPS, 2 * CAP, COLS), "exp")
    core = ids // EXPS
    target = jnp.where(slots >= 0, ((ids - core * EXPS) * 2 + core) * CAP + slots, -1)
    mixed = call(
        mix_kernel,
        shape_of(TOK, COLS, dtype=F32),
        [],
        [results.reshape(ROWS, COLS), target, gate_probs[0], resid],
    )
    return mixed[None]


def solution(mesh):
    split = Mesh(
        mesh.devices.reshape(mesh.shape["tok"], GRID_Y, GRID_X, mesh.shape["exp"]),
        ("tok", "head_0", "head_1", "exp"),
    )
    in_specs = (
        P("exp", "tok", HEAD),
        P(HEAD, "exp"),
        P("exp", "tok", HEAD),
        P(),
        P("exp", "tok", None),
        P("exp", "tok", None),
        P("exp", "tok", None),
        P(("tok", "exp"), HEAD, None),
        P(("tok", "exp"), HEAD, None),
        P(("tok", "exp"), HEAD, None),
    )
    return jax.shard_map(
        on_device,
        mesh=split,
        in_specs=in_specs,
        out_specs=P("exp", "tok", HEAD),
        check_vma=False,
    )
```

time: 317 us -> 216 us (0.68)
  the two profiles are of different devices: /device:TPU:1 before, /device:TPU:17 now
where the time goes in v1:
time: 216 us; the launch traced here: 215 us
  blocking collectives  80.4 us (37%)
  starting transfers between devices  78.2 us (36%)
  waiting for transfers between devices  40.2 us (19%)
  Pallas kernels  11.7 us (5%)
  local copies, waits for them, and re-layouts  3.4 us (2%)
    all_to_all x3, blocking collectives, exchange(): return lax.all_to_all(x, axes, split_axis=0, concat_axis=0, tiled=True)  80.4 us
    all_to_all x4, starting transfers between devices, exchange(): return lax.all_to_all(x, axes, split_axis=0, concat_axis=0, tiled=True)  40.9 us
    all_to_all x4, waiting for transfers between devices, exchange(): return lax.all_to_all(x, axes, split_axis=0, concat_axis=0, tiled=True)  18 us
    ppermute x1, starting transfers between devices, on_device(): resid = lax.ppermute(resid_turned, turned, turn)  14 us
    ppermute x1, starting transfers between devices, on_device(): stream_turned = lax.ppermute(stream[0], turned, turn)  11.8 us
    pallas_call x8, Pallas kernels, call(): pl.pallas_call(kernel, out_shape=out_shape, in_specs=[SMEM] * len(scalars...  11.7 us
    ppermute x3, starting transfers between devices, on_device(): down_parts.append(lax.ppermute(downs[step], 'head_1', ring))  11.4 us
    ppermute x3, waiting for transfers between devices, on_device(): down_parts.append(lax.ppermute(downs[step], 'head_1', ring))  9.95 us
  transfers between devices with their start and end apart: 9, of which 5 were waited for; matrix products, arithmetic and copies ran while one was open for 0% of the time, Pallas kernels for 0%

profile of v1, /device:TPU:17, one launch (start us, length us, event | category | flops | bytes accessed | tf_op | source)
XLA Modules:
  0.0 215.2 jit_solution(13080166261300660998)
XLA Ops:
  0.0 0.8 copy.17
  0.8 0.8 copy.18
  1.5 0.1 pad_maximum_fusion.1
  1.6 0.1 copy.19
  1.7 0.1 fusion.11
  1.8 0.8 pad_maximum_fusion
  2.6 0.8 broadcast_in_dim.20
  3.4 14.9 %all-to-all-start = ((bf16[16,48,256]{2,1,0:T(8,128)(2,1)}), bf16[16,48,256]{2,1,0:T(8,128)(2,1)S(1)}, u32[]{:S(2)}, u32[]{:S(2)}) async-start(bf16[16,48,256]{2,1,0:T(8,128)(2,1)} %broadcast_in_dim.20), calls=%async_computation | async-start | bytes 786432 | tf_op jit(solution)/shard_map/all_to_all | solution.py:47
  18.3 18.0 %all-to-all-done.got_ref = bf16[16,48,256]{2,1,0:T(8,128)(2,1)S(1)} async-done(((bf16[16,48,256]{2,1,0:T(8,128)(2,1)}), bf16[16,48,256]{2,1,0:T(8,128)(2,1)S(1)}, u32[]{:S(2)}, u32[]{:S(2)}) %all-to-all-start) | async-done | bytes 393248 | tf_op jit(solution)/shard_map/all_to_all | solution.py:47
  36.3 0.9 copy-done.5
  37.2 0.9 shard_map.118
  38.2 6.8 %all-to-all-start.1 = ((bf16[16,32,256]{2,1,0:T(8,128)(2,1)}), bf16[16,32,256]{2,1,0:T(8,128)(2,1)S(1)}, u32[]{:S(2)}, u32[]{:S(2)}) async-start(bf16[16,32,256]{2,1,0:T(8,128)(2,1)} %get-tuple-element.18), calls=%async_computation.1 | async-start | bytes 524288 | tf_op jit(solution)/shard_map/all_to_all | solution.py:47
  45.0 0.0 copy-done.8
  45.0 11.8 %collective-permute-start = (f32[32,256]{1,0:T(8,128)S(1)}, f32[32,256]{1,0:T(8,128)S(1)}, u32[]{:S(2)}, u32[]{:S(2)}) collective-permute-start(f32[32,256]{1,0:T(8,128)S(1)} %bitcast.66), channel_id=1, source_target_pairs={{0,0},{1,16},{2,32},{3,48},{4,64},{5,80},{6,96},{7,112},{8,128},{9... | collective-permute-start | bytes 98312 | tf_op jit(solution)/shard_map/ppermute | solution.py:204
  56.9 4.0 %collective-permute-done.stream_ref = f32[32,256]{1,0:T(8,128)S(1)} collective-permute-done((f32[32,256]{1,0:T(8,128)S(1)}, f32[32,256]{1,0:T(8,128)S(1)}, u32[]{:S(2)}, u32[]{:S(2)}) %collective-permute-start) | collective-permute-done | bytes 32800 | tf_op jit(solution)/shard_map/ppermute | solution.py:204
  60.8 0.0 all-to-all-done.1.parts_ref
  60.8 0.8 shard_map.119
  61.6 7.7 %all-to-all-start.2 = ((bf16[16,32,256]{2,1,0:T(8,128)(2,1)}), bf16[16,32,256]{2,1,0:T(8,128)(2,1)S(1)}, u32[]{:S(2)}, u32[]{:S(2)}) async-start(bf16[16,32,256]{2,1,0:T(8,128)(2,1)} %get-tuple-element.19), calls=%async_computation.2 | async-start | bytes 524288 | tf_op jit(solution)/shard_map/all_to_all | solution.py:47
  69.3 0.0 copy-done.2
  69.3 0.2 shard_map.120
  69.6 4.3 %collective-permute-start.1 = (bf16[192,1024]{1,0:T(8,128)(2,1)S(1)}, bf16[192,1024]{1,0:T(8,128)(2,1)S(1)}, u32[]{:S(2)}, u32[]{:S(2)}) collective-permute-start(bf16[192,1024]{1,0:T(8,128)(2,1)S(1)} %get-tuple-element.21), channel_id=1, source_target_pairs={{0,16},{16,32},{32,48},{48,0},{1,17},{17,33},{33,49},{49,1},{2,18}... | collective-permute-start | bytes 1179656 | tf_op jit(solution)/shard_map/ppermute | solution.py:211
  73.9 3.6 %collective-permute-start.2 = (bf16[192,1024]{1,0:T(8,128)(2,1)S(1)}, bf16[192,1024]{1,0:T(8,128)(2,1)S(1)}, u32[]{:S(2)}, u32[]{:S(2)}) collective-permute-start(bf16[192,1024]{1,0:T(8,128)(2,1)S(1)} %get-tuple-element.22), channel_id=1, source_target_pairs={{0,32},{16,48},{32,0},{48,16},{1,33},{17,49},{33,1},{49,17},{2,34}... | collective-permute-start | bytes 1179656 | tf_op jit(solution)/shard_map/ppermute | solution.py:211
  77.5 3.5 %collective-permute-start.3 = (bf16[192,1024]{1,0:T(8,128)(2,1)S(1)}, bf16[192,1024]{1,0:T(8,128)(2,1)S(1)}, u32[]{:S(2)}, u32[]{:S(2)}) collective-permute-start(bf16[192,1024]{1,0:T(8,128)(2,1)S(1)} %get-tuple-element.23), channel_id=1, source_target_pairs={{0,48},{16,0},{32,16},{48,32},{1,49},{17,1},{33,17},{49,33},{2,50}... | collective-permute-start | bytes 1179656 | tf_op jit(solution)/shard_map/ppermute | solution.py:211
  81.0 0.0 collective-permute-done.1.refs_1_
  81.0 7.8 %collective-permute-done.2.refs_2_ = bf16[192,1024]{1,0:T(8,128)(2,1)S(1)} collective-permute-done((bf16[192,1024]{1,0:T(8,128)(2,1)S(1)}, bf16[192,1024]{1,0:T(8,128)(2,1)S(1)}, u32[]{:S(2)}, u32[]{:S(2)}) %collective-permute-start.2) | collective-permute-done | bytes 393248 | tf_op jit(solution)/shard_map/ppermute | solution.py:211
  88.8 2.2 %collective-permute-done.3.refs_3_ = bf16[192,1024]{1,0:T(8,128)(2,1)S(1)} collective-permute-done((bf16[192,1024]{1,0:T(8,128)(2,1)S(1)}, bf16[192,1024]{1,0:T(8,128)(2,1)S(1)}, u32[]{:S(2)}, u32[]{:S(2)}) %collective-permute-start.3) | collective-permute-done | bytes 393248 | tf_op jit(solution)/shard_map/ppermute | solution.py:211
  91.0 0.0 all-to-all-done.2.rows_ref
  91.0 0.0 copy-done.6
  91.0 0.6 shard_map.121
  91.6 0.0 copy-start
  91.6 0.0 copy-start.1
  91.6 0.0 copy-start.3
  91.6 52.7 %all_to_all.35 = bf16[32,24,2048]{2,1,0:T(8,128)(2,1)} all-to-all(bf16[32,24,2048]{2,1,0:T(8,128)(2,1)S(1)} %bitcast.57), channel_id=1, replica_groups=mesh['tok'=2,'head_0'=4,'head_1'=4,'exp'=16] {'head_0','head_1','tok'}, dimensions={0} | all-to-all | bytes 6291456 | tf_op jit(solution)/shard_map/all_to_all | solution.py:47
  144.3 0.0 copy-done
  144.3 0.0 copy-done.1
  144.3 0.0 copy-done.3
  144.3 6.3 %shard_map.122 = bf16[4,192,384]{2,1,0:T(8,128)(2,1)S(1)} custom-call(bf16[768,2048]{1,0:T(8,128)(2,1)} %bitcast.64, bf16[192,4096]{1,0:T(8,128)(2,1)S(1)} %bitcast.58, bf16[192,4096]{1,0:T(8,128)(2,1)S(1)} %bitcast.59, bf16[768,384]{1,0:T(8,128)(2,1)S(1)} %copy-done.3), custom_call_target="tpu_custom_call" | custom-call | tf_op jit(solution)/shard_map/pallas_call | solution.py:32
  150.6 12.8 %all_to_all.36.hidden_ref = bf16[4,192,384]{2,1,0:T(8,128)(2,1)S(1)} all-to-all(bf16[4,192,384]{2,1,0:T(8,128)(2,1)S(1)} %shard_map.122), channel_id=1, replica_groups=mesh['tok'=2,'head_0'=4,'head_1'=4,'exp'=16] {'head_1'}, dimensions={0} | all-to-all | bytes 1179648 | tf_op jit(solution)/shard_map/all_to_all | solution.py:47
  163.4 1.0 shard_map.123
  164.4 0.0 copy-start.7
  164.4 15.0 %all_to_all.37.parts_ref = bf16[8,192,256]{2,1,0:T(8,128)(2,1)S(1)} all-to-all(bf16[8,192,256]{2,1,0:T(8,128)(2,1)S(1)} %shard_map.123), channel_id=1, replica_groups=mesh['tok'=2,'head_0'=4,'head_1'=4,'exp'=16] {'tok','head_0'}, dimensions={0} | all-to-all | bytes 1572864 | tf_op jit(solution)/shard_map/all_to_all | solution.py:47
  179.4 1.0 shard_map.124
  180.4 11.5 %all-to-all-start.6 = ((bf16[16,24,256]{2,1,0:T(8,128)(2,1)}), bf16[16,24,256]{2,1,0:T(8,128)(2,1)S(1)}, u32[]{:S(2)}, u32[]{:S(2)}) async-start(bf16[16,24,256]{2,1,0:T(8,128)(2,1)} %bitcast.15), calls=%async_computation.6 | async-start | bytes 393216 | tf_op jit(solution)/shard_map/all_to_all | solution.py:47
  191.8 14.0 %collective-permute-start.4 = (f32[32,256]{1,0:T(8,128)S(1)}, f32[32,256]{1,0:T(8,128)S(1)}, u32[]{:S(2)}, u32[]{:S(2)}) collective-permute-start(f32[32,256]{1,0:T(8,128)S(1)} %get-tuple-element.30), channel_id=1, source_target_pairs={{0,0},{1,16},{2,32},{3,48},{4,64},{5,80},{6,96},{7,112},{8,128},{9... | collective-permute-start | bytes 98312 | tf_op jit(solution)/shard_map/ppermute | solution.py:226
  205.9 0.1 copy.21
  206.0 8.3 %collective-permute-done.4.resid_ref = f32[32,256]{1,0:T(8,128)S(1)} collective-permute-done((f32[32,256]{1,0:T(8,128)S(1)}, f32[32,256]{1,0:T(8,128)S(1)}, u32[]{:S(2)}, u32[]{:S(2)}) %collective-permute-start.4) | collective-permute-done | bytes 32800 | tf_op jit(solution)/shard_map/ppermute | solution.py:226
  214.3 0.0 all-to-all-done.6
  214.3 0.9 shard_map.125
  (9 shorter events, 0.0 us)
Async XLA Ops:
  0.0 45.0 %copy-start.8 = (f32[1,32,256]{2,1,0:T(8,128)S(1)}, f32[1,32,256]{2,1,0:T(8,128)}, u32[]{:S(2)}) copy-start(f32[1,32,256]{2,1,0:T(8,128)} %param.14) | copy-start | bytes 98308
  1.8 67.5 %copy-start.2 = (bf16[1,192,4096]{2,1,0:T(8,128)(2,1)S(1)}, bf16[1,192,4096]{2,1,0:T(8,128)(2,1)}, u32[]{:S(2)}) copy-start(bf16[1,192,4096]{2,1,0:T(8,128)(2,1)} %param.21) | copy-start | bytes 4718596
  3.4 32.9 %all-to-all-start = ((bf16[16,48,256]{2,1,0:T(8,128)(2,1)}), bf16[16,48,256]{2,1,0:T(8,128)(2,1)S(1)}, u32[]{:S(2)}, u32[]{:S(2)}) async-start(bf16[16,48,256]{2,1,0:T(8,128)(2,1)} %broadcast_in_dim.20), calls=%async_computation | async-start | bytes 786432 | tf_op jit(solution)/shard_map/all_to_all | solution.py:47
  36.3 0.9 copy-start.5
  38.2 52.8 %copy-start.6 = (f32[4096]{0:T(1024)S(1)}, f32[4096]{0:T(1024)}, u32[]{:S(2)}) copy-start(f32[4096]{0:T(1024)} %param.15) | copy-start | bytes 49156
  38.2 22.7 %all-to-all-start.1 = ((bf16[16,32,256]{2,1,0:T(8,128)(2,1)}), bf16[16,32,256]{2,1,0:T(8,128)(2,1)S(1)}, u32[]{:S(2)}, u32[]{:S(2)}) async-start(bf16[16,32,256]{2,1,0:T(8,128)(2,1)} %get-tuple-element.18), calls=%async_computation.1 | async-start | bytes 524288 | tf_op jit(solution)/shard_map/all_to_all | solution.py:47
  45.0 15.8 %collective-permute-start = (f32[32,256]{1,0:T(8,128)S(1)}, f32[32,256]{1,0:T(8,128)S(1)}, u32[]{:S(2)}, u32[]{:S(2)}) collective-permute-start(f32[32,256]{1,0:T(8,128)S(1)} %bitcast.66), channel_id=1, source_target_pairs={{0,0},{1,16},{2,32},{3,48},{4,64},{5,80},{6,96},{7,112},{8,128},{9... | collective-permute-start | bytes 98312 | tf_op jit(solution)/shard_map/ppermute | solution.py:204
  61.6 29.4 %all-to-all-start.2 = ((bf16[16,32,256]{2,1,0:T(8,128)(2,1)}), bf16[16,32,256]{2,1,0:T(8,128)(2,1)S(1)}, u32[]{:S(2)}, u32[]{:S(2)}) async-start(bf16[16,32,256]{2,1,0:T(8,128)(2,1)} %get-tuple-element.19), calls=%async_computation.2 | async-start | bytes 524288 | tf_op jit(solution)/shard_map/all_to_all | solution.py:47
  69.6 11.5 %collective-permute-start.1 = (bf16[192,1024]{1,0:T(8,128)(2,1)S(1)}, bf16[192,1024]{1,0:T(8,128)(2,1)S(1)}, u32[]{:S(2)}, u32[]{:S(2)}) collective-permute-start(bf16[192,1024]{1,0:T(8,128)(2,1)S(1)} %get-tuple-element.21), channel_id=1, source_target_pairs={{0,16},{16,32},{32,48},{48,0},{1,17},{17,33},{33,49},{49,1},{2,18}... | collective-permute-start | bytes 1179656 | tf_op jit(solution)/shard_map/ppermute | solution.py:211
  73.9 14.9 %collective-permute-start.2 = (bf16[192,1024]{1,0:T(8,128)(2,1)S(1)}, bf16[192,1024]{1,0:T(8,128)(2,1)S(1)}, u32[]{:S(2)}, u32[]{:S(2)}) collective-permute-start(bf16[192,1024]{1,0:T(8,128)(2,1)S(1)} %get-tuple-element.22), channel_id=1, source_target_pairs={{0,32},{16,48},{32,0},{48,16},{1,33},{17,49},{33,1},{49,17},{2,34}... | collective-permute-start | bytes 1179656 | tf_op jit(solution)/shard_map/ppermute | solution.py:211
  77.5 13.5 %collective-permute-start.3 = (bf16[192,1024]{1,0:T(8,128)(2,1)S(1)}, bf16[192,1024]{1,0:T(8,128)(2,1)S(1)}, u32[]{:S(2)}, u32[]{:S(2)}) collective-permute-start(bf16[192,1024]{1,0:T(8,128)(2,1)S(1)} %get-tuple-element.23), channel_id=1, source_target_pairs={{0,48},{16,0},{32,16},{48,32},{1,49},{17,1},{33,17},{49,33},{2,50}... | collective-permute-start | bytes 1179656 | tf_op jit(solution)/shard_map/ppermute | solution.py:211
  91.6 52.7 %copy-start = (bf16[1,192,4096]{2,1,0:T(8,128)(2,1)S(1)}, bf16[1,192,4096]{2,1,0:T(8,128)(2,1)}, u32[]{:S(2)}) copy-start(bf16[1,192,4096]{2,1,0:T(8,128)(2,1)} %param.19) | copy-start | bytes 4718596
  91.6 52.7 %copy-start.1 = (bf16[1,192,4096]{2,1,0:T(8,128)(2,1)S(1)}, bf16[1,192,4096]{2,1,0:T(8,128)(2,1)}, u32[]{:S(2)}) copy-start(bf16[1,192,4096]{2,1,0:T(8,128)(2,1)} %param.20) | copy-start | bytes 4718596
  91.6 52.7 %copy-start.3 = (bf16[768,384]{1,0:T(8,128)(2,1)S(1)}, bf16[768,384]{1,0:T(8,128)(2,1)}, u32[]{:S(2)}) copy-start(bf16[768,384]{1,0:T(8,128)(2,1)} %constant.45.clone.order_ref) | copy-start | bytes 1769476
  163.4 16.0 %copy-start.4 = (bf16[384,384]{1,0:T(8,128)(2,1)S(1)}, bf16[384,384]{1,0:T(8,128)(2,1)}, u32[]{:S(2)}) copy-start(bf16[384,384]{1,0:T(8,128)(2,1)} %constant.46.clone.order_ref) | copy-start | bytes 884740
  164.4 41.5 %copy-start.7 = (f32[1,32,8]{1,2,0:T(8,128)S(1)}, f32[1,32,8]{1,2,0:T(8,128)}, u32[]{:S(2)}) copy-start(f32[1,32,8]{1,2,0:T(8,128)} %param.18) | copy-start | bytes 3076
  180.4 33.9 %all-to-all-start.6 = ((bf16[16,24,256]{2,1,0:T(8,128)(2,1)}), bf16[16,24,256]{2,1,0:T(8,128)(2,1)S(1)}, u32[]{:S(2)}, u32[]{:S(2)}) async-start(bf16[16,24,256]{2,1,0:T(8,128)(2,1)} %bitcast.15), calls=%async_computation.6 | async-start | bytes 393216 | tf_op jit(solution)/shard_map/all_to_all | solution.py:47
  191.8 22.4 %collective-permute-start.4 = (f32[32,256]{1,0:T(8,128)S(1)}, f32[32,256]{1,0:T(8,128)S(1)}, u32[]{:S(2)}, u32[]{:S(2)}) collective-permute-start(f32[32,256]{1,0:T(8,128)S(1)} %get-tuple-element.30), channel_id=1, source_target_pairs={{0,0},{1,16},{2,32},{3,48},{4,64},{5,80},{6,96},{7,112},{8,128},{9... | collective-permute-start | bytes 98312 | tf_op jit(solution)/shard_map/ppermute | solution.py:226

commit v2 on v0

v2 whole, which is shorter than its diff:
```python
import jax
import jax.numpy as jnp
import numpy as np
from jax import lax
from jax.experimental import pallas as pl
from jax.experimental.pallas import tpu as pltpu
from jax.sharding import Mesh
from jax.sharding import PartitionSpec as P

CAP = 12
LINE = 4
GROUP = LINE * CAP
TOK = 32
COLS = 256
HEADS = 16
EXPS = 16
WIDTH = HEADS * COLS
ROWS = 2 * EXPS * CAP
HEAD = ("head_0", "head_1")
PLANE = ("tok", "head_0", "head_1")
EPS = 1e-05
BF16 = jnp.bfloat16
F32 = jnp.float32

VMEM = pl.BlockSpec(memory_space=pltpu.VMEM)
SMEM = pl.BlockSpec(memory_space=pltpu.SMEM)


def call(kernel, out_shape, scalars, arrays, flops=0, moved=0):
    return pl.pallas_call(
        kernel,
        out_shape=out_shape,
        in_specs=[SMEM] * len(scalars) + [VMEM] * len(arrays),
        out_specs=jax.tree.map(lambda _: VMEM, out_shape),
        compiler_params=pltpu.CompilerParams(vmem_limit_bytes=48 * 1024 * 1024),
        cost_estimate=pl.CostEstimate(flops=flops, bytes_accessed=moved, transcendentals=0),
    )(*scalars, *arrays)


def shape_of(*dims, dtype=BF16):
    return jax.ShapeDtypeStruct(dims, dtype)


def exchange(x, axes):
    return lax.all_to_all(x, axes, split_axis=0, concat_axis=0, tiled=True)


def project_kernel(rows_ref, weight_ref, partial_ref):
    partial_ref[...] = jnp.dot(
        rows_ref[...], weight_ref[...], preferred_element_type=F32
    ).astype(BF16)


def residual_kernel(parts_ref, turned_ref, resid_ref, slots_ref):
    total = parts_ref[0].astype(F32)
    for index in range(1, HEADS):
        total = total + parts_ref[index].astype(F32)
    total = total + turned_ref[0:TOK, :]
    resid_ref[...] = total
    place = lax.broadcasted_iota(jnp.int32, (ROWS, TOK), 0).astype(F32)
    select = jnp.zeros((ROWS, TOK), F32)
    for choice in range(8):
        wanted = turned_ref[TOK + choice : TOK + choice + 1, 0:TOK]
        select = jnp.where(place == wanted, 1.0, select)
    picked = jnp.dot(select.astype(BF16), total.astype(BF16), preferred_element_type=F32)
    slots_ref[...] = picked.astype(BF16)


def norm_kernel(rows_ref, gain_ref, out_ref):
    squares = jnp.zeros((2 * CAP, COLS), F32)
    for block in range(EXPS):
        value = rows_ref[block].astype(F32)
        squares = squares + value * value
    scale = lax.rsqrt(jnp.sum(squares, axis=1, keepdims=True) / WIDTH + EPS)
    for block in range(EXPS):
        at = slice(block * COLS, (block + 1) * COLS)
        value = (rows_ref[block].astype(F32) * scale * gain_ref[0:1, at]).astype(BF16)
        for peer in range(LINE):
            out_ref[peer, :, at] = value


def forward_kernel(core_ref, rows_ref, order_ref, out_ref):
    order = order_ref[core_ref[0]]
    for block in range(HEADS):
        at = slice(block * COLS, (block + 1) * COLS)
        value = jnp.dot(order, rows_ref[:, at], preferred_element_type=F32).astype(BF16)
        for peer in range(LINE):
            out_ref[peer, :, at] = value


def expert_kernel(core_ref, rows_ref, *refs):
    weights, out_ref = refs[:-1], refs[-1]
    contract = (((1,), (1,)), ((), ()))
    hidden = []
    for number in range(2):
        gate_ref, up_ref = weights[number], weights[2 + number]
        rows = rows_ref[:, number * GROUP : (number + 1) * GROUP, :].reshape(LINE * GROUP, WIDTH)
        gate = lax.dot_general(rows, gate_ref[...], contract, preferred_element_type=F32)
        up = lax.dot_general(rows, up_ref[...], contract, preferred_element_type=F32)
        hidden.append((gate / (1.0 + jnp.exp(-gate)) * up).astype(BF16))
    first = core_ref[0] == 0
    for peer in range(LINE):
        for sub in range(LINE):
            block = jnp.where(first, sub * LINE + peer, peer * LINE + sub)
            at = pl.ds(pl.multiple_of(block * COLS, COLS), COLS)
            for number in range(2):
                value = jnp.dot(
                    hidden[number], weights[4 + number][:, at], preferred_element_type=F32
                )
                out_ref[peer, sub * 2 + number] = value.astype(BF16)


def add_kernel(parts_ref, out_ref):
    for index in range(2 * LINE):
        total = parts_ref[0, index].astype(F32)
        for source in range(1, LINE):
            total = total + parts_ref[source, index].astype(F32)
        out_ref[index] = total.astype(BF16)


def collect_kernel(core_ref, parts_ref, order_ref, out_ref):
    total = parts_ref[0].astype(F32)
    for source in range(1, LINE):
        total = total + parts_ref[source].astype(F32)
    order = order_ref[core_ref[0]]
    out_ref[...] = jnp.dot(order, total.astype(BF16), preferred_element_type=F32).astype(BF16)


def mix_kernel(results_ref, target_ref, probs_ref, resid_ref, out_ref):
    place = lax.broadcasted_iota(jnp.int32, (TOK, ROWS), 1)
    weights = jnp.zeros((TOK, ROWS), F32)
    for choice in range(8):
        hit = place == target_ref[:, choice : choice + 1]
        weights = weights + jnp.where(hit, probs_ref[:, choice : choice + 1], 0.0)
    coarse = weights.astype(BF16)
    fine = (weights - coarse.astype(F32)).astype(BF16)
    results = results_ref[...]
    mixed = jnp.dot(coarse, results, preferred_element_type=F32)
    mixed = mixed + jnp.dot(fine, results, preferred_element_type=F32)
    out_ref[...] = resid_ref[...] + mixed


def forward_order():
    order = np.zeros((2, 2 * GROUP, 2 * GROUP), np.float32)
    for core in range(2):
        for number in range(2):
            for inner in range(LINE):
                for slot in range(CAP):
                    source = (inner * 2 + (core ^ number)) * CAP + slot
                    order[core, (number * LINE + inner) * CAP + slot, source] = 1
    return jnp.asarray(order, BF16)


def return_order():
    order = np.zeros((2, ROWS, ROWS), np.float32)
    for core in range(2):
        for number in range(2):
            for outer in range(LINE):
                for inner in range(LINE):
                    image = outer * LINE + inner if core == 0 else inner * LINE + outer
                    for slot in range(CAP):
                        source = ((number * LINE + outer) * LINE + inner) * CAP + slot
                        order[core, (image * 2 + (core ^ number)) * CAP + slot, source] = 1
    return jnp.asarray(order, BF16)


def plane_lines():
    lines_x = [[[(t * LINE + y) * LINE + x for x in range(LINE)] for y in range(LINE)] for t in (0, 1)]
    lines_y = [[[(t * LINE + y) * LINE + x for y in range(LINE)] for x in range(LINE)] for t in (0, 1)]
    return lines_x[0] + lines_y[1], lines_y[0] + lines_x[1]


def exchange_lines(x, lines):
    return lax.all_to_all(
        x, PLANE, split_axis=0, concat_axis=0, tiled=True, axis_index_groups=lines
    )


def on_device(
    context, out_proj, stream, norm_gain, expert_ids, slot_ids, gate_probs, w_gate, w_up, w_down
):
    core = lax.axis_index("tok").astype(jnp.int32)[None]
    turn = [(a * EXPS + b, b * EXPS + a) for a in range(HEADS) for b in range(EXPS)]
    turned = HEAD + ("exp",)
    first_lines, second_lines = plane_lines()

    got = exchange(jnp.broadcast_to(context[0], (EXPS, TOK, COLS)), "exp")

    ids, slots = expert_ids[0], slot_ids[0]
    owner = ids // EXPS
    target = jnp.where(slots >= 0, ((ids - owner * EXPS) * 2 + owner) * CAP + slots, -1)
    routes = jnp.pad(target.T.astype(F32), ((0, 0), (0, COLS - TOK)))
    stream_turned = lax.ppermute(jnp.concatenate([stream[0], routes], axis=0), turned, turn)
    got, stream_turned = lax.optimization_barrier((got, stream_turned))

    partial = call(
        project_kernel, shape_of(EXPS * TOK, COLS), [], [got.reshape(EXPS * TOK, COLS), out_proj]
    )
    parts = exchange(partial.reshape(HEADS, TOK, COLS), HEAD)
    resid_turned, picked = call(
        residual_kernel,
        (shape_of(TOK, COLS, dtype=F32), shape_of(ROWS, COLS)),
        [],
        [parts, stream_turned],
    )
    resid = lax.ppermute(resid_turned, turned, turn)
    weights = []
    for weight in (w_gate[0], w_up[0], w_down[0]):
        weights += [weight, lax.ppermute(weight, "tok", [(0, 1), (1, 0)])]
    rows = exchange(picked.reshape(EXPS, 2 * CAP, COLS), "exp")
    rows, *weights = lax.optimization_barrier((rows, *weights))
    normed = call(
        norm_kernel,
        shape_of(LINE, 2 * CAP, WIDTH),
        [],
        [rows, norm_gain.reshape(1, WIDTH)],
    )
    line = exchange_lines(normed, first_lines)
    forward = call(
        forward_kernel,
        shape_of(LINE, 2 * GROUP, WIDTH),
        [core],
        [line.reshape(2 * GROUP, WIDTH), forward_order()],
    )
    arrived = exchange_lines(forward, second_lines)
    arrived, resid = lax.optimization_barrier((arrived, resid))
    produced = call(
        expert_kernel,
        shape_of(LINE, 2 * LINE, LINE * GROUP, COLS),
        [core],
        [arrived, *weights],
    )
    summed = call(
        add_kernel,
        shape_of(2 * LINE, LINE * GROUP, COLS),
        [],
        [exchange_lines(produced, first_lines)],
    )
    collected = call(
        collect_kernel,
        shape_of(ROWS, COLS),
        [core],
        [exchange_lines(summed.reshape(LINE, ROWS, COLS), second_lines), return_order()],
    )
    results = exchange(collected.reshape(EXPS, 2 * CAP, COLS), "exp")
    mixed = call(
        mix_kernel,
        shape_of(TOK, COLS, dtype=F32),
        [],
        [results.reshape(ROWS, COLS), target, gate_probs[0], resid],
    )
    return mixed[None]


def solution(mesh):
    split = Mesh(
        mesh.devices.reshape(mesh.shape["tok"], LINE, LINE, mesh.shape["exp"]),
        ("tok", "head_0", "head_1", "exp"),
    )
    in_specs = (
        P("exp", "tok", HEAD),
        P(HEAD, "exp"),
        P("exp", "tok", HEAD),
        P(),
        P("exp", "tok", None),
        P("exp", "tok", None),
        P("exp", "tok", None),
        P(("tok", "exp"), HEAD, None),
        P(("tok", "exp"), HEAD, None),
        P(("tok", "exp"), HEAD, None),
    )
    return jax.shard_map(
        on_device,
        mesh=split,
        in_specs=in_specs,
        out_specs=P("exp", "tok", HEAD),
        check_vma=False,
    )
```

time: 317 us -> 199 us (0.63)
  the two profiles are of different devices: /device:TPU:1 before, /device:TPU:32 now
where the time goes in v2:
time: 199 us; the launch traced here: 198 us
  blocking collectives  62.5 us (31%)
  waiting for transfers between devices  62.4 us (31%)
  starting transfers between devices  51.8 us (26%)
  Pallas kernels  14.3 us (7%)
  local copies, waits for them, and re-layouts  6.62 us (3%)
    all_to_all x2, blocking collectives, exchange_lines(): lax.all_to_all(x, PLANE, split_axis=0, concat_axis=0, tiled=True, axis_in...  38 us
    all_to_all x3, starting transfers between devices, exchange(): return lax.all_to_all(x, axes, split_axis=0, concat_axis=0, tiled=True)  31.7 us
    all_to_all x3, waiting for transfers between devices, exchange(): return lax.all_to_all(x, axes, split_axis=0, concat_axis=0, tiled=True)  29.3 us
    all_to_all x2, waiting for transfers between devices, exchange_lines(): lax.all_to_all(x, PLANE, split_axis=0, concat_axis=0, tiled=True, axis_in...  24.8 us
    all_to_all x1, blocking collectives, exchange(): return lax.all_to_all(x, axes, split_axis=0, concat_axis=0, tiled=True)  24.4 us
    pallas_call x8, Pallas kernels, call(): pl.pallas_call(kernel, out_shape=out_shape, in_specs=[SMEM] * len(scalars...  14.3 us
    all_to_all x2, starting transfers between devices, exchange_lines(): lax.all_to_all(x, PLANE, split_axis=0, concat_axis=0, tiled=True, axis_in...  8.4 us
    ppermute x3, starting transfers between devices, on_device(): weights += [weight, lax.ppermute(weight, 'tok', [(0, 1), (1, 0)])]  6.24 us
  transfers between devices with their start and end apart: 10, of which 7 were waited for; matrix products, arithmetic and copies ran while one was open for 1% of the time, Pallas kernels for 1%

profile of v2, /device:TPU:32, one launch (start us, length us, event | category | flops | bytes accessed | tf_op | source)
XLA Modules:
  0.0 198.4 jit_solution(11427052912051609826)
XLA Ops:
  0.0 1.5 broadcast_in_dim.12
  1.5 15.2 %all-to-all-start = ((bf16[16,32,256]{2,1,0:T(8,128)(2,1)}), bf16[16,32,256]{2,1,0:T(8,128)(2,1)S(1)}, u32[]{:S(2)}, u32[]{:S(2)}) async-start(bf16[16,32,256]{2,1,0:T(8,128)(2,1)} %broadcast_in_dim.12), calls=%async_computation | async-start | bytes 524288 | tf_op jit(solution)/shard_map/all_to_all | solution.py:45
  16.7 1.9 collective-permute-start.1
  18.6 2.4 %collective-permute-start.2 = (bf16[192,4096]{1,0:T(8,128)(2,1)}, bf16[192,4096]{1,0:T(8,128)(2,1)S(1)}, u32[]{:S(2)}, u32[]{:S(2)}) collective-permute-start(bf16[192,4096]{1,0:T(8,128)(2,1)} %bitcast.56), channel_id=1, source_target_pairs={{0,256},{256,0},{1,257},{257,1},{2,258},{258,2},{3,259},{259,3},{4... | collective-permute-start | bytes 4718600 | tf_op jit(solution)/shard_map/ppermute | solution.py:209
  21.0 1.9 collective-permute-start.3
  22.9 0.8 copy.13
  23.7 0.8 copy.14
  24.5 0.1 copy.17
  24.6 0.8 select_maximum_fusion
  25.3 2.9 %collective-permute-start = (f32[40,256]{1,0:T(8,128)S(1)}, f32[40,256]{1,0:T(8,128)S(1)}, u32[]{:S(2)}, u32[]{:S(2)}) collective-permute-start(f32[40,256]{1,0:T(8,128)S(1)} %select_maximum_fusion), channel_id=1, source_target_pairs={{0,0},{1,16},{2,32},{3,48},{4,64},{5,80},{6,96},{7,112},{8,128},{9... | collective-permute-start | bytes 122888 | tf_op jit(solution)/shard_map/ppermute | solution.py:193
  28.3 4.0 %collective-permute-done.turned_ref = f32[40,256]{1,0:T(8,128)S(1)} collective-permute-done((f32[40,256]{1,0:T(8,128)S(1)}, f32[40,256]{1,0:T(8,128)S(1)}, u32[]{:S(2)}, u32[]{:S(2)}) %collective-permute-start) | collective-permute-done | bytes 40992 | tf_op jit(solution)/shard_map/ppermute | solution.py:193
  32.2 2.3 %all-to-all-done = bf16[16,32,256]{2,1,0:T(8,128)(2,1)S(1)} async-done(((bf16[16,32,256]{2,1,0:T(8,128)(2,1)}), bf16[16,32,256]{2,1,0:T(8,128)(2,1)S(1)}, u32[]{:S(2)}, u32[]{:S(2)}) %all-to-all-start) | async-done | bytes 262176 | tf_op jit(solution)/shard_map/all_to_all | solution.py:45
  34.6 0.9 copy-done.5
  35.5 0.2 shard_map.118
  35.7 24.4 %all_to_all.40.parts_ref = bf16[16,32,256]{2,1,0:T(8,128)(2,1)S(1)} all-to-all(bf16[16,32,256]{2,1,0:T(8,128)(2,1)S(1)} %bitcast.59), channel_id=1, replica_groups=mesh['tok'=2,'head_0'=4,'head_1'=4,'exp'=16] {'head_0','head_1'}, dimensions={0} | all-to-all | bytes 524288 | tf_op jit(solution)/shard_map/all_to_all | solution.py:45
  60.2 1.0 shard_map.119
  61.1 10.3 %all-to-all-start.2 = ((bf16[16,24,256]{2,1,0:T(8,128)(2,1)}), bf16[16,24,256]{2,1,0:T(8,128)(2,1)S(1)}, u32[]{:S(2)}, u32[]{:S(2)}) async-start(bf16[16,24,256]{2,1,0:T(8,128)(2,1)} %bitcast.8), calls=%async_computation.2 | async-start | bytes 393216 | tf_op jit(solution)/shard_map/all_to_all | solution.py:45
  71.4 0.0 collective-permute-done.1.refs_1_
  71.4 0.0 copy-start.2
  71.4 1.1 copy-done.2
  72.5 0.0 collective-permute-done.2.refs_3_
  72.6 0.0 collective-permute-done.3.refs_5_
  72.6 13.7 %all-to-all-done.2.rows_ref = bf16[16,24,256]{2,1,0:T(8,128)(2,1)S(1)} async-done(((bf16[16,24,256]{2,1,0:T(8,128)(2,1)}), bf16[16,24,256]{2,1,0:T(8,128)(2,1)S(1)}, u32[]{:S(2)}, u32[]{:S(2)}) %all-to-all-start.2) | async-done | bytes 196640 | tf_op jit(solution)/shard_map/all_to_all | solution.py:45
  86.3 0.0 copy-done.7
  86.3 1.1 shard_map.120
  87.3 3.5 %all-to-all-start.3 = ((bf16[4,24,4096]{2,1,0:T(8,128)(2,1)}), bf16[4,24,4096]{2,1,0:T(8,128)(2,1)S(1)}, u32[]{:S(2)}, u32[]{:S(2)}) async-start(bf16[4,24,4096]{2,1,0:T(8,128)(2,1)} %shard_map.120), calls=%async_computation.3 | async-start | bytes 1572864 | tf_op jit(solution)/shard_map/all_to_all | solution.py:174
  90.8 9.4 %all-to-all-done.3 = bf16[4,24,4096]{2,1,0:T(8,128)(2,1)S(1)} async-done(((bf16[4,24,4096]{2,1,0:T(8,128)(2,1)}), bf16[4,24,4096]{2,1,0:T(8,128)(2,1)S(1)}, u32[]{:S(2)}, u32[]{:S(2)}) %all-to-all-start.3) | async-done | bytes 786464 | tf_op jit(solution)/shard_map/all_to_all | solution.py:174
  100.3 0.0 copy-done.8
  100.3 0.0 copy-done.6
  100.3 2.1 %shard_map.121 = bf16[4,96,4096]{2,1,0:T(8,128)(2,1)} custom-call(s32[1]{0:T(128)} %bitcast.core_ref, bf16[96,4096]{1,0:T(8,128)(2,1)S(1)} %bitcast.52, bf16[2,96,96]{2,1,0:T(8,128)(2,1)S(1)} %copy-done.6), custom_call_target="tpu_custom_call" | custom-call | tf_op jit(solution)/shard_map/pallas_call | solution.py:30
  102.4 4.9 %all-to-all-start.4 = ((bf16[4,96,4096]{2,1,0:T(8,128)(2,1)}), bf16[4,96,4096]{2,1,0:T(8,128)(2,1)}, u32[]{:S(2)}, u32[]{:S(2)}) async-start(bf16[4,96,4096]{2,1,0:T(8,128)(2,1)} %shard_map.121), calls=%async_computation.4 | async-start | bytes 6291456 | tf_op jit(solution)/shard_map/all_to_all | solution.py:174
  107.3 2.5 %collective-permute-start.4 = (f32[32,256]{1,0:T(8,128)S(1)}, f32[32,256]{1,0:T(8,128)S(1)}, u32[]{:S(2)}, u32[]{:S(2)}) collective-permute-start(f32[32,256]{1,0:T(8,128)S(1)} %get-tuple-element.22), channel_id=1, source_target_pairs={{0,0},{1,16},{2,32},{3,48},{4,64},{5,80},{6,96},{7,112},{8,128},{9... | collective-permute-start | bytes 98312 | tf_op jit(solution)/shard_map/ppermute | solution.py:206
  109.8 4.3 %collective-permute-done.4.resid_ref = f32[32,256]{1,0:T(8,128)S(1)} collective-permute-done((f32[32,256]{1,0:T(8,128)S(1)}, f32[32,256]{1,0:T(8,128)S(1)}, u32[]{:S(2)}, u32[]{:S(2)}) %collective-permute-start.4) | collective-permute-done | bytes 32800 | tf_op jit(solution)/shard_map/ppermute | solution.py:206
  114.1 15.4 %all-to-all-done.4.rows_ref = bf16[4,96,4096]{2,1,0:T(8,128)(2,1)} async-done(((bf16[4,96,4096]{2,1,0:T(8,128)(2,1)}), bf16[4,96,4096]{2,1,0:T(8,128)(2,1)}, u32[]{:S(2)}, u32[]{:S(2)}) %all-to-all-start.4) | async-done | bytes 3145760 | tf_op jit(solution)/shard_map/all_to_all | solution.py:174
  129.5 0.0 copy-done
  129.5 1.4 copy-done.3
  130.9 7.7 %shard_map.122 = bf16[4,8,192,256]{3,2,1,0:T(8,128)(2,1)} custom-call(s32[1]{0:T(128)} %bitcast.core_ref, bf16[4,96,4096]{2,1,0:T(8,128)(2,1)} %all-to-all-done.4.rows_ref, bf16[192,4096]{1,0:T(8,128)(2,1)S(1)} %bitcast.55, bf16[192,4096]{1,0:T(8,128)(2,1)S(1)} %copy-done.3, bf16[192,4096]{1,0:T(8,128)(2,1)S(1)} %bitcast.57, bf16[192,4096]{1,0:T(8,128)(2,1)} %copy-done.8, ...), custom_call_target="tpu_custom_call" | custom-call | tf_op jit(solution)/shard_map/pallas_call | solution.py:30
  138.6 25.8 %all_to_all.41.parts_ref = bf16[4,8,192,256]{3,2,1,0:T(8,128)(2,1)S(1)} all-to-all(bf16[4,8,192,256]{3,2,1,0:T(8,128)(2,1)} %shard_map.122), channel_id=1, replica_groups={{0,16,32,48},{64,80,96,112},{128,144,160,176},{192,208,224,240},{256,32..., dimensions={0} | all-to-all | bytes 6291456 | tf_op jit(solution)/shard_map/all_to_all | solution.py:174
  164.4 0.4 shard_map.123
  164.8 0.0 copy-start.4
  164.8 0.0 copy-start.9
  164.8 12.2 %all_to_all.42.parts_ref = bf16[4,384,256]{2,1,0:T(8,128)(2,1)S(1)} all-to-all(bf16[4,384,256]{2,1,0:T(8,128)(2,1)S(1)} %bitcast.53), channel_id=1, replica_groups={{0,64,128,192},{16,80,144,208},{32,96,160,224},{48,112,176,240},{256,27..., dimensions={0} | all-to-all | bytes 1572864 | tf_op jit(solution)/shard_map/all_to_all | solution.py:174
  177.0 0.0 copy-done.4
  177.0 1.0 shard_map.124
  178.0 6.2 %all-to-all-start.7 = ((bf16[16,24,256]{2,1,0:T(8,128)(2,1)}), bf16[16,24,256]{2,1,0:T(8,128)(2,1)S(1)}, u32[]{:S(2)}, u32[]{:S(2)}) async-start(bf16[16,24,256]{2,1,0:T(8,128)(2,1)} %bitcast.15), calls=%async_computation.7 | async-start | bytes 393216 | tf_op jit(solution)/shard_map/all_to_all | solution.py:45
  184.2 0.1 copy.16
  184.3 13.2 %all-to-all-done.7 = bf16[16,24,256]{2,1,0:T(8,128)(2,1)S(1)} async-done(((bf16[16,24,256]{2,1,0:T(8,128)(2,1)}), bf16[16,24,256]{2,1,0:T(8,128)(2,1)S(1)}, u32[]{:S(2)}, u32[]{:S(2)}) %all-to-all-start.7) | async-done | bytes 196640 | tf_op jit(solution)/shard_map/all_to_all | solution.py:45
  197.5 0.9 shard_map.125
  (10 shorter events, 0.0 us)
Async XLA Ops:
  0.0 86.3 %copy-start.7 = (f32[4096]{0:T(1024)S(1)}, f32[4096]{0:T(1024)}, u32[]{:S(2)}) copy-start(f32[4096]{0:T(1024)} %param.15) | copy-start | bytes 49156
  1.5 33.1 %all-to-all-start = ((bf16[16,32,256]{2,1,0:T(8,128)(2,1)}), bf16[16,32,256]{2,1,0:T(8,128)(2,1)S(1)}, u32[]{:S(2)}, u32[]{:S(2)}) async-start(bf16[16,32,256]{2,1,0:T(8,128)(2,1)} %broadcast_in_dim.12), calls=%async_computation | async-start | bytes 524288 | tf_op jit(solution)/shard_map/all_to_all | solution.py:45
  16.7 54.7 %collective-permute-start.1 = (bf16[192,4096]{1,0:T(8,128)(2,1)}, bf16[192,4096]{1,0:T(8,128)(2,1)S(1)}, u32[]{:S(2)}, u32[]{:S(2)}) collective-permute-start(bf16[192,4096]{1,0:T(8,128)(2,1)} %bitcast.54), channel_id=1, source_target_pairs={{0,256},{256,0},{1,257},{257,1},{2,258},{258,2},{3,259},{259,3},{4... | collective-permute-start | bytes 4718600 | tf_op jit(solution)/shard_map/ppermute | solution.py:209
  18.6 54.0 %collective-permute-start.2 = (bf16[192,4096]{1,0:T(8,128)(2,1)}, bf16[192,4096]{1,0:T(8,128)(2,1)S(1)}, u32[]{:S(2)}, u32[]{:S(2)}) collective-permute-start(bf16[192,4096]{1,0:T(8,128)(2,1)} %bitcast.56), channel_id=1, source_target_pairs={{0,256},{256,0},{1,257},{257,1},{2,258},{258,2},{3,259},{259,3},{4... | collective-permute-start | bytes 4718600 | tf_op jit(solution)/shard_map/ppermute | solution.py:209
  21.0 51.5 %collective-permute-start.3 = (bf16[192,4096]{1,0:T(8,128)(2,1)}, bf16[192,4096]{1,0:T(8,128)(2,1)}, u32[]{:S(2)}, u32[]{:S(2)}) collective-permute-start(bf16[192,4096]{1,0:T(8,128)(2,1)} %bitcast.63), channel_id=1, source_target_pairs={{0,256},{256,0},{1,257},{257,1},{2,258},{258,2},{3,259},{259,3},{4... | collective-permute-start | bytes 4718600 | tf_op jit(solution)/shard_map/ppermute | solution.py:209
  25.3 6.9 %collective-permute-start = (f32[40,256]{1,0:T(8,128)S(1)}, f32[40,256]{1,0:T(8,128)S(1)}, u32[]{:S(2)}, u32[]{:S(2)}) collective-permute-start(f32[40,256]{1,0:T(8,128)S(1)} %select_maximum_fusion), channel_id=1, source_target_pairs={{0,0},{1,16},{2,32},{3,48},{4,64},{5,80},{6,96},{7,112},{8,128},{9... | collective-permute-start | bytes 122888 | tf_op jit(solution)/shard_map/ppermute | solution.py:193
  34.6 0.9 copy-start.5
  60.2 40.1 %copy-start.6 = (bf16[2,96,96]{2,1,0:T(8,128)(2,1)S(1)}, bf16[2,96,96]{2,1,0:T(8,128)(2,1)}, u32[]{:S(2)}) copy-start(bf16[2,96,96]{2,1,0:T(8,128)(2,1)} %constant.37.clone.order_ref) | copy-start | bytes 110596
  61.1 25.2 %all-to-all-start.2 = ((bf16[16,24,256]{2,1,0:T(8,128)(2,1)}), bf16[16,24,256]{2,1,0:T(8,128)(2,1)S(1)}, u32[]{:S(2)}, u32[]{:S(2)}) async-start(bf16[16,24,256]{2,1,0:T(8,128)(2,1)} %bitcast.8), calls=%async_computation.2 | async-start | bytes 393216 | tf_op jit(solution)/shard_map/all_to_all | solution.py:45
  71.4 1.2 copy-start.2
  72.5 27.8 %copy-start.8 = (bf16[192,4096]{1,0:T(8,128)(2,1)}, bf16[192,4096]{1,0:T(8,128)(2,1)S(1)}, u32[]{:S(2)}) copy-start(bf16[192,4096]{1,0:T(8,128)(2,1)S(1)} %collective-permute-done.2.refs_3_) | copy-start | bytes 4718596
  87.3 13.0 %all-to-all-start.3 = ((bf16[4,24,4096]{2,1,0:T(8,128)(2,1)}), bf16[4,24,4096]{2,1,0:T(8,128)(2,1)S(1)}, u32[]{:S(2)}, u32[]{:S(2)}) async-start(bf16[4,24,4096]{2,1,0:T(8,128)(2,1)} %shard_map.120), calls=%async_computation.3 | async-start | bytes 1572864 | tf_op jit(solution)/shard_map/all_to_all | solution.py:174
  102.4 27.1 %copy-start = (bf16[1,192,4096]{2,1,0:T(8,128)(2,1)S(1)}, bf16[1,192,4096]{2,1,0:T(8,128)(2,1)}, u32[]{:S(2)}) copy-start(bf16[1,192,4096]{2,1,0:T(8,128)(2,1)} %param.19) | copy-start | bytes 4718596
  102.4 27.1 %copy-start.1 = (bf16[1,192,4096]{2,1,0:T(8,128)(2,1)S(1)}, bf16[1,192,4096]{2,1,0:T(8,128)(2,1)}, u32[]{:S(2)}) copy-start(bf16[1,192,4096]{2,1,0:T(8,128)(2,1)} %param.20) | copy-start | bytes 4718596
  102.4 27.1 %all-to-all-start.4 = ((bf16[4,96,4096]{2,1,0:T(8,128)(2,1)}), bf16[4,96,4096]{2,1,0:T(8,128)(2,1)}, u32[]{:S(2)}, u32[]{:S(2)}) async-start(bf16[4,96,4096]{2,1,0:T(8,128)(2,1)} %shard_map.121), calls=%async_computation.4 | async-start | bytes 6291456 | tf_op jit(solution)/shard_map/all_to_all | solution.py:174
  107.3 6.8 %collective-permute-start.4 = (f32[32,256]{1,0:T(8,128)S(1)}, f32[32,256]{1,0:T(8,128)S(1)}, u32[]{:S(2)}, u32[]{:S(2)}) collective-permute-start(f32[32,256]{1,0:T(8,128)S(1)} %get-tuple-element.22), channel_id=1, source_target_pairs={{0,0},{1,16},{2,32},{3,48},{4,64},{5,80},{6,96},{7,112},{8,128},{9... | collective-permute-start | bytes 98312 | tf_op jit(solution)/shard_map/ppermute | solution.py:206
  129.5 1.4 copy-start.3
  164.8 12.2 %copy-start.4 = (bf16[2,384,384]{2,1,0:T(8,128)(2,1)S(1)}, bf16[2,384,384]{2,1,0:T(8,128)(2,1)}, u32[]{:S(2)}) copy-start(bf16[2,384,384]{2,1,0:T(8,128)(2,1)} %constant.38.clone.order_ref) | copy-start | bytes 1769476
  164.8 19.4 %copy-start.9 = (f32[1,32,8]{1,2,0:T(8,128)S(1)}, f32[1,32,8]{1,2,0:T(8,128)}, u32[]{:S(2)}) copy-start(f32[1,32,8]{1,2,0:T(8,128)} %param.18) | copy-start | bytes 3076
  178.0 19.5 %all-to-all-start.7 = ((bf16[16,24,256]{2,1,0:T(8,128)(2,1)}), bf16[16,24,256]{2,1,0:T(8,128)(2,1)S(1)}, u32[]{:S(2)}, u32[]{:S(2)}) async-start(bf16[16,24,256]{2,1,0:T(8,128)(2,1)} %bitcast.15), calls=%async_computation.7 | async-start | bytes 393216 | tf_op jit(solution)/shard_map/all_to_all | solution.py:45

commit v3 on v2

--- a/solution.py
+++ b/solution.py
@@ -9,6 +9,7 @@
 
 CAP = 12
 LINE = 4
+UNITS = 192
 GROUP = LINE * CAP
 TOK = 32
 COLS = 256
@@ -23,17 +24,17 @@
 F32 = jnp.float32
 
 VMEM = pl.BlockSpec(memory_space=pltpu.VMEM)
+HBM = pl.BlockSpec(memory_space=pltpu.HBM)
 SMEM = pl.BlockSpec(memory_space=pltpu.SMEM)
 
 
-def call(kernel, out_shape, scalars, arrays, flops=0, moved=0):
+def call(kernel, out_shape, scalars, arrays, mib=12):
     return pl.pallas_call(
         kernel,
         out_shape=out_shape,
         in_specs=[SMEM] * len(scalars) + [VMEM] * len(arrays),
         out_specs=jax.tree.map(lambda _: VMEM, out_shape),
-        compiler_params=pltpu.CompilerParams(vmem_limit_bytes=48 * 1024 * 1024),
-        cost_estimate=pl.CostEstimate(flops=flops, bytes_accessed=moved, transcendentals=0),
+        compiler_params=pltpu.CompilerParams(vmem_limit_bytes=mib << 20),
     )(*scalars, *arrays)
 
 
@@ -89,25 +90,58 @@
 
 
 def expert_kernel(core_ref, rows_ref, *refs):
-    weights, out_ref = refs[:-1], refs[-1]
+    sources, out_ref, rows_held, held, staged, sems = refs[:6], *refs[6:]
+
+    def load_rows(number):
+        copies = []
+        for source in range(LINE):
+            at = pl.ds(number * GROUP, GROUP)
+            to = pl.ds(source * GROUP, GROUP)
+            sem = sems.at[6 + LINE + number * LINE + source]
+            copies.append(
+                pltpu.make_async_copy(rows_ref.at[source, at], rows_held.at[number, to], sem)
+            )
+            copies[-1].start()
+        return copies
+
+    def load(index):
+        copy = pltpu.make_async_copy(sources[index], held.at[index], sems.at[index])
+        copy.start()
+        return copy
+
+    rows_copies, gates, ups = [], [], []
+    for number in range(2):
+        rows_copies.append(load_rows(number))
+        gates.append(load(number))
+        ups.append(load(2 + number))
+    downs = [load(4), load(5)]
     contract = (((1,), (1,)), ((), ()))
     hidden = []
     for number in range(2):
-        gate_ref, up_ref = weights[number], weights[2 + number]
-        rows = rows_ref[:, number * GROUP : (number + 1) * GROUP, :].reshape(LINE * GROUP, WIDTH)
-        gate = lax.dot_general(rows, gate_ref[...], contract, preferred_element_type=F32)
-        up = lax.dot_general(rows, up_ref[...], contract, preferred_element_type=F32)
+        for copy in rows_copies[number]:
+            copy.wait()
+        gates[number].wait()
+        rows = rows_held[number]
+        gate = lax.dot_general(rows, held[number], contract, preferred_element_type=F32)
+        ups[number].wait()
+        up = lax.dot_general(rows, held[2 + number], contract, preferred_element_type=F32)
         hidden.append((gate / (1.0 + jnp.exp(-gate)) * up).astype(BF16))
+    for copy in downs:
+        copy.wait()
     first = core_ref[0] == 0
+    writes = []
     for peer in range(LINE):
         for sub in range(LINE):
             block = jnp.where(first, sub * LINE + peer, peer * LINE + sub)
             at = pl.ds(pl.multiple_of(block * COLS, COLS), COLS)
             for number in range(2):
-                value = jnp.dot(
-                    hidden[number], weights[4 + number][:, at], preferred_element_type=F32
-                )
-                out_ref[peer, sub * 2 + number] = value.astype(BF16)
+                value = jnp.dot(hidden[number], held[4 + number, :, at], preferred_element_type=F32)
+                staged[peer, sub * 2 + number] = value.astype(BF16)
+        write = pltpu.make_async_copy(staged.at[peer], out_ref.at[peer], sems.at[6 + peer])
+        write.start()
+        writes.append(write)
+    for write in writes:
+        write.wait()
 
 
 def add_kernel(parts_ref, out_ref):
@@ -208,7 +242,6 @@
     for weight in (w_gate[0], w_up[0], w_down[0]):
         weights += [weight, lax.ppermute(weight, "tok", [(0, 1), (1, 0)])]
     rows = exchange(picked.reshape(EXPS, 2 * CAP, COLS), "exp")
-    rows, *weights = lax.optimization_barrier((rows, *weights))
     normed = call(
         norm_kernel,
         shape_of(LINE, 2 * CAP, WIDTH),
@@ -224,12 +257,19 @@
     )
     arrived = exchange_lines(forward, second_lines)
     arrived, resid = lax.optimization_barrier((arrived, resid))
-    produced = call(
+    produced = pl.pallas_call(
         expert_kernel,
-        shape_of(LINE, 2 * LINE, LINE * GROUP, COLS),
-        [core],
-        [arrived, *weights],
-    )
+        out_shape=shape_of(LINE, 2 * LINE, LINE * GROUP, COLS),
+        in_specs=[SMEM] + [HBM] * 7,
+        out_specs=HBM,
+        scratch_shapes=[
+            pltpu.VMEM((2, LINE * GROUP, WIDTH), BF16),
+            pltpu.VMEM((6, UNITS, WIDTH), BF16),
+            pltpu.VMEM((LINE, 2 * LINE, LINE * GROUP, COLS), BF16),
+            pltpu.SemaphoreType.DMA((6 + 3 * LINE,)),
+        ],
+        compiler_params=pltpu.CompilerParams(vmem_limit_bytes=59 << 20),
+    )(core, arrived, *weights)
     summed = call(
         add_kernel,
         shape_of(2 * LINE, LINE * GROUP, COLS),

time: 199 us -> 194 us (0.975)
  blocking collectives: 62.5 us -> 85.7 us
  waiting for transfers between devices: 62.4 us -> 49.3 us
  starting transfers between devices: 51.8 us -> 39.7 us
  local copies, waits for them, and re-layouts: 6.62 us -> 4.05 us
    all_to_all x1 -> x2, blocking collectives: 24.4 us -> 44.1 us  [exchange(): return lax.all_to_all(x, axes, split_axis=0, concat_axis=0, tiled=True)]
    all_to_all x3 -> x2, waiting for transfers between devices: 29.3 us -> 16.1 us  [exchange(): return lax.all_to_all(x, axes, split_axis=0, concat_axis=0, tiled=True)]
    all_to_all x3 -> x2, starting transfers between devices: 31.7 us -> 20.2 us  [exchange(): return lax.all_to_all(x, axes, split_axis=0, concat_axis=0, tiled=True)]
    pallas_call x8 -> x7, Pallas kernels: 14.3 us -> 5.89 us  [call(): pl.pallas_call(kernel, out_shape=out_shape, in_specs=[SMEM] * len(scalars...]
    pallas_call x0 -> x1, Pallas kernels: none -> 8.03 us  [on_device(): pl.pallas_call(expert_kernel, out_shape=shape_of(LINE, 2 * LINE, LINE * G...]
    all_to_all x2, waiting for transfers between devices: 24.8 us -> 18.6 us  [exchange_lines(): lax.all_to_all(x, PLANE, split_axis=0, concat_axis=0, tiled=True, axis_in...]
    ppermute x1, waiting for transfers between devices: 3.98 us -> 9.76 us  [on_device(): lax.ppermute(jnp.concatenate([stream[0], routes], axis=0), turned, turn)]
    all_to_all x2, blocking collectives: 38 us -> 41.6 us  [exchange_lines(): lax.all_to_all(x, PLANE, split_axis=0, concat_axis=0, tiled=True, axis_in...]
  transfers between devices with their start and end apart: 10 -> 9, of which waited for: 7 -> 6; matrix products, arithmetic and copies ran while one was open for 1% -> 1% of each run, Pallas kernels for 1% -> 0%
where the time goes in v3:
time: 194 us; the launch traced here: 193 us
  blocking collectives  85.7 us (44%)
  waiting for transfers between devices  49.3 us (25%)
  starting transfers between devices  39.7 us (20%)
  Pallas kernels  13.9 us (7%)
  local copies, waits for them, and re-layouts  4.05 us (2%)
    all_to_all x2, blocking collectives, exchange(): return lax.all_to_all(x, axes, split_axis=0, concat_axis=0, tiled=True)  44.1 us
    all_to_all x2, blocking collectives, exchange_lines(): lax.all_to_all(x, PLANE, split_axis=0, concat_axis=0, tiled=True, axis_in...  41.6 us
    all_to_all x2, starting transfers between devices, exchange(): return lax.all_to_all(x, axes, split_axis=0, concat_axis=0, tiled=True)  20.2 us
    all_to_all x2, waiting for transfers between devices, exchange_lines(): lax.all_to_all(x, PLANE, split_axis=0, concat_axis=0, tiled=True, axis_in...  18.6 us
    all_to_all x2, waiting for transfers between devices, exchange(): return lax.all_to_all(x, axes, split_axis=0, concat_axis=0, tiled=True)  16.1 us
    ppermute x1, waiting for transfers between devices, on_device(): lax.ppermute(jnp.concatenate([stream[0], routes], axis=0), turned, turn)  9.76 us
    all_to_all x2, starting transfers between devices, exchange_lines(): lax.all_to_all(x, PLANE, split_axis=0, concat_axis=0, tiled=True, axis_in...  8.39 us
    pallas_call x1, Pallas kernels, on_device(): pl.pallas_call(expert_kernel, out_shape=shape_of(LINE, 2 * LINE, LINE * G...  8.03 us
  transfers between devices with their start and end apart: 9, of which 6 were waited for; matrix products, arithmetic and copies ran while one was open for 1% of the time, Pallas kernels for 0%

profile of v3, /device:TPU:32, one launch (start us, length us, event | category | flops | bytes accessed | tf_op | source)
XLA Modules:
  0.0 193.5 jit_solution(15823789429550651326)
XLA Ops:
  0.0 1.5 broadcast_in_dim.12
  1.5 15.2 %all-to-all-start = ((bf16[16,32,256]{2,1,0:T(8,128)(2,1)}), bf16[16,32,256]{2,1,0:T(8,128)(2,1)S(1)}, u32[]{:S(2)}, u32[]{:S(2)}) async-start(bf16[16,32,256]{2,1,0:T(8,128)(2,1)} %broadcast_in_dim.12), calls=%async_computation | async-start | bytes 524288 | tf_op jit(solution)/shard_map/all_to_all | solution.py:46
  16.7 0.8 copy.13
  17.4 0.8 copy.14
  18.2 0.1 copy.17
  18.3 0.8 select_maximum_fusion
  19.0 2.9 %collective-permute-start = (f32[40,256]{1,0:T(8,128)S(1)}, f32[40,256]{1,0:T(8,128)S(1)}, u32[]{:S(2)}, u32[]{:S(2)}) collective-permute-start(f32[40,256]{1,0:T(8,128)S(1)} %select_maximum_fusion), channel_id=1, source_target_pairs={{0,0},{1,16},{2,32},{3,48},{4,64},{5,80},{6,96},{7,112},{8,128},{9... | collective-permute-start | bytes 122888 | tf_op jit(solution)/shard_map/ppermute | solution.py:227
  22.0 9.8 %collective-permute-done.turned_ref = f32[40,256]{1,0:T(8,128)S(1)} collective-permute-done((f32[40,256]{1,0:T(8,128)S(1)}, f32[40,256]{1,0:T(8,128)S(1)}, u32[]{:S(2)}, u32[]{:S(2)}) %collective-permute-start) | collective-permute-done | bytes 40992 | tf_op jit(solution)/shard_map/ppermute | solution.py:227
  31.7 2.6 %all-to-all-done = bf16[16,32,256]{2,1,0:T(8,128)(2,1)S(1)} async-done(((bf16[16,32,256]{2,1,0:T(8,128)(2,1)}), bf16[16,32,256]{2,1,0:T(8,128)(2,1)S(1)}, u32[]{:S(2)}, u32[]{:S(2)}) %all-to-all-start) | async-done | bytes 262176 | tf_op jit(solution)/shard_map/all_to_all | solution.py:46
  34.4 0.0 copy-start.1
  34.4 0.9 copy-done.1
  35.3 0.2 shard_map.118
  35.5 18.7 %all_to_all.40.parts_ref = bf16[16,32,256]{2,1,0:T(8,128)(2,1)S(1)} all-to-all(bf16[16,32,256]{2,1,0:T(8,128)(2,1)S(1)} %bitcast.55), channel_id=1, replica_groups=mesh['tok'=2,'head_0'=4,'head_1'=4,'exp'=16] {'head_0','head_1'}, dimensions={0} | all-to-all | bytes 524288 | tf_op jit(solution)/shard_map/all_to_all | solution.py:46
  54.3 0.0 copy-start.2
  54.3 0.3 shard_map.119
  54.5 25.3 %all_to_all.41.rows_ref = bf16[16,24,256]{2,1,0:T(8,128)(2,1)S(1)} all-to-all(bf16[16,24,256]{2,1,0:T(8,128)(2,1)S(1)} %bitcast.57), channel_id=1, replica_groups=mesh['tok'=2,'head_0'=4,'head_1'=4,'exp'=16] {'exp'}, dimensions={0} | all-to-all | bytes 393216 | tf_op jit(solution)/shard_map/all_to_all | solution.py:46
  79.9 0.0 copy-done.3
  79.9 1.0 shard_map.120
  80.9 3.5 %all-to-all-start.3 = ((bf16[4,24,4096]{2,1,0:T(8,128)(2,1)}), bf16[4,24,4096]{2,1,0:T(8,128)(2,1)S(1)}, u32[]{:S(2)}, u32[]{:S(2)}) async-start(bf16[4,24,4096]{2,1,0:T(8,128)(2,1)} %shard_map.120), calls=%async_computation.3 | async-start | bytes 1572864 | tf_op jit(solution)/shard_map/all_to_all | solution.py:208
  84.4 9.4 %all-to-all-done.3 = bf16[4,24,4096]{2,1,0:T(8,128)(2,1)S(1)} async-done(((bf16[4,24,4096]{2,1,0:T(8,128)(2,1)}), bf16[4,24,4096]{2,1,0:T(8,128)(2,1)S(1)}, u32[]{:S(2)}, u32[]{:S(2)}) %all-to-all-start.3) | async-done | bytes 786464 | tf_op jit(solution)/shard_map/all_to_all | solution.py:208
  93.9 0.0 copy-done.2
  93.9 2.1 %shard_map.121 = bf16[4,96,4096]{2,1,0:T(8,128)(2,1)} custom-call(s32[1]{0:T(128)} %bitcast.core_ref, bf16[96,4096]{1,0:T(8,128)(2,1)S(1)} %bitcast.52, bf16[2,96,96]{2,1,0:T(8,128)(2,1)S(1)} %copy-done.2), custom_call_target="tpu_custom_call" | custom-call | tf_op jit(solution)/shard_map/pallas_call | solution.py:32
  95.9 0.0 copy-start.4
  96.0 4.9 %all-to-all-start.4 = ((bf16[4,96,4096]{2,1,0:T(8,128)(2,1)}), bf16[4,96,4096]{2,1,0:T(8,128)(2,1)}, u32[]{:S(2)}, u32[]{:S(2)}) async-start(bf16[4,96,4096]{2,1,0:T(8,128)(2,1)} %shard_map.121), calls=%async_computation.4 | async-start | bytes 6291456 | tf_op jit(solution)/shard_map/all_to_all | solution.py:208
  100.9 0.0 copy-done.4
  100.9 1.9 collective-permute-start.2
  102.8 0.0 copy-done.5
  102.8 2.4 %collective-permute-start.3 = (bf16[192,4096]{1,0:T(8,128)(2,1)S(1)}, bf16[192,4096]{1,0:T(8,128)(2,1)}, u32[]{:S(2)}, u32[]{:S(2)}) collective-permute-start(bf16[192,4096]{1,0:T(8,128)(2,1)S(1)} %bitcast.63), channel_id=1, source_target_pairs={{0,256},{256,0},{1,257},{257,1},{2,258},{258,2},{3,259},{259,3},{4... | collective-permute-start | bytes 4718600 | tf_op jit(solution)/shard_map/ppermute | solution.py:243
  105.2 1.9 collective-permute-start.4
  107.2 1.9 collective-permute-start.1
  109.1 4.8 %collective-permute-done.1.resid_ref = f32[32,256]{1,0:T(8,128)S(1)} collective-permute-done((f32[32,256]{1,0:T(8,128)S(1)}, f32[32,256]{1,0:T(8,128)S(1)}, u32[]{:S(2)}, u32[]{:S(2)}) %collective-permute-start.1) | collective-permute-done | bytes 32800 | tf_op jit(solution)/shard_map/ppermute | solution.py:240
  113.9 9.2 %all-to-all-done.4.rows_ref = bf16[4,96,4096]{2,1,0:T(8,128)(2,1)} async-done(((bf16[4,96,4096]{2,1,0:T(8,128)(2,1)}), bf16[4,96,4096]{2,1,0:T(8,128)(2,1)}, u32[]{:S(2)}, u32[]{:S(2)}) %all-to-all-start.4) | async-done | bytes 3145760 | tf_op jit(solution)/shard_map/all_to_all | solution.py:208
  123.0 0.0 collective-permute-done.2.refs_1_
  123.0 0.0 collective-permute-done.3.refs_3_
  123.1 0.0 collective-permute-done.4.refs_5_
  123.1 8.0 %shard_map.122 = bf16[4,8,192,256]{3,2,1,0:T(8,128)(2,1)} custom-call(s32[1]{0:T(128)} %bitcast.core_ref, bf16[4,96,4096]{2,1,0:T(8,128)(2,1)} %all-to-all-done.4.rows_ref, bf16[192,4096]{1,0:T(8,128)(2,1)} %bitcast.60, bf16[192,4096]{1,0:T(8,128)(2,1)} %collective-permute-done.2.refs_1_, bf16[192,4096]{1,0:T(8,128)(2,1)} %bitcast.62, ...), custom_call_target="tpu_custom_call" | custom-call | tf_op jit(solution)/shard_map/pallas_call | solution.py:260
  131.1 25.8 %all_to_all.42.parts_ref = bf16[4,8,192,256]{3,2,1,0:T(8,128)(2,1)S(1)} all-to-all(bf16[4,8,192,256]{3,2,1,0:T(8,128)(2,1)} %shard_map.122), channel_id=1, replica_groups={{0,16,32,48},{64,80,96,112},{128,144,160,176},{192,208,224,240},{256,32..., dimensions={0} | all-to-all | bytes 6291456 | tf_op jit(solution)/shard_map/all_to_all | solution.py:208
  156.9 0.4 shard_map.123
  157.3 0.0 copy-start
  157.3 0.0 copy-start.6
  157.3 15.8 %all_to_all.43.parts_ref = bf16[4,384,256]{2,1,0:T(8,128)(2,1)S(1)} all-to-all(bf16[4,384,256]{2,1,0:T(8,128)(2,1)S(1)} %bitcast.53), channel_id=1, replica_groups={{0,64,128,192},{16,80,144,208},{32,96,160,224},{48,112,176,240},{256,27..., dimensions={0} | all-to-all | bytes 1572864 | tf_op jit(solution)/shard_map/all_to_all | solution.py:208
  173.1 0.0 copy-done
  173.1 1.0 shard_map.124
  174.1 5.0 %all-to-all-start.7 = ((bf16[16,24,256]{2,1,0:T(8,128)(2,1)}), bf16[16,24,256]{2,1,0:T(8,128)(2,1)S(1)}, u32[]{:S(2)}, u32[]{:S(2)}) async-start(bf16[16,24,256]{2,1,0:T(8,128)(2,1)} %bitcast.15), calls=%async_computation.7 | async-start | bytes 393216 | tf_op jit(solution)/shard_map/all_to_all | solution.py:46
  179.1 0.0 copy-done.6
  179.1 0.1 copy.16
  179.1 13.5 %all-to-all-done.7 = bf16[16,24,256]{2,1,0:T(8,128)(2,1)S(1)} async-done(((bf16[16,24,256]{2,1,0:T(8,128)(2,1)}), bf16[16,24,256]{2,1,0:T(8,128)(2,1)S(1)}, u32[]{:S(2)}, u32[]{:S(2)}) %all-to-all-start.7) | async-done | bytes 196640 | tf_op jit(solution)/shard_map/all_to_all | solution.py:46
  192.6 0.9 shard_map.125
  (3 shorter events, 0.0 us)
Async XLA Ops:
  0.0 79.9 %copy-start.3 = (f32[4096]{0:T(1024)S(1)}, f32[4096]{0:T(1024)}, u32[]{:S(2)}) copy-start(f32[4096]{0:T(1024)} %param.15) | copy-start | bytes 49156
  1.5 32.9 %all-to-all-start = ((bf16[16,32,256]{2,1,0:T(8,128)(2,1)}), bf16[16,32,256]{2,1,0:T(8,128)(2,1)S(1)}, u32[]{:S(2)}, u32[]{:S(2)}) async-start(bf16[16,32,256]{2,1,0:T(8,128)(2,1)} %broadcast_in_dim.12), calls=%async_computation | async-start | bytes 524288 | tf_op jit(solution)/shard_map/all_to_all | solution.py:46
  19.0 12.7 %collective-permute-start = (f32[40,256]{1,0:T(8,128)S(1)}, f32[40,256]{1,0:T(8,128)S(1)}, u32[]{:S(2)}, u32[]{:S(2)}) collective-permute-start(f32[40,256]{1,0:T(8,128)S(1)} %select_maximum_fusion), channel_id=1, source_target_pairs={{0,0},{1,16},{2,32},{3,48},{4,64},{5,80},{6,96},{7,112},{8,128},{9... | collective-permute-start | bytes 122888 | tf_op jit(solution)/shard_map/ppermute | solution.py:227
  34.4 0.9 copy-start.1
  54.3 39.6 %copy-start.2 = (bf16[2,96,96]{2,1,0:T(8,128)(2,1)S(1)}, bf16[2,96,96]{2,1,0:T(8,128)(2,1)}, u32[]{:S(2)}) copy-start(bf16[2,96,96]{2,1,0:T(8,128)(2,1)} %constant.37.clone.order_ref) | copy-start | bytes 110596
  80.9 13.0 %all-to-all-start.3 = ((bf16[4,24,4096]{2,1,0:T(8,128)(2,1)}), bf16[4,24,4096]{2,1,0:T(8,128)(2,1)S(1)}, u32[]{:S(2)}, u32[]{:S(2)}) async-start(bf16[4,24,4096]{2,1,0:T(8,128)(2,1)} %shard_map.120), calls=%async_computation.3 | async-start | bytes 1572864 | tf_op jit(solution)/shard_map/all_to_all | solution.py:208
  95.9 4.9 %copy-start.4 = (bf16[1,192,4096]{2,1,0:T(8,128)(2,1)S(1)}, bf16[1,192,4096]{2,1,0:T(8,128)(2,1)}, u32[]{:S(2)}) copy-start(bf16[1,192,4096]{2,1,0:T(8,128)(2,1)} %param.19) | copy-start | bytes 4718596
  95.9 6.9 %copy-start.5 = (bf16[1,192,4096]{2,1,0:T(8,128)(2,1)S(1)}, bf16[1,192,4096]{2,1,0:T(8,128)(2,1)}, u32[]{:S(2)}) copy-start(bf16[1,192,4096]{2,1,0:T(8,128)(2,1)} %param.20) | copy-start | bytes 4718596
  96.0 27.1 %all-to-all-start.4 = ((bf16[4,96,4096]{2,1,0:T(8,128)(2,1)}), bf16[4,96,4096]{2,1,0:T(8,128)(2,1)}, u32[]{:S(2)}, u32[]{:S(2)}) async-start(bf16[4,96,4096]{2,1,0:T(8,128)(2,1)} %shard_map.121), calls=%async_computation.4 | async-start | bytes 6291456 | tf_op jit(solution)/shard_map/all_to_all | solution.py:208
  100.9 22.2 %collective-permute-start.2 = (bf16[192,4096]{1,0:T(8,128)(2,1)S(1)}, bf16[192,4096]{1,0:T(8,128)(2,1)}, u32[]{:S(2)}, u32[]{:S(2)}) collective-permute-start(bf16[192,4096]{1,0:T(8,128)(2,1)S(1)} %bitcast.61), channel_id=1, source_target_pairs={{0,256},{256,0},{1,257},{257,1},{2,258},{258,2},{3,259},{259,3},{4... | collective-permute-start | bytes 4718600 | tf_op jit(solution)/shard_map/ppermute | solution.py:243
  102.8 20.2 %collective-permute-start.3 = (bf16[192,4096]{1,0:T(8,128)(2,1)S(1)}, bf16[192,4096]{1,0:T(8,128)(2,1)}, u32[]{:S(2)}, u32[]{:S(2)}) collective-permute-start(bf16[192,4096]{1,0:T(8,128)(2,1)S(1)} %bitcast.63), channel_id=1, source_target_pairs={{0,256},{256,0},{1,257},{257,1},{2,258},{258,2},{3,259},{259,3},{4... | collective-permute-start | bytes 4718600 | tf_op jit(solution)/shard_map/ppermute | solution.py:243
  105.2 17.8 %collective-permute-start.4 = (bf16[192,4096]{1,0:T(8,128)(2,1)}, bf16[192,4096]{1,0:T(8,128)(2,1)}, u32[]{:S(2)}, u32[]{:S(2)}) collective-permute-start(bf16[192,4096]{1,0:T(8,128)(2,1)} %bitcast.64), channel_id=1, source_target_pairs={{0,256},{256,0},{1,257},{257,1},{2,258},{258,2},{3,259},{259,3},{4... | collective-permute-start | bytes 4718600 | tf_op jit(solution)/shard_map/ppermute | solution.py:243
  107.2 6.7 %collective-permute-start.1 = (f32[32,256]{1,0:T(8,128)S(1)}, f32[32,256]{1,0:T(8,128)S(1)}, u32[]{:S(2)}, u32[]{:S(2)}) collective-permute-start(f32[32,256]{1,0:T(8,128)S(1)} %get-tuple-element.14), channel_id=1, source_target_pairs={{0,0},{1,16},{2,32},{3,48},{4,64},{5,80},{6,96},{7,112},{8,128},{9... | collective-permute-start | bytes 98312 | tf_op jit(solution)/shard_map/ppermute | solution.py:240
  157.3 15.8 %copy-start = (bf16[2,384,384]{2,1,0:T(8,128)(2,1)S(1)}, bf16[2,384,384]{2,1,0:T(8,128)(2,1)}, u32[]{:S(2)}) copy-start(bf16[2,384,384]{2,1,0:T(8,128)(2,1)} %constant.38.clone.order_ref) | copy-start | bytes 1769476
  157.3 21.8 %copy-start.6 = (f32[1,32,8]{1,2,0:T(8,128)S(1)}, f32[1,32,8]{1,2,0:T(8,128)}, u32[]{:S(2)}) copy-start(f32[1,32,8]{1,2,0:T(8,128)} %param.18) | copy-start | bytes 3076
  174.1 18.5 %all-to-all-start.7 = ((bf16[16,24,256]{2,1,0:T(8,128)(2,1)}), bf16[16,24,256]{2,1,0:T(8,128)(2,1)S(1)}, u32[]{:S(2)}, u32[]{:S(2)}) async-start(bf16[16,24,256]{2,1,0:T(8,128)(2,1)} %bitcast.15), calls=%async_computation.7 | async-start | bytes 393216 | tf_op jit(solution)/shard_map/all_to_all | solution.py:46

commit v4 on v3

--- a/solution.py
+++ b/solution.py
@@ -80,53 +80,55 @@
             out_ref[peer, :, at] = value
 
 
-def forward_kernel(core_ref, rows_ref, order_ref, out_ref):
+def forward_kernel(core_ref, rows_ref, order_ref, out_ref, held, sems):
     order = order_ref[core_ref[0]]
-    for block in range(HEADS):
-        at = slice(block * COLS, (block + 1) * COLS)
-        value = jnp.dot(order, rows_ref[:, at], preferred_element_type=F32).astype(BF16)
+    writes = []
+    for part in range(LINE):
+        for block in range(part * LINE, (part + 1) * LINE):
+            at = slice(block * COLS, (block + 1) * COLS)
+            value = jnp.dot(order, rows_ref[:, at], preferred_element_type=F32)
+            held[:, at] = value.astype(BF16)
+        at = pl.ds(part * LINE * COLS, LINE * COLS)
         for peer in range(LINE):
-            out_ref[peer, :, at] = value
+            sem = sems.at[part * LINE + peer]
+            writes.append(pltpu.make_async_copy(held.at[:, at], out_ref.at[peer, :, at], sem))
+            writes[-1].start()
+    for write in writes:
+        write.wait()
 
 
 def expert_kernel(core_ref, rows_ref, *refs):
-    sources, out_ref, rows_held, held, staged, sems = refs[:6], *refs[6:]
-
-    def load_rows(number):
+    sources, out_ref, rows_held, both, downs, staged, sems = refs[:6], *refs[6:]
+    started = []
+
+    def start(source, target):
+        copy = pltpu.make_async_copy(source, target, sems.at[len(started)])
+        copy.start()
+        started.append(copy)
+        return copy
+
+    inputs = []
+    for number in range(2):
         copies = []
         for source in range(LINE):
             at = pl.ds(number * GROUP, GROUP)
             to = pl.ds(source * GROUP, GROUP)
-            sem = sems.at[6 + LINE + number * LINE + source]
-            copies.append(
-                pltpu.make_async_copy(rows_ref.at[source, at], rows_held.at[number, to], sem)
-            )
-            copies[-1].start()
-        return copies
-
-    def load(index):
-        copy = pltpu.make_async_copy(sources[index], held.at[index], sems.at[index])
-        copy.start()
-        return copy
-
-    rows_copies, gates, ups = [], [], []
-    for number in range(2):
-        rows_copies.append(load_rows(number))
-        gates.append(load(number))
-        ups.append(load(2 + number))
-    downs = [load(4), load(5)]
+            copies.append(start(rows_ref.at[source, at], rows_held.at[number, to]))
+        copies.append(start(sources[number], both.at[number, pl.ds(0, UNITS)]))
+        copies.append(start(sources[2 + number], both.at[number, pl.ds(UNITS, UNITS)]))
+        inputs.append(copies)
+    lasts = [start(sources[4 + number], downs.at[number]) for number in range(2)]
     contract = (((1,), (1,)), ((), ()))
     hidden = []
     for number in range(2):
-        for copy in rows_copies[number]:
+        for copy in inputs[number]:
             copy.wait()
-        gates[number].wait()
-        rows = rows_held[number]
-        gate = lax.dot_general(rows, held[number], contract, preferred_element_type=F32)
-        ups[number].wait()
-        up = lax.dot_general(rows, held[2 + number], contract, preferred_element_type=F32)
-        hidden.append((gate / (1.0 + jnp.exp(-gate)) * up).astype(BF16))
-    for copy in downs:
+        product = lax.dot_general(
+            rows_held[number], both[number], contract, preferred_element_type=F32
+        ).T
+        gate, up = product[:UNITS], product[UNITS:]
+        hidden.append((gate / (1.0 + jnp.exp(-gate)) * up).astype(BF16).T)
+    for copy in lasts:
         copy.wait()
     first = core_ref[0] == 0
     writes = []
@@ -135,11 +137,9 @@
             block = jnp.where(first, sub * LINE + peer, peer * LINE + sub)
             at = pl.ds(pl.multiple_of(block * COLS, COLS), COLS)
             for number in range(2):
-                value = jnp.dot(hidden[number], held[4 + number, :, at], preferred_element_type=F32)
+                value = jnp.dot(hidden[number], downs[number, :, at], preferred_element_type=F32)
                 staged[peer, sub * 2 + number] = value.astype(BF16)
-        write = pltpu.make_async_copy(staged.at[peer], out_ref.at[peer], sems.at[6 + peer])
-        write.start()
-        writes.append(write)
+        writes.append(start(staged.at[peer], out_ref.at[peer]))
     for write in writes:
         write.wait()
 
@@ -227,6 +227,9 @@
     stream_turned = lax.ppermute(jnp.concatenate([stream[0], routes], axis=0), turned, turn)
     got, stream_turned = lax.optimization_barrier((got, stream_turned))
 
+    weights = []
+    for weight in (w_gate[0], w_up[0], w_down[0]):
+        weights += [weight, lax.ppermute(weight, "tok", [(0, 1), (1, 0)])]
     partial = call(
         project_kernel, shape_of(EXPS * TOK, COLS), [], [got.reshape(EXPS * TOK, COLS), out_proj]
     )
@@ -238,9 +241,6 @@
         [parts, stream_turned],
     )
     resid = lax.ppermute(resid_turned, turned, turn)
-    weights = []
-    for weight in (w_gate[0], w_up[0], w_down[0]):
-        weights += [weight, lax.ppermute(weight, "tok", [(0, 1), (1, 0)])]
     rows = exchange(picked.reshape(EXPS, 2 * CAP, COLS), "exp")
     normed = call(
         norm_kernel,
@@ -249,12 +249,18 @@
         [rows, norm_gain.reshape(1, WIDTH)],
     )
     line = exchange_lines(normed, first_lines)
-    forward = call(
+    line, *weights[1::2] = lax.optimization_barrier((line, *weights[1::2]))
+    forward = pl.pallas_call(
         forward_kernel,
-        shape_of(LINE, 2 * GROUP, WIDTH),
-        [core],
-        [line.reshape(2 * GROUP, WIDTH), forward_order()],
-    )
+        out_shape=shape_of(LINE, 2 * GROUP, WIDTH),
+        in_specs=[SMEM, VMEM, VMEM],
+        out_specs=HBM,
+        scratch_shapes=[
+            pltpu.VMEM((2 * GROUP, WIDTH), BF16),
+            pltpu.SemaphoreType.DMA((LINE * LINE,)),
+        ],
+        compiler_params=pltpu.CompilerParams(vmem_limit_bytes=12 << 20),
+    )(core, line.reshape(2 * GROUP, WIDTH), forward_order())
     arrived = exchange_lines(forward, second_lines)
     arrived, resid = lax.optimization_barrier((arrived, resid))
     produced = pl.pallas_call(
@@ -264,7 +270,8 @@
         out_specs=HBM,
         scratch_shapes=[
             pltpu.VMEM((2, LINE * GROUP, WIDTH), BF16),
-            pltpu.VMEM((6, UNITS, WIDTH), BF16),
+            pltpu.VMEM((2, 2 * UNITS, WIDTH), BF16),
+            pltpu.VMEM((2, UNITS, WIDTH), BF16),
             pltpu.VMEM((LINE, 2 * LINE, LINE * GROUP, COLS), BF16),
             pltpu.SemaphoreType.DMA((6 + 3 * LINE,)),
         ],

time: 194 us -> 194 us (level)
  the two profiles are of different devices: /device:TPU:32 before, /device:TPU:2 now
where the time goes in v4:
time: 194 us; the launch traced here: 193 us
  blocking collectives  62.5 us (32%)
  starting transfers between devices  57.1 us (29%)
  waiting for transfers between devices  54.2 us (28%)
  Pallas kernels  14.1 us (7%)
  local copies, waits for them, and re-layouts  4.05 us (2%)
    all_to_all x2, blocking collectives, exchange_lines(): lax.all_to_all(x, PLANE, split_axis=0, concat_axis=0, tiled=True, axis_in...  37.9 us
    all_to_all x3, starting transfers between devices, exchange(): return lax.all_to_all(x, axes, split_axis=0, concat_axis=0, tiled=True)  33.2 us
    all_to_all x1, blocking collectives, exchange(): return lax.all_to_all(x, axes, split_axis=0, concat_axis=0, tiled=True)  24.6 us
    all_to_all x2, waiting for transfers between devices, exchange_lines(): lax.all_to_all(x, PLANE, split_axis=0, concat_axis=0, tiled=True, axis_in...  23.3 us
    all_to_all x3, waiting for transfers between devices, exchange(): return lax.all_to_all(x, axes, split_axis=0, concat_axis=0, tiled=True)  16.5 us
    ppermute x1, waiting for transfers between devices, on_device(): lax.ppermute(jnp.concatenate([stream[0], routes], axis=0), turned, turn)  12.2 us
    all_to_all x2, starting transfers between devices, exchange_lines(): lax.all_to_all(x, PLANE, split_axis=0, concat_axis=0, tiled=True, axis_in...  8.88 us
    pallas_call x1, Pallas kernels, on_device(): pl.pallas_call(expert_kernel, out_shape=shape_of(LINE, 2 * LINE, LINE * G...  7.51 us
  transfers between devices with their start and end apart: 10, of which 6 were waited for; matrix products, arithmetic and copies ran while one was open for 1% of the time, Pallas kernels for 1%

profile of v4, /device:TPU:2, one launch (start us, length us, event | category | flops | bytes accessed | tf_op | source)
XLA Modules:
  0.0 192.9 jit_solution(5836801460007879344)
XLA Ops:
  0.0 0.0 copy-start.3
  0.0 1.5 broadcast_in_dim.12
  1.5 15.2 %all-to-all-start = ((bf16[16,32,256]{2,1,0:T(8,128)(2,1)}), bf16[16,32,256]{2,1,0:T(8,128)(2,1)S(1)}, u32[]{:S(2)}, u32[]{:S(2)}) async-start(bf16[16,32,256]{2,1,0:T(8,128)(2,1)} %broadcast_in_dim.12), calls=%async_computation | async-start | bytes 524288 | tf_op jit(solution)/shard_map/all_to_all | solution.py:46
  16.7 0.8 copy.13
  17.4 0.8 copy.14
  18.2 0.1 copy.17
  18.3 0.8 select_maximum_fusion
  19.0 3.8 %collective-permute-start = (f32[40,256]{1,0:T(8,128)S(1)}, f32[40,256]{1,0:T(8,128)S(1)}, u32[]{:S(2)}, u32[]{:S(2)}) collective-permute-start(f32[40,256]{1,0:T(8,128)S(1)} %select_maximum_fusion), channel_id=1, source_target_pairs={{0,0},{1,16},{2,32},{3,48},{4,64},{5,80},{6,96},{7,112},{8,128},{9... | collective-permute-start | bytes 122888 | tf_op jit(solution)/shard_map/ppermute | solution.py:227
  22.8 12.2 %collective-permute-done.turned_ref = f32[40,256]{1,0:T(8,128)S(1)} collective-permute-done((f32[40,256]{1,0:T(8,128)S(1)}, f32[40,256]{1,0:T(8,128)S(1)}, u32[]{:S(2)}, u32[]{:S(2)}) %collective-permute-start) | collective-permute-done | bytes 40992 | tf_op jit(solution)/shard_map/ppermute | solution.py:227
  35.1 0.0 all-to-all-done
  35.1 0.0 copy-start.1
  35.1 0.9 copy-done.1
  36.0 0.9 shard_map.118
  36.9 11.3 %all-to-all-start.1 = ((bf16[16,32,256]{2,1,0:T(8,128)(2,1)}), bf16[16,32,256]{2,1,0:T(8,128)(2,1)S(1)}, u32[]{:S(2)}, u32[]{:S(2)}) async-start(bf16[16,32,256]{2,1,0:T(8,128)(2,1)} %bitcast.7), calls=%async_computation.1 | async-start | bytes 524288 | tf_op jit(solution)/shard_map/all_to_all | solution.py:46
  48.2 1.9 collective-permute-start.1
  50.2 2.4 %collective-permute-start.2 = (bf16[192,4096]{1,0:T(8,128)(2,1)}, bf16[192,4096]{1,0:T(8,128)(2,1)}, u32[]{:S(2)}, u32[]{:S(2)}) collective-permute-start(bf16[192,4096]{1,0:T(8,128)(2,1)} %bitcast.61), channel_id=1, source_target_pairs={{0,256},{256,0},{1,257},{257,1},{2,258},{258,2},{3,259},{259,3},{4... | collective-permute-start | bytes 4718600 | tf_op jit(solution)/shard_map/ppermute | solution.py:232
  52.6 0.0 copy-start.2
  52.6 2.1 %collective-permute-start.3 = (bf16[192,4096]{1,0:T(8,128)(2,1)}, bf16[192,4096]{1,0:T(8,128)(2,1)}, u32[]{:S(2)}, u32[]{:S(2)}) collective-permute-start(bf16[192,4096]{1,0:T(8,128)(2,1)} %bitcast.63), channel_id=1, source_target_pairs={{0,256},{256,0},{1,257},{257,1},{2,258},{258,2},{3,259},{259,3},{4... | collective-permute-start | bytes 4718600 | tf_op jit(solution)/shard_map/ppermute | solution.py:232
  54.6 0.9 all-to-all-done.1.parts_ref
  55.6 0.3 shard_map.119
  55.8 24.6 %all_to_all.40.rows_ref = bf16[16,24,256]{2,1,0:T(8,128)(2,1)S(1)} all-to-all(bf16[16,24,256]{2,1,0:T(8,128)(2,1)S(1)} %bitcast.56), channel_id=1, replica_groups=mesh['tok'=2,'head_0'=4,'head_1'=4,'exp'=16] {'exp'}, dimensions={0} | all-to-all | bytes 393216 | tf_op jit(solution)/shard_map/all_to_all | solution.py:46
  80.4 0.0 copy-done.3
  80.5 1.1 shard_map.120
  81.5 4.2 %all-to-all-start.3 = ((bf16[4,24,4096]{2,1,0:T(8,128)(2,1)}), bf16[4,24,4096]{2,1,0:T(8,128)(2,1)S(1)}, u32[]{:S(2)}, u32[]{:S(2)}) async-start(bf16[4,24,4096]{2,1,0:T(8,128)(2,1)} %shard_map.120), calls=%async_computation.3 | async-start | bytes 1572864 | tf_op jit(solution)/shard_map/all_to_all | solution.py:208
  85.7 0.0 collective-permute-done.1.refs_1_
  85.7 0.0 collective-permute-done.2.refs_3_
  85.7 0.0 collective-permute-done.3.refs_5_
  85.8 8.0 %all-to-all-done.3 = bf16[4,24,4096]{2,1,0:T(8,128)(2,1)S(1)} async-done(((bf16[4,24,4096]{2,1,0:T(8,128)(2,1)}), bf16[4,24,4096]{2,1,0:T(8,128)(2,1)S(1)}, u32[]{:S(2)}, u32[]{:S(2)}) %all-to-all-start.3) | async-done | bytes 786464 | tf_op jit(solution)/shard_map/all_to_all | solution.py:208
  93.8 0.0 copy-done.2
  93.8 2.1 %shard_map.121 = bf16[4,96,4096]{2,1,0:T(8,128)(2,1)} custom-call(s32[1]{0:T(128)} %bitcast.core_ref, bf16[96,4096]{1,0:T(8,128)(2,1)S(1)} %bitcast.52, bf16[2,96,96]{2,1,0:T(8,128)(2,1)S(1)} %copy-done.2), custom_call_target="tpu_custom_call" | custom-call | tf_op jit(solution)/shard_map/pallas_call | solution.py:253
  95.8 0.0 copy-done.4
  95.8 4.7 %all-to-all-start.4 = ((bf16[4,96,4096]{2,1,0:T(8,128)(2,1)}), bf16[4,96,4096]{2,1,0:T(8,128)(2,1)}, u32[]{:S(2)}, u32[]{:S(2)}) async-start(bf16[4,96,4096]{2,1,0:T(8,128)(2,1)} %shard_map.121), calls=%async_computation.4 | async-start | bytes 6291456 | tf_op jit(solution)/shard_map/all_to_all | solution.py:208
  100.5 4.8 %collective-permute-start.4 = (f32[32,256]{1,0:T(8,128)S(1)}, f32[32,256]{1,0:T(8,128)S(1)}, u32[]{:S(2)}, u32[]{:S(2)}) collective-permute-start(f32[32,256]{1,0:T(8,128)S(1)} %get-tuple-element.19), channel_id=1, source_target_pairs={{0,0},{1,16},{2,32},{3,48},{4,64},{5,80},{6,96},{7,112},{8,128},{9... | collective-permute-start | bytes 98312 | tf_op jit(solution)/shard_map/ppermute | solution.py:243
  105.3 2.1 %collective-permute-done.4.resid_ref = f32[32,256]{1,0:T(8,128)S(1)} collective-permute-done((f32[32,256]{1,0:T(8,128)S(1)}, f32[32,256]{1,0:T(8,128)S(1)}, u32[]{:S(2)}, u32[]{:S(2)}) %collective-permute-start.4) | collective-permute-done | bytes 32800 | tf_op jit(solution)/shard_map/ppermute | solution.py:243
  107.4 15.3 %all-to-all-done.4.rows_ref = bf16[4,96,4096]{2,1,0:T(8,128)(2,1)} async-done(((bf16[4,96,4096]{2,1,0:T(8,128)(2,1)}), bf16[4,96,4096]{2,1,0:T(8,128)(2,1)}, u32[]{:S(2)}, u32[]{:S(2)}) %all-to-all-start.4) | async-done | bytes 3145760 | tf_op jit(solution)/shard_map/all_to_all | solution.py:208
  122.7 7.5 %shard_map.122 = bf16[4,8,192,256]{3,2,1,0:T(8,128)(2,1)} custom-call(s32[1]{0:T(128)} %bitcast.core_ref, bf16[4,96,4096]{2,1,0:T(8,128)(2,1)} %all-to-all-done.4.rows_ref, bf16[192,4096]{1,0:T(8,128)(2,1)} %bitcast.60, bf16[192,4096]{1,0:T(8,128)(2,1)} %copy-done.4, bf16[192,4096]{1,0:T(8,128)(2,1)} %bitcast.62, ...), custom_call_target="tpu_custom_call" | custom-call | tf_op jit(solution)/shard_map/pallas_call | solution.py:266
  130.2 25.8 %all_to_all.41.parts_ref = bf16[4,8,192,256]{3,2,1,0:T(8,128)(2,1)S(1)} all-to-all(bf16[4,8,192,256]{3,2,1,0:T(8,128)(2,1)} %shard_map.122), channel_id=1, replica_groups={{0,16,32,48},{64,80,96,112},{128,144,160,176},{192,208,224,240},{256,32..., dimensions={0} | all-to-all | bytes 6291456 | tf_op jit(solution)/shard_map/all_to_all | solution.py:208
  156.0 0.4 shard_map.123
  156.4 0.0 copy-start
  156.4 0.0 copy-start.5
  156.4 12.1 %all_to_all.42.parts_ref = bf16[4,384,256]{2,1,0:T(8,128)(2,1)S(1)} all-to-all(bf16[4,384,256]{2,1,0:T(8,128)(2,1)S(1)} %bitcast.53), channel_id=1, replica_groups={{0,64,128,192},{16,80,144,208},{32,96,160,224},{48,112,176,240},{256,27..., dimensions={0} | all-to-all | bytes 1572864 | tf_op jit(solution)/shard_map/all_to_all | solution.py:208
  168.5 0.0 copy-done
  168.5 1.0 shard_map.124
  169.5 6.7 %all-to-all-start.7 = ((bf16[16,24,256]{2,1,0:T(8,128)(2,1)}), bf16[16,24,256]{2,1,0:T(8,128)(2,1)S(1)}, u32[]{:S(2)}, u32[]{:S(2)}) async-start(bf16[16,24,256]{2,1,0:T(8,128)(2,1)} %bitcast.15), calls=%async_computation.7 | async-start | bytes 393216 | tf_op jit(solution)/shard_map/all_to_all | solution.py:46
  176.3 0.0 copy-done.5
  176.3 0.1 copy.16
  176.4 15.6 %all-to-all-done.7 = bf16[16,24,256]{2,1,0:T(8,128)(2,1)S(1)} async-done(((bf16[16,24,256]{2,1,0:T(8,128)(2,1)}), bf16[16,24,256]{2,1,0:T(8,128)(2,1)S(1)}, u32[]{:S(2)}, u32[]{:S(2)}) %all-to-all-start.7) | async-done | bytes 196640 | tf_op jit(solution)/shard_map/all_to_all | solution.py:46
  192.0 0.9 shard_map.125
  (2 shorter events, 0.0 us)
Async XLA Ops:
  0.0 80.5 %copy-start.3 = (f32[4096]{0:T(1024)S(1)}, f32[4096]{0:T(1024)}, u32[]{:S(2)}) copy-start(f32[4096]{0:T(1024)} %param.15) | copy-start | bytes 49156
  1.5 33.6 %all-to-all-start = ((bf16[16,32,256]{2,1,0:T(8,128)(2,1)}), bf16[16,32,256]{2,1,0:T(8,128)(2,1)S(1)}, u32[]{:S(2)}, u32[]{:S(2)}) async-start(bf16[16,32,256]{2,1,0:T(8,128)(2,1)} %broadcast_in_dim.12), calls=%async_computation | async-start | bytes 524288 | tf_op jit(solution)/shard_map/all_to_all | solution.py:46
  19.0 16.0 %collective-permute-start = (f32[40,256]{1,0:T(8,128)S(1)}, f32[40,256]{1,0:T(8,128)S(1)}, u32[]{:S(2)}, u32[]{:S(2)}) collective-permute-start(f32[40,256]{1,0:T(8,128)S(1)} %select_maximum_fusion), channel_id=1, source_target_pairs={{0,0},{1,16},{2,32},{3,48},{4,64},{5,80},{6,96},{7,112},{8,128},{9... | collective-permute-start | bytes 122888 | tf_op jit(solution)/shard_map/ppermute | solution.py:227
  35.1 0.9 copy-start.1
  36.9 18.6 %all-to-all-start.1 = ((bf16[16,32,256]{2,1,0:T(8,128)(2,1)}), bf16[16,32,256]{2,1,0:T(8,128)(2,1)S(1)}, u32[]{:S(2)}, u32[]{:S(2)}) async-start(bf16[16,32,256]{2,1,0:T(8,128)(2,1)} %bitcast.7), calls=%async_computation.1 | async-start | bytes 524288 | tf_op jit(solution)/shard_map/all_to_all | solution.py:46
  48.2 37.5 %collective-permute-start.1 = (bf16[192,4096]{1,0:T(8,128)(2,1)}, bf16[192,4096]{1,0:T(8,128)(2,1)S(1)}, u32[]{:S(2)}, u32[]{:S(2)}) collective-permute-start(bf16[192,4096]{1,0:T(8,128)(2,1)} %bitcast.59), channel_id=1, source_target_pairs={{0,256},{256,0},{1,257},{257,1},{2,258},{258,2},{3,259},{259,3},{4... | collective-permute-start | bytes 4718600 | tf_op jit(solution)/shard_map/ppermute | solution.py:232
  50.2 35.6 %collective-permute-start.2 = (bf16[192,4096]{1,0:T(8,128)(2,1)}, bf16[192,4096]{1,0:T(8,128)(2,1)}, u32[]{:S(2)}, u32[]{:S(2)}) collective-permute-start(bf16[192,4096]{1,0:T(8,128)(2,1)} %bitcast.61), channel_id=1, source_target_pairs={{0,256},{256,0},{1,257},{257,1},{2,258},{258,2},{3,259},{259,3},{4... | collective-permute-start | bytes 4718600 | tf_op jit(solution)/shard_map/ppermute | solution.py:232
  52.6 41.2 %copy-start.2 = (bf16[2,96,96]{2,1,0:T(8,128)(2,1)S(1)}, bf16[2,96,96]{2,1,0:T(8,128)(2,1)}, u32[]{:S(2)}) copy-start(bf16[2,96,96]{2,1,0:T(8,128)(2,1)} %constant.37.clone.order_ref) | copy-start | bytes 110596
  52.6 33.2 %collective-permute-start.3 = (bf16[192,4096]{1,0:T(8,128)(2,1)}, bf16[192,4096]{1,0:T(8,128)(2,1)}, u32[]{:S(2)}, u32[]{:S(2)}) collective-permute-start(bf16[192,4096]{1,0:T(8,128)(2,1)} %bitcast.63), channel_id=1, source_target_pairs={{0,256},{256,0},{1,257},{257,1},{2,258},{258,2},{3,259},{259,3},{4... | collective-permute-start | bytes 4718600 | tf_op jit(solution)/shard_map/ppermute | solution.py:232
  81.5 12.3 %all-to-all-start.3 = ((bf16[4,24,4096]{2,1,0:T(8,128)(2,1)}), bf16[4,24,4096]{2,1,0:T(8,128)(2,1)S(1)}, u32[]{:S(2)}, u32[]{:S(2)}) async-start(bf16[4,24,4096]{2,1,0:T(8,128)(2,1)} %shard_map.120), calls=%async_computation.3 | async-start | bytes 1572864 | tf_op jit(solution)/shard_map/all_to_all | solution.py:208
  85.7 10.1 %copy-start.4 = (bf16[192,4096]{1,0:T(8,128)(2,1)}, bf16[192,4096]{1,0:T(8,128)(2,1)S(1)}, u32[]{:S(2)}) copy-start(bf16[192,4096]{1,0:T(8,128)(2,1)S(1)} %collective-permute-done.1.refs_1_) | copy-start | bytes 4718596
  95.8 26.9 %all-to-all-start.4 = ((bf16[4,96,4096]{2,1,0:T(8,128)(2,1)}), bf16[4,96,4096]{2,1,0:T(8,128)(2,1)}, u32[]{:S(2)}, u32[]{:S(2)}) async-start(bf16[4,96,4096]{2,1,0:T(8,128)(2,1)} %shard_map.121), calls=%async_computation.4 | async-start | bytes 6291456 | tf_op jit(solution)/shard_map/all_to_all | solution.py:208
  100.5 6.9 %collective-permute-start.4 = (f32[32,256]{1,0:T(8,128)S(1)}, f32[32,256]{1,0:T(8,128)S(1)}, u32[]{:S(2)}, u32[]{:S(2)}) collective-permute-start(f32[32,256]{1,0:T(8,128)S(1)} %get-tuple-element.19), channel_id=1, source_target_pairs={{0,0},{1,16},{2,32},{3,48},{4,64},{5,80},{6,96},{7,112},{8,128},{9... | collective-permute-start | bytes 98312 | tf_op jit(solution)/shard_map/ppermute | solution.py:243
  156.4 12.1 %copy-start = (bf16[2,384,384]{2,1,0:T(8,128)(2,1)S(1)}, bf16[2,384,384]{2,1,0:T(8,128)(2,1)}, u32[]{:S(2)}) copy-start(bf16[2,384,384]{2,1,0:T(8,128)(2,1)} %constant.38.clone.order_ref) | copy-start | bytes 1769476
  156.4 19.9 %copy-start.5 = (f32[1,32,8]{1,2,0:T(8,128)S(1)}, f32[1,32,8]{1,2,0:T(8,128)}, u32[]{:S(2)}) copy-start(f32[1,32,8]{1,2,0:T(8,128)} %param.18) | copy-start | bytes 3076
  169.5 22.5 %all-to-all-start.7 = ((bf16[16,24,256]{2,1,0:T(8,128)(2,1)}), bf16[16,24,256]{2,1,0:T(8,128)(2,1)S(1)}, u32[]{:S(2)}, u32[]{:S(2)}) async-start(bf16[16,24,256]{2,1,0:T(8,128)(2,1)} %bitcast.15), calls=%async_computation.7 | async-start | bytes 393216 | tf_op jit(solution)/shard_map/all_to_all | solution.py:46

commit v5 on v4

--- a/solution.py
+++ b/solution.py
@@ -29,12 +29,14 @@
 
 
 def call(kernel, out_shape, scalars, arrays, mib=12):
+    moved = sum(a.size * a.dtype.itemsize for a in arrays)
     return pl.pallas_call(
         kernel,
         out_shape=out_shape,
         in_specs=[SMEM] * len(scalars) + [VMEM] * len(arrays),
         out_specs=jax.tree.map(lambda _: VMEM, out_shape),
         compiler_params=pltpu.CompilerParams(vmem_limit_bytes=mib << 20),
+        cost_estimate=pl.CostEstimate(flops=1 << 24, bytes_accessed=2 * moved, transcendentals=0),
     )(*scalars, *arrays)
 
 
@@ -97,51 +99,45 @@
         write.wait()
 
 
-def expert_kernel(core_ref, rows_ref, *refs):
-    sources, out_ref, rows_held, both, downs, staged, sems = refs[:6], *refs[6:]
-    started = []
-
-    def start(source, target):
-        copy = pltpu.make_async_copy(source, target, sems.at[len(started)])
-        copy.start()
-        started.append(copy)
-        return copy
-
-    inputs = []
+def hold_kernel(*refs):
+    sources, held, sems = refs[:6], *refs[6:]
+    copies = []
     for number in range(2):
-        copies = []
-        for source in range(LINE):
-            at = pl.ds(number * GROUP, GROUP)
-            to = pl.ds(source * GROUP, GROUP)
-            copies.append(start(rows_ref.at[source, at], rows_held.at[number, to]))
-        copies.append(start(sources[number], both.at[number, pl.ds(0, UNITS)]))
-        copies.append(start(sources[2 + number], both.at[number, pl.ds(UNITS, UNITS)]))
-        inputs.append(copies)
-    lasts = [start(sources[4 + number], downs.at[number]) for number in range(2)]
+        for part in range(3):
+            place = held.at[pl.ds((3 * number + part) * UNITS, UNITS)]
+            sem = sems.at[len(copies)]
+            copies.append(pltpu.make_async_copy(sources[2 * part + number], place, sem))
+            copies[-1].start()
+    for copy in copies:
+        copy.wait()
+
+
+def expert_kernel(core_ref, rows_ref, held_ref, out_ref, held, sems):
+    loads = []
+    for number in range(2):
+        for part, units in ((0, 2 * UNITS), (2 * UNITS, UNITS)):
+            at = pl.ds(3 * number * UNITS + part, units)
+            loads.append(pltpu.make_async_copy(held_ref.at[at], held.at[at], sems.at[len(loads)]))
+            loads[-1].start()
     contract = (((1,), (1,)), ((), ()))
-    hidden = []
+    first = core_ref[0] == 0
     for number in range(2):
-        for copy in inputs[number]:
-            copy.wait()
+        rows = rows_ref[:, number * GROUP : (number + 1) * GROUP, :].reshape(LINE * GROUP, WIDTH)
+        base = 3 * number * UNITS
+        loads[2 * number].wait()
         product = lax.dot_general(
-            rows_held[number], both[number], contract, preferred_element_type=F32
+            rows, held[base : base + 2 * UNITS], contract, preferred_element_type=F32
         ).T
         gate, up = product[:UNITS], product[UNITS:]
-        hidden.append((gate / (1.0 + jnp.exp(-gate)) * up).astype(BF16).T)
-    for copy in lasts:
-        copy.wait()
-    first = core_ref[0] == 0
-    writes = []
-    for peer in range(LINE):
-        for sub in range(LINE):
-            block = jnp.where(first, sub * LINE + peer, peer * LINE + sub)
-            at = pl.ds(pl.multiple_of(block * COLS, COLS), COLS)
-            for number in range(2):
-                value = jnp.dot(hidden[number], downs[number, :, at], preferred_element_type=F32)
-                staged[peer, sub * 2 + number] = value.astype(BF16)
-        writes.append(start(staged.at[peer], out_ref.at[peer]))
-    for write in writes:
-        write.wait()
+        hidden = (gate / (1.0 + jnp.exp(-gate)) * up).astype(BF16).T
+        loads[2 * number + 1].wait()
+        down = pl.ds(base + 2 * UNITS, UNITS)
+        for peer in range(LINE):
+            for sub in range(LINE):
+                block = jnp.where(first, sub * LINE + peer, peer * LINE + sub)
+                at = pl.ds(pl.multiple_of(block * COLS, COLS), COLS)
+                value = jnp.dot(hidden, held[down, at], preferred_element_type=F32)
+                out_ref[peer, sub * 2 + number] = value.astype(BF16)
 
 
 def add_kernel(parts_ref, out_ref):
@@ -263,20 +259,24 @@
     )(core, line.reshape(2 * GROUP, WIDTH), forward_order())
     arrived = exchange_lines(forward, second_lines)
     arrived, resid = lax.optimization_barrier((arrived, resid))
+    held = pl.pallas_call(
+        hold_kernel,
+        out_shape=shape_of(6 * UNITS, WIDTH),
+        in_specs=[HBM] * 6,
+        out_specs=HBM,
+        scratch_shapes=[pltpu.SemaphoreType.DMA((6,))],
+        compiler_params=pltpu.CompilerParams(vmem_limit_bytes=60 << 20),
+        cost_estimate=pl.CostEstimate(flops=0, bytes_accessed=18 << 20, transcendentals=0),
+    )(*weights)
     produced = pl.pallas_call(
         expert_kernel,
         out_shape=shape_of(LINE, 2 * LINE, LINE * GROUP, COLS),
-        in_specs=[SMEM] + [HBM] * 7,
-        out_specs=HBM,
-        scratch_shapes=[
-            pltpu.VMEM((2, LINE * GROUP, WIDTH), BF16),
-            pltpu.VMEM((2, 2 * UNITS, WIDTH), BF16),
-            pltpu.VMEM((2, UNITS, WIDTH), BF16),
-            pltpu.VMEM((LINE, 2 * LINE, LINE * GROUP, COLS), BF16),
-            pltpu.SemaphoreType.DMA((6 + 3 * LINE,)),
-        ],
-        compiler_params=pltpu.CompilerParams(vmem_limit_bytes=59 << 20),
-    )(core, arrived, *weights)
+        in_specs=[SMEM, VMEM, HBM],
+        out_specs=VMEM,
+        scratch_shapes=[pltpu.VMEM((6 * UNITS, WIDTH), BF16), pltpu.SemaphoreType.DMA((4,))],
+        compiler_params=pltpu.CompilerParams(vmem_limit_bytes=44 << 20),
+        cost_estimate=pl.CostEstimate(flops=1 << 31, bytes_accessed=16 << 20, transcendentals=0),
+    )(core, arrived, held)
     summed = call(
         add_kernel,
         shape_of(2 * LINE, LINE * GROUP, COLS),

time: 194 us -> 466 us (2.40)
  the two profiles are of different devices: /device:TPU:2 before, /device:TPU:32 now
where the time goes in v5:
time: 466 us
  Pallas kernels  300 us (64%)
  blocking collectives  67.9 us (15%)
  starting transfers between devices  55.4 us (12%)
  waiting for transfers between devices  37.2 us (8%)
    pallas_call x1, Pallas kernels, on_device(): pl.pallas_call(hold_kernel, out_shape=shape_of(6 * UNITS, WIDTH), in_spec...  287 us
    all_to_all x2, blocking collectives, exchange_lines(): lax.all_to_all(x, PLANE, split_axis=0, concat_axis=0, tiled=True, axis_in...  42.6 us
    all_to_all x3, starting transfers between devices, exchange(): return lax.all_to_all(x, axes, split_axis=0, concat_axis=0, tiled=True)  36.4 us
    all_to_all x1, blocking collectives, exchange(): return lax.all_to_all(x, axes, split_axis=0, concat_axis=0, tiled=True)  25.3 us
    all_to_all x3, waiting for transfers between devices, exchange(): return lax.all_to_all(x, axes, split_axis=0, concat_axis=0, tiled=True)  18 us
    ppermute x1, waiting for transfers between devices, on_device(): lax.ppermute(jnp.concatenate([stream[0], routes], axis=0), turned, turn)  9.76 us
    all_to_all x2, waiting for transfers between devices, exchange_lines(): lax.all_to_all(x, PLANE, split_axis=0, concat_axis=0, tiled=True, axis_in...  9.41 us
  transfers between devices with their start and end apart: 10, of which 5 were waited for; matrix products, arithmetic and copies ran while one was open for 1% of the time, Pallas kernels for 62%

profile of v5, /device:TPU:32, one launch (start us, length us, event | category | flops | bytes accessed | tf_op | source)
XLA Modules:
  0.0 465.5 jit_solution(3069959603119142611)
XLA Ops:
  0.0 1.5 broadcast_in_dim.12
  1.5 15.2 %all-to-all-start = ((bf16[16,32,256]{2,1,0:T(8,128)(2,1)}), bf16[16,32,256]{2,1,0:T(8,128)(2,1)S(1)}, u32[]{:S(2)}, u32[]{:S(2)}) async-start(bf16[16,32,256]{2,1,0:T(8,128)(2,1)} %broadcast_in_dim.12), calls=%async_computation | async-start | bytes 524288 | tf_op jit(solution)/shard_map/all_to_all | solution.py:48
  16.7 0.8 copy.13
  17.4 0.8 copy.14
  18.2 0.1 copy.17
  18.3 0.8 select_maximum_fusion
  19.0 2.9 collective-permute-start
  22.0 9.8 %collective-permute-done.turned_ref = f32[40,256]{1,0:T(8,128)S(1)} collective-permute-done((f32[40,256]{1,0:T(8,128)S(1)}, f32[40,256]{1,0:T(8,128)S(1)}, u32[]{:S(2)}, u32[]{:S(2)}) %collective-permute-start) | collective-permute-done | bytes 40992 | tf_op jit(solution)/shard_map/ppermute | solution.py:223
  31.7 2.6 all-to-all-done
  34.4 0.9 copy-done.1
  35.3 0.9 shard_map.118
  36.2 10.2 %all-to-all-start.1 = ((bf16[16,32,256]{2,1,0:T(8,128)(2,1)}), bf16[16,32,256]{2,1,0:T(8,128)(2,1)S(1)}, u32[]{:S(2)}, u32[]{:S(2)}) async-start(bf16[16,32,256]{2,1,0:T(8,128)(2,1)} %bitcast.7), calls=%async_computation.1 | async-start | bytes 524288 | tf_op jit(solution)/shard_map/all_to_all | solution.py:48
  46.4 1.9 collective-permute-start.1
  48.3 2.4 collective-permute-start.2
  50.7 0.0 copy-start.2
  50.7 2.1 collective-permute-start.3
  52.8 2.4 all-to-all-done.1.parts_ref
  55.2 0.3 shard_map.119
  55.4 25.3 %all_to_all.40.rows_ref = bf16[16,24,256]{2,1,0:T(8,128)(2,1)S(1)} all-to-all(bf16[16,24,256]{2,1,0:T(8,128)(2,1)S(1)} %bitcast.56), channel_id=1, replica_groups=mesh['tok'=2,'head_0'=4,'head_1'=4,'exp'=16] {'exp'}, dimensions={0} | all-to-all | bytes 393216 | tf_op jit(solution)/shard_map/all_to_all | solution.py:48
  80.8 0.0 copy-done.3
  80.8 1.1 shard_map.120
  81.8 3.5 all-to-all-start.3
  85.3 0.0 collective-permute-done.1.refs_1_
  85.4 0.0 copy-start.4
  85.4 0.0 collective-permute-done.2.refs_3_
  85.4 0.0 collective-permute-done.3.refs_5_
  85.4 9.4 %all-to-all-done.3 = bf16[4,24,4096]{2,1,0:T(8,128)(2,1)S(1)} async-done(((bf16[4,24,4096]{2,1,0:T(8,128)(2,1)}), bf16[4,24,4096]{2,1,0:T(8,128)(2,1)S(1)}, u32[]{:S(2)}, u32[]{:S(2)}) %all-to-all-start.3) | async-done | bytes 786464 | tf_op jit(solution)/shard_map/all_to_all | solution.py:204
  94.8 0.0 copy-done.2
  94.8 2.1 shard_map.121
  96.9 0.0 copy-done.4
  96.9 4.2 all-to-all-start.4
  101.1 1.9 collective-permute-start.4
  103.0 287.0 %shard_map.122.held_ref = bf16[1152,4096]{1,0:T(8,128)(2,1)} custom-call(bf16[192,4096]{1,0:T(8,128)(2,1)} %bitcast.60, bf16[192,4096]{1,0:T(8,128)(2,1)} %copy-done.4, bf16[192,4096]{1,0:T(8,128)(2,1)} %bitcast.62, bf16[192,4096]{1,0:T(8,128)(2,1)} %collective-permute-done.2.refs_3_, bf16[192,4096]{1,0:T(8,128)(2,1)} %bitcast.64, ...), custom_call_target="tpu_custom_call" | custom-call | bytes 18874368 | tf_op jit(solution)/shard_map/pallas_call | solution.py:262
  390.0 0.0 collective-permute-done.4.resid_ref
  390.1 0.0 all-to-all-done.4.rows_ref
  390.1 6.4 %shard_map.123 = bf16[4,8,192,256]{3,2,1,0:T(8,128)(2,1)S(1)} custom-call(s32[1]{0:T(128)} %bitcast.core_ref, bf16[4,96,4096]{2,1,0:T(8,128)(2,1)S(1)} %all-to-all-done.4.rows_ref, bf16[1152,4096]{1,0:T(8,128)(2,1)} %shard_map.122.held_ref), custom_call_target="tpu_custom_call" | custom-call | flops 2147483648 | bytes 16777216 | tf_op jit(solution)/shard_map/pallas_call | solution.py:271
  396.4 27.4 %all_to_all.41.parts_ref = bf16[4,8,192,256]{3,2,1,0:T(8,128)(2,1)S(1)} all-to-all(bf16[4,8,192,256]{3,2,1,0:T(8,128)(2,1)S(1)} %shard_map.123), channel_id=1, replica_groups={{0,16,32,48},{64,80,96,112},{128,144,160,176},{192,208,224,240},{256,32..., dimensions={0} | all-to-all | bytes 6291456 | tf_op jit(solution)/shard_map/all_to_all | solution.py:204
  423.9 0.4 shard_map.124
  424.2 0.0 copy-start
  424.3 0.0 copy-start.5
  424.3 15.2 %all_to_all.42.parts_ref = bf16[4,384,256]{2,1,0:T(8,128)(2,1)S(1)} all-to-all(bf16[4,384,256]{2,1,0:T(8,128)(2,1)S(1)} %bitcast.53), channel_id=1, replica_groups={{0,64,128,192},{16,80,144,208},{32,96,160,224},{48,112,176,240},{256,27..., dimensions={0} | all-to-all | bytes 1572864 | tf_op jit(solution)/shard_map/all_to_all | solution.py:204
  439.5 0.0 copy-done
  439.5 1.0 shard_map.125
  440.5 11.1 %all-to-all-start.7 = ((bf16[16,24,256]{2,1,0:T(8,128)(2,1)}), bf16[16,24,256]{2,1,0:T(8,128)(2,1)S(1)}, u32[]{:S(2)}, u32[]{:S(2)}) async-start(bf16[16,24,256]{2,1,0:T(8,128)(2,1)} %bitcast.15), calls=%async_computation.7 | async-start | bytes 393216 | tf_op jit(solution)/shard_map/all_to_all | solution.py:48
  451.5 0.0 copy-done.5
  451.5 0.1 copy.16
  451.6 13.0 %all-to-all-done.7 = bf16[16,24,256]{2,1,0:T(8,128)(2,1)S(1)} async-done(((bf16[16,24,256]{2,1,0:T(8,128)(2,1)}), bf16[16,24,256]{2,1,0:T(8,128)(2,1)S(1)}, u32[]{:S(2)}, u32[]{:S(2)}) %all-to-all-start.7) | async-done | bytes 196640 | tf_op jit(solution)/shard_map/all_to_all | solution.py:48
  464.6 0.9 shard_map.126
  (3 shorter events, 0.0 us)
Async XLA Ops:
  0.0 80.8 %copy-start.3 = (f32[4096]{0:T(1024)S(1)}, f32[4096]{0:T(1024)}, u32[]{:S(2)}) copy-start(f32[4096]{0:T(1024)} %param.15) | copy-start | bytes 49156
  1.5 32.9 %all-to-all-start = ((bf16[16,32,256]{2,1,0:T(8,128)(2,1)}), bf16[16,32,256]{2,1,0:T(8,128)(2,1)S(1)}, u32[]{:S(2)}, u32[]{:S(2)}) async-start(bf16[16,32,256]{2,1,0:T(8,128)(2,1)} %broadcast_in_dim.12), calls=%async_computation | async-start | bytes 524288 | tf_op jit(solution)/shard_map/all_to_all | solution.py:48
  19.0 12.7 %collective-permute-start = (f32[40,256]{1,0:T(8,128)S(1)}, f32[40,256]{1,0:T(8,128)S(1)}, u32[]{:S(2)}, u32[]{:S(2)}) collective-permute-start(f32[40,256]{1,0:T(8,128)S(1)} %select_maximum_fusion), channel_id=1, source_target_pairs={{0,0},{1,16},{2,32},{3,48},{4,64},{5,80},{6,96},{7,112},{8,128},{9... | collective-permute-start | bytes 122888 | tf_op jit(solution)/shard_map/ppermute | solution.py:223
  34.4 0.9 copy-start.1
  36.2 19.0 %all-to-all-start.1 = ((bf16[16,32,256]{2,1,0:T(8,128)(2,1)}), bf16[16,32,256]{2,1,0:T(8,128)(2,1)S(1)}, u32[]{:S(2)}, u32[]{:S(2)}) async-start(bf16[16,32,256]{2,1,0:T(8,128)(2,1)} %bitcast.7), calls=%async_computation.1 | async-start | bytes 524288 | tf_op jit(solution)/shard_map/all_to_all | solution.py:48
  46.4 39.0 %collective-permute-start.1 = (bf16[192,4096]{1,0:T(8,128)(2,1)}, bf16[192,4096]{1,0:T(8,128)(2,1)S(1)}, u32[]{:S(2)}, u32[]{:S(2)}) collective-permute-start(bf16[192,4096]{1,0:T(8,128)(2,1)} %bitcast.59), channel_id=1, source_target_pairs={{0,256},{256,0},{1,257},{257,1},{2,258},{258,2},{3,259},{259,3},{4... | collective-permute-start | bytes 4718600 | tf_op jit(solution)/shard_map/ppermute | solution.py:228
  48.3 37.1 %collective-permute-start.2 = (bf16[192,4096]{1,0:T(8,128)(2,1)}, bf16[192,4096]{1,0:T(8,128)(2,1)}, u32[]{:S(2)}, u32[]{:S(2)}) collective-permute-start(bf16[192,4096]{1,0:T(8,128)(2,1)} %bitcast.61), channel_id=1, source_target_pairs={{0,256},{256,0},{1,257},{257,1},{2,258},{258,2},{3,259},{259,3},{4... | collective-permute-start | bytes 4718600 | tf_op jit(solution)/shard_map/ppermute | solution.py:228
  50.7 44.1 %copy-start.2 = (bf16[2,96,96]{2,1,0:T(8,128)(2,1)S(1)}, bf16[2,96,96]{2,1,0:T(8,128)(2,1)}, u32[]{:S(2)}) copy-start(bf16[2,96,96]{2,1,0:T(8,128)(2,1)} %constant.37.clone.order_ref) | copy-start | bytes 110596
  50.7 34.6 %collective-permute-start.3 = (bf16[192,4096]{1,0:T(8,128)(2,1)}, bf16[192,4096]{1,0:T(8,128)(2,1)}, u32[]{:S(2)}, u32[]{:S(2)}) collective-permute-start(bf16[192,4096]{1,0:T(8,128)(2,1)} %bitcast.63), channel_id=1, source_target_pairs={{0,256},{256,0},{1,257},{257,1},{2,258},{258,2},{3,259},{259,3},{4... | collective-permute-start | bytes 4718600 | tf_op jit(solution)/shard_map/ppermute | solution.py:228
  81.8 13.0 %all-to-all-start.3 = ((bf16[4,24,4096]{2,1,0:T(8,128)(2,1)}), bf16[4,24,4096]{2,1,0:T(8,128)(2,1)S(1)}, u32[]{:S(2)}, u32[]{:S(2)}) async-start(bf16[4,24,4096]{2,1,0:T(8,128)(2,1)} %shard_map.120), calls=%async_computation.3 | async-start | bytes 1572864 | tf_op jit(solution)/shard_map/all_to_all | solution.py:204
  85.4 11.5 %copy-start.4 = (bf16[192,4096]{1,0:T(8,128)(2,1)}, bf16[192,4096]{1,0:T(8,128)(2,1)S(1)}, u32[]{:S(2)}) copy-start(bf16[192,4096]{1,0:T(8,128)(2,1)S(1)} %collective-permute-done.1.refs_1_) | copy-start | bytes 4718596
  96.9 293.2 %all-to-all-start.4 = ((bf16[4,96,4096]{2,1,0:T(8,128)(2,1)}), bf16[4,96,4096]{2,1,0:T(8,128)(2,1)S(1)}, u32[]{:S(2)}, u32[]{:S(2)}) async-start(bf16[4,96,4096]{2,1,0:T(8,128)(2,1)} %shard_map.121), calls=%async_computation.4 | async-start | bytes 6291456 | tf_op jit(solution)/shard_map/all_to_all | solution.py:204
  101.1 289.0 %collective-permute-start.4 = (f32[32,256]{1,0:T(8,128)S(1)}, f32[32,256]{1,0:T(8,128)S(1)}, u32[]{:S(2)}, u32[]{:S(2)}) collective-permute-start(f32[32,256]{1,0:T(8,128)S(1)} %get-tuple-element.19), channel_id=1, source_target_pairs={{0,0},{1,16},{2,32},{3,48},{4,64},{5,80},{6,96},{7,112},{8,128},{9... | collective-permute-start | bytes 98312 | tf_op jit(solution)/shard_map/ppermute | solution.py:239
  424.2 15.2 %copy-start = (bf16[2,384,384]{2,1,0:T(8,128)(2,1)S(1)}, bf16[2,384,384]{2,1,0:T(8,128)(2,1)}, u32[]{:S(2)}) copy-start(bf16[2,384,384]{2,1,0:T(8,128)(2,1)} %constant.38.clone.order_ref) | copy-start | bytes 1769476
  424.3 27.3 %copy-start.5 = (f32[1,32,8]{1,2,0:T(8,128)S(1)}, f32[1,32,8]{1,2,0:T(8,128)}, u32[]{:S(2)}) copy-start(f32[1,32,8]{1,2,0:T(8,128)} %param.18) | copy-start | bytes 3076
  440.5 24.2 %all-to-all-start.7 = ((bf16[16,24,256]{2,1,0:T(8,128)(2,1)}), bf16[16,24,256]{2,1,0:T(8,128)(2,1)S(1)}, u32[]{:S(2)}, u32[]{:S(2)}) async-start(bf16[16,24,256]{2,1,0:T(8,128)(2,1)} %bitcast.15), calls=%async_computation.7 | async-start | bytes 393216 | tf_op jit(solution)/shard_map/all_to_all | solution.py:48

commit v6 on v5

--- a/solution.py
+++ b/solution.py
@@ -99,25 +99,29 @@
         write.wait()
 
 
-def hold_kernel(*refs):
-    sources, held, sems = refs[:6], *refs[6:]
-    copies = []
-    for number in range(2):
-        for part in range(3):
-            place = held.at[pl.ds((3 * number + part) * UNITS, UNITS)]
-            sem = sems.at[len(copies)]
-            copies.append(pltpu.make_async_copy(sources[2 * part + number], place, sem))
-            copies[-1].start()
-    for copy in copies:
-        copy.wait()
-
-
-def expert_kernel(core_ref, rows_ref, held_ref, out_ref, held, sems):
+def stack_kernel(*refs):
+    sources, out_ref, held, sems = refs[:3], *refs[3:]
+    loads, writes = [], []
+    for part in range(3):
+        loads.append(pltpu.make_async_copy(sources[part], held.at[part], sems.at[part]))
+        at = pl.ds(part * UNITS, UNITS)
+        writes.append(pltpu.make_async_copy(held.at[part], out_ref.at[at], sems.at[3 + part]))
+    for load in loads:
+        load.start()
+    for load, write in zip(loads, writes):
+        load.wait()
+        write.start()
+    for write in writes:
+        write.wait()
+
+
+def expert_kernel(core_ref, rows_ref, own_ref, other_ref, out_ref, held, sems):
     loads = []
-    for number in range(2):
+    for number, source in enumerate((own_ref, other_ref)):
         for part, units in ((0, 2 * UNITS), (2 * UNITS, UNITS)):
             at = pl.ds(3 * number * UNITS + part, units)
-            loads.append(pltpu.make_async_copy(held_ref.at[at], held.at[at], sems.at[len(loads)]))
+            sem = sems.at[len(loads)]
+            loads.append(pltpu.make_async_copy(source.at[pl.ds(part, units)], held.at[at], sem))
             loads[-1].start()
     contract = (((1,), (1,)), ((), ()))
     first = core_ref[0] == 0
@@ -221,11 +225,18 @@
     target = jnp.where(slots >= 0, ((ids - owner * EXPS) * 2 + owner) * CAP + slots, -1)
     routes = jnp.pad(target.T.astype(F32), ((0, 0), (0, COLS - TOK)))
     stream_turned = lax.ppermute(jnp.concatenate([stream[0], routes], axis=0), turned, turn)
-    got, stream_turned = lax.optimization_barrier((got, stream_turned))
-
-    weights = []
-    for weight in (w_gate[0], w_up[0], w_down[0]):
-        weights += [weight, lax.ppermute(weight, "tok", [(0, 1), (1, 0)])]
+    own = pl.pallas_call(
+        stack_kernel,
+        out_shape=shape_of(3 * UNITS, WIDTH),
+        in_specs=[HBM] * 3,
+        out_specs=HBM,
+        scratch_shapes=[pltpu.VMEM((3, UNITS, WIDTH), BF16), pltpu.SemaphoreType.DMA((6,))],
+        compiler_params=pltpu.CompilerParams(vmem_limit_bytes=60 << 20),
+        cost_estimate=pl.CostEstimate(flops=0, bytes_accessed=9 << 20, transcendentals=0),
+    )(w_gate[0], w_up[0], w_down[0])
+    got, stream_turned, own = lax.optimization_barrier((got, stream_turned, own))
+
+    other = lax.ppermute(own, "tok", [(0, 1), (1, 0)])
     partial = call(
         project_kernel, shape_of(EXPS * TOK, COLS), [], [got.reshape(EXPS * TOK, COLS), out_proj]
     )
@@ -245,7 +256,7 @@
         [rows, norm_gain.reshape(1, WIDTH)],
     )
     line = exchange_lines(normed, first_lines)
-    line, *weights[1::2] = lax.optimization_barrier((line, *weights[1::2]))
+    line, other = lax.optimization_barrier((line, other))
     forward = pl.pallas_call(
         forward_kernel,
         out_shape=shape_of(LINE, 2 * GROUP, WIDTH),
@@ -259,24 +270,15 @@
     )(core, line.reshape(2 * GROUP, WIDTH), forward_order())
     arrived = exchange_lines(forward, second_lines)
     arrived, resid = lax.optimization_barrier((arrived, resid))
-    held = pl.pallas_call(
-        hold_kernel,
-        out_shape=shape_of(6 * UNITS, WIDTH),
-        in_specs=[HBM] * 6,
-        out_specs=HBM,
-        scratch_shapes=[pltpu.SemaphoreType.DMA((6,))],
-        compiler_params=pltpu.CompilerParams(vmem_limit_bytes=60 << 20),
-        cost_estimate=pl.CostEstimate(flops=0, bytes_accessed=18 << 20, transcendentals=0),
-    )(*weights)
     produced = pl.pallas_call(
         expert_kernel,
         out_shape=shape_of(LINE, 2 * LINE, LINE * GROUP, COLS),
-        in_specs=[SMEM, VMEM, HBM],
+        in_specs=[SMEM, VMEM, HBM, HBM],
         out_specs=VMEM,
         scratch_shapes=[pltpu.VMEM((6 * UNITS, WIDTH), BF16), pltpu.SemaphoreType.DMA((4,))],
         compiler_params=pltpu.CompilerParams(vmem_limit_bytes=44 << 20),
         cost_estimate=pl.CostEstimate(flops=1 << 31, bytes_accessed=16 << 20, transcendentals=0),
-    )(core, arrived, held)
+    )(core, arrived, own, other)
     summed = call(
         add_kernel,
         shape_of(2 * LINE, LINE * GROUP, COLS),

time: 466 us -> 190 us (0.41)
  the two profiles are of different devices: /device:TPU:32 before, /device:TPU:8 now
where the time goes in v6:
time: 190 us
  blocking collectives  76.6 us (40%)
  waiting for transfers between devices  48.4 us (25%)
  starting transfers between devices  44.7 us (24%)
  Pallas kernels  15.8 us (8%)
  local copies, waits for them, and re-layouts  3.14 us (2%)
    all_to_all x2, blocking collectives, exchange(): return lax.all_to_all(x, axes, split_axis=0, concat_axis=0, tiled=True)  40 us
    all_to_all x2, blocking collectives, exchange_lines(): lax.all_to_all(x, PLANE, split_axis=0, concat_axis=0, tiled=True, axis_in...  36.6 us
    all_to_all x2, starting transfers between devices, exchange(): return lax.all_to_all(x, axes, split_axis=0, concat_axis=0, tiled=True)  21.4 us
    all_to_all x2, waiting for transfers between devices, exchange_lines(): lax.all_to_all(x, PLANE, split_axis=0, concat_axis=0, tiled=True, axis_in...  19.4 us
    all_to_all x2, waiting for transfers between devices, exchange(): return lax.all_to_all(x, axes, split_axis=0, concat_axis=0, tiled=True)  15.2 us
    all_to_all x2, starting transfers between devices, exchange_lines(): lax.all_to_all(x, PLANE, split_axis=0, concat_axis=0, tiled=True, axis_in...  9.7 us
    ppermute x1, starting transfers between devices, on_device(): lax.ppermute(jnp.concatenate([stream[0], routes], axis=0), turned, turn)  7.61 us
    ppermute x1, waiting for transfers between devices, on_device(): lax.ppermute(jnp.concatenate([stream[0], routes], axis=0), turned, turn)  7.13 us
  transfers between devices with their start and end apart: 7, of which 5 were waited for; matrix products, arithmetic and copies ran while one was open for 1% of the time, Pallas kernels for 3%

profile of v6, /device:TPU:8, one launch (start us, length us, event | category | flops | bytes accessed | tf_op | source)
XLA Modules:
  0.0 189.6 jit_solution(9900868443926368851)
XLA Ops:
  0.0 1.4 broadcast_in_dim.12
  1.4 15.2 %all-to-all-start = ((bf16[16,32,256]{2,1,0:T(8,128)(2,1)}), bf16[16,32,256]{2,1,0:T(8,128)(2,1)S(1)}, u32[]{:S(2)}, u32[]{:S(2)}) async-start(bf16[16,32,256]{2,1,0:T(8,128)(2,1)} %broadcast_in_dim.12), calls=%async_computation | async-start | bytes 524288 | tf_op jit(solution)/shard_map/all_to_all | solution.py:48
  16.6 0.8 copy.13
  17.4 0.8 copy.14
  18.2 0.1 copy.17
  18.3 0.8 select_maximum_fusion
  19.0 7.6 %collective-permute-start = (f32[40,256]{1,0:T(8,128)S(1)}, f32[40,256]{1,0:T(8,128)S(1)}, u32[]{:S(2)}, u32[]{:S(2)}) collective-permute-start(f32[40,256]{1,0:T(8,128)S(1)} %select_maximum_fusion), channel_id=1, source_target_pairs={{0,0},{1,16},{2,32},{3,48},{4,64},{5,80},{6,96},{7,112},{8,128},{9... | collective-permute-start | bytes 122888 | tf_op jit(solution)/shard_map/ppermute | solution.py:227
  26.7 0.0 copy-start.1
  26.7 0.0 copy-start.3
  26.7 3.6 %shard_map.118.own_ref = bf16[576,4096]{1,0:T(8,128)(2,1)} custom-call(bf16[192,4096]{1,0:T(8,128)(2,1)} %bitcast.60, bf16[192,4096]{1,0:T(8,128)(2,1)} %bitcast.61, bf16[192,4096]{1,0:T(8,128)(2,1)} %bitcast.62), custom_call_target="tpu_custom_call" | custom-call | bytes 9437184 | tf_op jit(solution)/shard_map/pallas_call | solution.py:228
  30.3 0.0 copy-start.2
  30.3 7.1 %collective-permute-done.turned_ref = f32[40,256]{1,0:T(8,128)S(1)} collective-permute-done((f32[40,256]{1,0:T(8,128)S(1)}, f32[40,256]{1,0:T(8,128)S(1)}, u32[]{:S(2)}, u32[]{:S(2)}) %collective-permute-start) | collective-permute-done | bytes 40992 | tf_op jit(solution)/shard_map/ppermute | solution.py:227
  37.5 0.0 all-to-all-done
  37.5 1.9 %collective-permute-start.1 = (bf16[576,4096]{1,0:T(8,128)(2,1)}, bf16[576,4096]{1,0:T(8,128)(2,1)}, u32[]{:S(2)}, u32[]{:S(2)}) collective-permute-start(bf16[576,4096]{1,0:T(8,128)(2,1)} %shard_map.118.own_ref), channel_id=1, source_target_pairs={{0,256},{256,0},{1,257},{257,1},{2,258},{258,2},{3,259},{259,3},{4... | collective-permute-start | bytes 14155784 | tf_op jit(solution)/shard_map/ppermute | solution.py:239
  39.4 0.0 copy-done.1
  39.4 0.2 shard_map.119
  39.6 16.0 %all_to_all.40.parts_ref = bf16[16,32,256]{2,1,0:T(8,128)(2,1)S(1)} all-to-all(bf16[16,32,256]{2,1,0:T(8,128)(2,1)S(1)} %bitcast.55), channel_id=1, replica_groups=mesh['tok'=2,'head_0'=4,'head_1'=4,'exp'=16] {'head_0','head_1'}, dimensions={0} | all-to-all | bytes 524288 | tf_op jit(solution)/shard_map/all_to_all | solution.py:48
  55.6 0.3 shard_map.120
  55.9 24.0 %all_to_all.41.rows_ref = bf16[16,24,256]{2,1,0:T(8,128)(2,1)S(1)} all-to-all(bf16[16,24,256]{2,1,0:T(8,128)(2,1)S(1)} %bitcast.57), channel_id=1, replica_groups=mesh['tok'=2,'head_0'=4,'head_1'=4,'exp'=16] {'exp'}, dimensions={0} | all-to-all | bytes 393216 | tf_op jit(solution)/shard_map/all_to_all | solution.py:48
  79.9 0.0 copy-done.3
  79.9 1.1 shard_map.121
  80.9 3.5 %all-to-all-start.3 = ((bf16[4,24,4096]{2,1,0:T(8,128)(2,1)}), bf16[4,24,4096]{2,1,0:T(8,128)(2,1)S(1)}, u32[]{:S(2)}, u32[]{:S(2)}) async-start(bf16[4,24,4096]{2,1,0:T(8,128)(2,1)} %shard_map.121), calls=%async_computation.3 | async-start | bytes 1572864 | tf_op jit(solution)/shard_map/all_to_all | solution.py:208
  84.4 9.4 %all-to-all-done.3 = bf16[4,24,4096]{2,1,0:T(8,128)(2,1)S(1)} async-done(((bf16[4,24,4096]{2,1,0:T(8,128)(2,1)}), bf16[4,24,4096]{2,1,0:T(8,128)(2,1)S(1)}, u32[]{:S(2)}, u32[]{:S(2)}) %all-to-all-start.3) | async-done | bytes 786464 | tf_op jit(solution)/shard_map/all_to_all | solution.py:208
  93.9 0.0 collective-permute-done.1.other_ref
  93.9 0.0 copy-done.2
  93.9 2.0 %shard_map.122 = bf16[4,96,4096]{2,1,0:T(8,128)(2,1)} custom-call(s32[1]{0:T(128)} %bitcast.core_ref, bf16[96,4096]{1,0:T(8,128)(2,1)S(1)} %bitcast.52, bf16[2,96,96]{2,1,0:T(8,128)(2,1)S(1)} %copy-done.2), custom_call_target="tpu_custom_call" | custom-call | tf_op jit(solution)/shard_map/pallas_call | solution.py:260
  95.9 6.2 %all-to-all-start.4 = ((bf16[4,96,4096]{2,1,0:T(8,128)(2,1)}), bf16[4,96,4096]{2,1,0:T(8,128)(2,1)S(1)}, u32[]{:S(2)}, u32[]{:S(2)}) async-start(bf16[4,96,4096]{2,1,0:T(8,128)(2,1)} %shard_map.122), calls=%async_computation.4 | async-start | bytes 6291456 | tf_op jit(solution)/shard_map/all_to_all | solution.py:208
  102.1 4.1 %collective-permute-start.2 = (f32[32,256]{1,0:T(8,128)S(1)}, f32[32,256]{1,0:T(8,128)S(1)}, u32[]{:S(2)}, u32[]{:S(2)}) collective-permute-start(f32[32,256]{1,0:T(8,128)S(1)} %get-tuple-element.19), channel_id=1, source_target_pairs={{0,0},{1,16},{2,32},{3,48},{4,64},{5,80},{6,96},{7,112},{8,128},{9... | collective-permute-start | bytes 98312 | tf_op jit(solution)/shard_map/ppermute | solution.py:250
  106.2 6.6 %collective-permute-done.2.resid_ref = f32[32,256]{1,0:T(8,128)S(1)} collective-permute-done((f32[32,256]{1,0:T(8,128)S(1)}, f32[32,256]{1,0:T(8,128)S(1)}, u32[]{:S(2)}, u32[]{:S(2)}) %collective-permute-start.2) | collective-permute-done | bytes 32800 | tf_op jit(solution)/shard_map/ppermute | solution.py:250
  112.8 10.0 %all-to-all-done.4.rows_ref = bf16[4,96,4096]{2,1,0:T(8,128)(2,1)S(1)} async-done(((bf16[4,96,4096]{2,1,0:T(8,128)(2,1)}), bf16[4,96,4096]{2,1,0:T(8,128)(2,1)S(1)}, u32[]{:S(2)}, u32[]{:S(2)}) %all-to-all-start.4) | async-done | bytes 3145760 | tf_op jit(solution)/shard_map/all_to_all | solution.py:208
  122.8 6.4 %shard_map.123 = bf16[4,8,192,256]{3,2,1,0:T(8,128)(2,1)S(1)} custom-call(s32[1]{0:T(128)} %bitcast.core_ref, bf16[4,96,4096]{2,1,0:T(8,128)(2,1)S(1)} %all-to-all-done.4.rows_ref, bf16[576,4096]{1,0:T(8,128)(2,1)} %shard_map.118.own_ref, bf16[576,4096]{1,0:T(8,128)(2,1)} %collective-permute-done.1.other_ref), custom_call_target="tpu_custom_call" | custom-call | flops 2147483648 | bytes 16777216 | tf_op jit(solution)/shard_map/pallas_call | solution.py:273
  129.2 24.6 %all_to_all.42.parts_ref = bf16[4,8,192,256]{3,2,1,0:T(8,128)(2,1)S(1)} all-to-all(bf16[4,8,192,256]{3,2,1,0:T(8,128)(2,1)S(1)} %shard_map.123), channel_id=1, replica_groups={{0,16,32,48},{64,80,96,112},{128,144,160,176},{192,208,224,240},{256,32..., dimensions={0} | all-to-all | bytes 6291456 | tf_op jit(solution)/shard_map/all_to_all | solution.py:208
  153.8 0.0 copy-start
  153.8 0.0 copy-start.4
  153.8 0.4 shard_map.124
  154.2 12.0 %all_to_all.43.parts_ref = bf16[4,384,256]{2,1,0:T(8,128)(2,1)S(1)} all-to-all(bf16[4,384,256]{2,1,0:T(8,128)(2,1)S(1)} %bitcast.53), channel_id=1, replica_groups={{0,64,128,192},{16,80,144,208},{32,96,160,224},{48,112,176,240},{256,27..., dimensions={0} | all-to-all | bytes 1572864 | tf_op jit(solution)/shard_map/all_to_all | solution.py:208
  166.2 0.0 copy-done
  166.2 1.0 shard_map.125
  167.2 6.2 %all-to-all-start.7 = ((bf16[16,24,256]{2,1,0:T(8,128)(2,1)}), bf16[16,24,256]{2,1,0:T(8,128)(2,1)S(1)}, u32[]{:S(2)}, u32[]{:S(2)}) async-start(bf16[16,24,256]{2,1,0:T(8,128)(2,1)} %bitcast.15), calls=%async_computation.7 | async-start | bytes 393216 | tf_op jit(solution)/shard_map/all_to_all | solution.py:48
  173.4 0.0 copy-done.4
  173.4 0.1 copy.16
  173.4 15.2 %all-to-all-done.7 = bf16[16,24,256]{2,1,0:T(8,128)(2,1)S(1)} async-done(((bf16[16,24,256]{2,1,0:T(8,128)(2,1)}), bf16[16,24,256]{2,1,0:T(8,128)(2,1)S(1)}, u32[]{:S(2)}, u32[]{:S(2)}) %all-to-all-start.7) | async-done | bytes 196640 | tf_op jit(solution)/shard_map/all_to_all | solution.py:48
  188.7 0.9 shard_map.126
  (1 shorter events, 0.0 us)
Async XLA Ops:
  1.4 36.0 %all-to-all-start = ((bf16[16,32,256]{2,1,0:T(8,128)(2,1)}), bf16[16,32,256]{2,1,0:T(8,128)(2,1)S(1)}, u32[]{:S(2)}, u32[]{:S(2)}) async-start(bf16[16,32,256]{2,1,0:T(8,128)(2,1)} %broadcast_in_dim.12), calls=%async_computation | async-start | bytes 524288 | tf_op jit(solution)/shard_map/all_to_all | solution.py:48
  19.0 18.4 %collective-permute-start = (f32[40,256]{1,0:T(8,128)S(1)}, f32[40,256]{1,0:T(8,128)S(1)}, u32[]{:S(2)}, u32[]{:S(2)}) collective-permute-start(f32[40,256]{1,0:T(8,128)S(1)} %select_maximum_fusion), channel_id=1, source_target_pairs={{0,0},{1,16},{2,32},{3,48},{4,64},{5,80},{6,96},{7,112},{8,128},{9... | collective-permute-start | bytes 122888 | tf_op jit(solution)/shard_map/ppermute | solution.py:227
  26.7 12.7 %copy-start.1 = (bf16[256,256]{1,0:T(8,128)(2,1)S(1)}, bf16[256,256]{1,0:T(8,128)(2,1)}, u32[]{:S(2)}) copy-start(bf16[256,256]{1,0:T(8,128)(2,1)} %weight_ref.1) | copy-start | bytes 393220
  26.7 53.2 %copy-start.3 = (f32[4096]{0:T(1024)S(1)}, f32[4096]{0:T(1024)}, u32[]{:S(2)}) copy-start(f32[4096]{0:T(1024)} %param.15) | copy-start | bytes 49156
  30.3 63.6 %copy-start.2 = (bf16[2,96,96]{2,1,0:T(8,128)(2,1)S(1)}, bf16[2,96,96]{2,1,0:T(8,128)(2,1)}, u32[]{:S(2)}) copy-start(bf16[2,96,96]{2,1,0:T(8,128)(2,1)} %constant.37.clone.order_ref) | copy-start | bytes 110596
  37.5 56.4 %collective-permute-start.1 = (bf16[576,4096]{1,0:T(8,128)(2,1)}, bf16[576,4096]{1,0:T(8,128)(2,1)}, u32[]{:S(2)}, u32[]{:S(2)}) collective-permute-start(bf16[576,4096]{1,0:T(8,128)(2,1)} %shard_map.118.own_ref), channel_id=1, source_target_pairs={{0,256},{256,0},{1,257},{257,1},{2,258},{258,2},{3,259},{259,3},{4... | collective-permute-start | bytes 14155784 | tf_op jit(solution)/shard_map/ppermute | solution.py:239
  80.9 13.0 %all-to-all-start.3 = ((bf16[4,24,4096]{2,1,0:T(8,128)(2,1)}), bf16[4,24,4096]{2,1,0:T(8,128)(2,1)S(1)}, u32[]{:S(2)}, u32[]{:S(2)}) async-start(bf16[4,24,4096]{2,1,0:T(8,128)(2,1)} %shard_map.121), calls=%async_computation.3 | async-start | bytes 1572864 | tf_op jit(solution)/shard_map/all_to_all | solution.py:208
  95.9 26.9 %all-to-all-start.4 = ((bf16[4,96,4096]{2,1,0:T(8,128)(2,1)}), bf16[4,96,4096]{2,1,0:T(8,128)(2,1)S(1)}, u32[]{:S(2)}, u32[]{:S(2)}) async-start(bf16[4,96,4096]{2,1,0:T(8,128)(2,1)} %shard_map.122), calls=%async_computation.4 | async-start | bytes 6291456 | tf_op jit(solution)/shard_map/all_to_all | solution.py:208
  102.1 10.7 %collective-permute-start.2 = (f32[32,256]{1,0:T(8,128)S(1)}, f32[32,256]{1,0:T(8,128)S(1)}, u32[]{:S(2)}, u32[]{:S(2)}) collective-permute-start(f32[32,256]{1,0:T(8,128)S(1)} %get-tuple-element.19), channel_id=1, source_target_pairs={{0,0},{1,16},{2,32},{3,48},{4,64},{5,80},{6,96},{7,112},{8,128},{9... | collective-permute-start | bytes 98312 | tf_op jit(solution)/shard_map/ppermute | solution.py:250
  153.8 12.4 %copy-start = (bf16[2,384,384]{2,1,0:T(8,128)(2,1)S(1)}, bf16[2,384,384]{2,1,0:T(8,128)(2,1)}, u32[]{:S(2)}) copy-start(bf16[2,384,384]{2,1,0:T(8,128)(2,1)} %constant.38.clone.order_ref) | copy-start | bytes 1769476
  153.8 19.5 %copy-start.4 = (f32[1,32,8]{1,2,0:T(8,128)S(1)}, f32[1,32,8]{1,2,0:T(8,128)}, u32[]{:S(2)}) copy-start(f32[1,32,8]{1,2,0:T(8,128)} %param.18) | copy-start | bytes 3076
  167.2 21.5 %all-to-all-start.7 = ((bf16[16,24,256]{2,1,0:T(8,128)(2,1)}), bf16[16,24,256]{2,1,0:T(8,128)(2,1)S(1)}, u32[]{:S(2)}, u32[]{:S(2)}) async-start(bf16[16,24,256]{2,1,0:T(8,128)(2,1)} %bitcast.15), calls=%async_computation.7 | async-start | bytes 393216 | tf_op jit(solution)/shard_map/all_to_all | solution.py:48

commit v7 on v6

--- a/solution.py
+++ b/solution.py
@@ -16,6 +16,7 @@
 HEADS = 16
 EXPS = 16
 WIDTH = HEADS * COLS
+HALF = WIDTH // 2
 ROWS = 2 * EXPS * CAP
 HEAD = ("head_0", "head_1")
 PLANE = ("tok", "head_0", "head_1")
@@ -115,32 +116,47 @@
         write.wait()
 
 
-def expert_kernel(core_ref, rows_ref, own_ref, other_ref, out_ref, held, sems):
+def expert_kernel(core_ref, rows_ref, own_ref, other_ref, out_ref, both, downs, sems):
+    started = []
+
+    def start(source, target):
+        copy = pltpu.make_async_copy(source, target, sems.at[len(started)])
+        copy.start()
+        started.append(copy)
+        return copy
+
+    halves = [pl.ds(half * HALF, HALF) for half in range(2)]
     loads = []
     for number, source in enumerate((own_ref, other_ref)):
-        for part, units in ((0, 2 * UNITS), (2 * UNITS, UNITS)):
-            at = pl.ds(3 * number * UNITS + part, units)
-            sem = sems.at[len(loads)]
-            loads.append(pltpu.make_async_copy(source.at[pl.ds(part, units)], held.at[at], sem))
-            loads[-1].start()
+        for at in halves:
+            gate = start(source.at[pl.ds(0, UNITS), at], both.at[number, pl.ds(0, UNITS), at])
+            up = start(source.at[pl.ds(UNITS, UNITS), at], both.at[number, pl.ds(COLS, UNITS), at])
+            loads.append((gate, up))
+        loads.append((start(source.at[pl.ds(2 * UNITS, UNITS)], downs.at[number]),))
+    for number in range(2):
+        both[number, UNITS:COLS, :] = jnp.zeros((COLS - UNITS, WIDTH), BF16)
     contract = (((1,), (1,)), ((), ()))
     first = core_ref[0] == 0
     for number in range(2):
-        rows = rows_ref[:, number * GROUP : (number + 1) * GROUP, :].reshape(LINE * GROUP, WIDTH)
-        base = 3 * number * UNITS
-        loads[2 * number].wait()
-        product = lax.dot_general(
-            rows, held[base : base + 2 * UNITS], contract, preferred_element_type=F32
-        ).T
-        gate, up = product[:UNITS], product[UNITS:]
-        hidden = (gate / (1.0 + jnp.exp(-gate)) * up).astype(BF16).T
-        loads[2 * number + 1].wait()
-        down = pl.ds(base + 2 * UNITS, UNITS)
+        product = jnp.zeros((LINE * GROUP, COLS + UNITS), F32)
+        for half, at in enumerate(halves):
+            for load in loads[3 * number + half]:
+                load.wait()
+            rows = rows_ref[:, number * GROUP : (number + 1) * GROUP, at]
+            product = product + lax.dot_general(
+                rows.reshape(LINE * GROUP, HALF),
+                both[number, :, at],
+                contract,
+                preferred_element_type=F32,
+            )
+        gate, up = product[:, :UNITS], product[:, COLS:]
+        hidden = (gate / (1.0 + jnp.exp(-gate)) * up).astype(BF16)
+        loads[3 * number + 2][0].wait()
         for peer in range(LINE):
             for sub in range(LINE):
                 block = jnp.where(first, sub * LINE + peer, peer * LINE + sub)
                 at = pl.ds(pl.multiple_of(block * COLS, COLS), COLS)
-                value = jnp.dot(hidden, held[down, at], preferred_element_type=F32)
+                value = jnp.dot(hidden, downs[number, :, at], preferred_element_type=F32)
                 out_ref[peer, sub * 2 + number] = value.astype(BF16)
 
 
@@ -275,7 +291,11 @@
         out_shape=shape_of(LINE, 2 * LINE, LINE * GROUP, COLS),
         in_specs=[SMEM, VMEM, HBM, HBM],
         out_specs=VMEM,
-        scratch_shapes=[pltpu.VMEM((6 * UNITS, WIDTH), BF16), pltpu.SemaphoreType.DMA((4,))],
+        scratch_shapes=[
+            pltpu.VMEM((2, COLS + UNITS, WIDTH), BF16),
+            pltpu.VMEM((2, UNITS, WIDTH), BF16),
+            pltpu.SemaphoreType.DMA((10,)),
+        ],
         compiler_params=pltpu.CompilerParams(vmem_limit_bytes=44 << 20),
         cost_estimate=pl.CostEstimate(flops=1 << 31, bytes_accessed=16 << 20, transcendentals=0),
     )(core, arrived, own, other)

time: 190 us -> 190 us (level)
  no operation moved by 1% of the time
where the time goes in v7:
time: 190 us; the launch traced here: 189 us
  blocking collectives  76.6 us (40%)
  waiting for transfers between devices  48.4 us (25%)
  starting transfers between devices  44.7 us (24%)
  Pallas kernels  15.6 us (8%)
  local copies, waits for them, and re-layouts  3.14 us (2%)
    all_to_all x2, blocking collectives, exchange(): return lax.all_to_all(x, axes, split_axis=0, concat_axis=0, tiled=True)  40 us
    all_to_all x2, blocking collectives, exchange_lines(): lax.all_to_all(x, PLANE, split_axis=0, concat_axis=0, tiled=True, axis_in...  36.6 us
    all_to_all x2, starting transfers between devices, exchange(): return lax.all_to_all(x, axes, split_axis=0, concat_axis=0, tiled=True)  21.4 us
    all_to_all x2, waiting for transfers between devices, exchange_lines(): lax.all_to_all(x, PLANE, split_axis=0, concat_axis=0, tiled=True, axis_in...  19.4 us
    all_to_all x2, waiting for transfers between devices, exchange(): return lax.all_to_all(x, axes, split_axis=0, concat_axis=0, tiled=True)  15.2 us
    all_to_all x2, starting transfers between devices, exchange_lines(): lax.all_to_all(x, PLANE, split_axis=0, concat_axis=0, tiled=True, axis_in...  9.7 us
    ppermute x1, starting transfers between devices, on_device(): lax.ppermute(jnp.concatenate([stream[0], routes], axis=0), turned, turn)  7.61 us
    ppermute x1, waiting for transfers between devices, on_device(): lax.ppermute(jnp.concatenate([stream[0], routes], axis=0), turned, turn)  7.13 us
  transfers between devices with their start and end apart: 7, of which 5 were waited for; matrix products, arithmetic and copies ran while one was open for 1% of the time, Pallas kernels for 3%

profile of v7, /device:TPU:8, one launch (start us, length us, event | category | flops | bytes accessed | tf_op | source)
XLA Modules:
  0.0 189.4 jit_solution(18049880075028306040)
XLA Ops:
  0.0 1.4 broadcast_in_dim.12
  1.4 15.2 %all-to-all-start = ((bf16[16,32,256]{2,1,0:T(8,128)(2,1)}), bf16[16,32,256]{2,1,0:T(8,128)(2,1)S(1)}, u32[]{:S(2)}, u32[]{:S(2)}) async-start(bf16[16,32,256]{2,1,0:T(8,128)(2,1)} %broadcast_in_dim.12), calls=%async_computation | async-start | bytes 524288 | tf_op jit(solution)/shard_map/all_to_all | solution.py:49
  16.6 0.8 copy.13
  17.4 0.8 copy.14
  18.2 0.1 copy.17
  18.3 0.8 select_maximum_fusion
  19.0 7.6 %collective-permute-start = (f32[40,256]{1,0:T(8,128)S(1)}, f32[40,256]{1,0:T(8,128)S(1)}, u32[]{:S(2)}, u32[]{:S(2)}) collective-permute-start(f32[40,256]{1,0:T(8,128)S(1)} %select_maximum_fusion), channel_id=1, source_target_pairs={{0,0},{1,16},{2,32},{3,48},{4,64},{5,80},{6,96},{7,112},{8,128},{9... | collective-permute-start | bytes 122888 | tf_op jit(solution)/shard_map/ppermute | solution.py:243
  26.7 0.0 copy-start.1
  26.7 0.0 copy-start.3
  26.7 3.6 %shard_map.118.own_ref = bf16[576,4096]{1,0:T(8,128)(2,1)} custom-call(bf16[192,4096]{1,0:T(8,128)(2,1)} %bitcast.60, bf16[192,4096]{1,0:T(8,128)(2,1)} %bitcast.61, bf16[192,4096]{1,0:T(8,128)(2,1)} %bitcast.62), custom_call_target="tpu_custom_call" | custom-call | bytes 9437184 | tf_op jit(solution)/shard_map/pallas_call | solution.py:244
  30.3 0.0 copy-start.2
  30.3 7.1 %collective-permute-done.turned_ref = f32[40,256]{1,0:T(8,128)S(1)} collective-permute-done((f32[40,256]{1,0:T(8,128)S(1)}, f32[40,256]{1,0:T(8,128)S(1)}, u32[]{:S(2)}, u32[]{:S(2)}) %collective-permute-start) | collective-permute-done | bytes 40992 | tf_op jit(solution)/shard_map/ppermute | solution.py:243
  37.5 0.0 all-to-all-done
  37.5 1.9 %collective-permute-start.1 = (bf16[576,4096]{1,0:T(8,128)(2,1)}, bf16[576,4096]{1,0:T(8,128)(2,1)}, u32[]{:S(2)}, u32[]{:S(2)}) collective-permute-start(bf16[576,4096]{1,0:T(8,128)(2,1)} %shard_map.118.own_ref), channel_id=1, source_target_pairs={{0,256},{256,0},{1,257},{257,1},{2,258},{258,2},{3,259},{259,3},{4... | collective-permute-start | bytes 14155784 | tf_op jit(solution)/shard_map/ppermute | solution.py:255
  39.4 0.0 copy-done.1
  39.4 0.2 shard_map.119
  39.6 16.0 %all_to_all.40.parts_ref = bf16[16,32,256]{2,1,0:T(8,128)(2,1)S(1)} all-to-all(bf16[16,32,256]{2,1,0:T(8,128)(2,1)S(1)} %bitcast.55), channel_id=1, replica_groups=mesh['tok'=2,'head_0'=4,'head_1'=4,'exp'=16] {'head_0','head_1'}, dimensions={0} | all-to-all | bytes 524288 | tf_op jit(solution)/shard_map/all_to_all | solution.py:49
  55.6 0.3 shard_map.120
  55.9 24.0 %all_to_all.41.rows_ref = bf16[16,24,256]{2,1,0:T(8,128)(2,1)S(1)} all-to-all(bf16[16,24,256]{2,1,0:T(8,128)(2,1)S(1)} %bitcast.57), channel_id=1, replica_groups=mesh['tok'=2,'head_0'=4,'head_1'=4,'exp'=16] {'exp'}, dimensions={0} | all-to-all | bytes 393216 | tf_op jit(solution)/shard_map/all_to_all | solution.py:49
  79.9 0.0 copy-done.3
  79.9 1.1 shard_map.121
  80.9 3.5 %all-to-all-start.3 = ((bf16[4,24,4096]{2,1,0:T(8,128)(2,1)}), bf16[4,24,4096]{2,1,0:T(8,128)(2,1)S(1)}, u32[]{:S(2)}, u32[]{:S(2)}) async-start(bf16[4,24,4096]{2,1,0:T(8,128)(2,1)} %shard_map.121), calls=%async_computation.3 | async-start | bytes 1572864 | tf_op jit(solution)/shard_map/all_to_all | solution.py:224
  84.4 9.4 %all-to-all-done.3 = bf16[4,24,4096]{2,1,0:T(8,128)(2,1)S(1)} async-done(((bf16[4,24,4096]{2,1,0:T(8,128)(2,1)}), bf16[4,24,4096]{2,1,0:T(8,128)(2,1)S(1)}, u32[]{:S(2)}, u32[]{:S(2)}) %all-to-all-start.3) | async-done | bytes 786464 | tf_op jit(solution)/shard_map/all_to_all | solution.py:224
  93.9 0.0 collective-permute-done.1.other_ref
  93.9 0.0 copy-done.2
  93.9 2.0 %shard_map.122 = bf16[4,96,4096]{2,1,0:T(8,128)(2,1)} custom-call(s32[1]{0:T(128)} %bitcast.core_ref, bf16[96,4096]{1,0:T(8,128)(2,1)S(1)} %bitcast.52, bf16[2,96,96]{2,1,0:T(8,128)(2,1)S(1)} %copy-done.2), custom_call_target="tpu_custom_call" | custom-call | tf_op jit(solution)/shard_map/pallas_call | solution.py:276
  95.9 6.2 %all-to-all-start.4 = ((bf16[4,96,4096]{2,1,0:T(8,128)(2,1)}), bf16[4,96,4096]{2,1,0:T(8,128)(2,1)S(1)}, u32[]{:S(2)}, u32[]{:S(2)}) async-start(bf16[4,96,4096]{2,1,0:T(8,128)(2,1)} %shard_map.122), calls=%async_computation.4 | async-start | bytes 6291456 | tf_op jit(solution)/shard_map/all_to_all | solution.py:224
  102.1 4.1 %collective-permute-start.2 = (f32[32,256]{1,0:T(8,128)S(1)}, f32[32,256]{1,0:T(8,128)S(1)}, u32[]{:S(2)}, u32[]{:S(2)}) collective-permute-start(f32[32,256]{1,0:T(8,128)S(1)} %get-tuple-element.19), channel_id=1, source_target_pairs={{0,0},{1,16},{2,32},{3,48},{4,64},{5,80},{6,96},{7,112},{8,128},{9... | collective-permute-start | bytes 98312 | tf_op jit(solution)/shard_map/ppermute | solution.py:266
  106.2 6.6 %collective-permute-done.2.resid_ref = f32[32,256]{1,0:T(8,128)S(1)} collective-permute-done((f32[32,256]{1,0:T(8,128)S(1)}, f32[32,256]{1,0:T(8,128)S(1)}, u32[]{:S(2)}, u32[]{:S(2)}) %collective-permute-start.2) | collective-permute-done | bytes 32800 | tf_op jit(solution)/shard_map/ppermute | solution.py:266
  112.8 10.0 %all-to-all-done.4.rows_ref = bf16[4,96,4096]{2,1,0:T(8,128)(2,1)S(1)} async-done(((bf16[4,96,4096]{2,1,0:T(8,128)(2,1)}), bf16[4,96,4096]{2,1,0:T(8,128)(2,1)S(1)}, u32[]{:S(2)}, u32[]{:S(2)}) %all-to-all-start.4) | async-done | bytes 3145760 | tf_op jit(solution)/shard_map/all_to_all | solution.py:224
  122.8 6.2 %shard_map.123 = bf16[4,8,192,256]{3,2,1,0:T(8,128)(2,1)S(1)} custom-call(s32[1]{0:T(128)} %bitcast.core_ref, bf16[4,96,4096]{2,1,0:T(8,128)(2,1)S(1)} %all-to-all-done.4.rows_ref, bf16[576,4096]{1,0:T(8,128)(2,1)} %shard_map.118.own_ref, bf16[576,4096]{1,0:T(8,128)(2,1)} %collective-permute-done.1.other_ref), custom_call_target="tpu_custom_call" | custom-call | flops 2147483648 | bytes 16777216 | tf_op jit(solution)/shard_map/pallas_call | solution.py:289
  129.0 24.6 %all_to_all.42.parts_ref = bf16[4,8,192,256]{3,2,1,0:T(8,128)(2,1)S(1)} all-to-all(bf16[4,8,192,256]{3,2,1,0:T(8,128)(2,1)S(1)} %shard_map.123), channel_id=1, replica_groups={{0,16,32,48},{64,80,96,112},{128,144,160,176},{192,208,224,240},{256,32..., dimensions={0} | all-to-all | bytes 6291456 | tf_op jit(solution)/shard_map/all_to_all | solution.py:224
  153.6 0.0 copy-start
  153.6 0.0 copy-start.4
  153.6 0.4 shard_map.124
  154.0 12.0 %all_to_all.43.parts_ref = bf16[4,384,256]{2,1,0:T(8,128)(2,1)S(1)} all-to-all(bf16[4,384,256]{2,1,0:T(8,128)(2,1)S(1)} %bitcast.53), channel_id=1, replica_groups={{0,64,128,192},{16,80,144,208},{32,96,160,224},{48,112,176,240},{256,27..., dimensions={0} | all-to-all | bytes 1572864 | tf_op jit(solution)/shard_map/all_to_all | solution.py:224
  166.0 0.0 copy-done
  166.0 1.0 shard_map.125
  167.0 6.2 %all-to-all-start.7 = ((bf16[16,24,256]{2,1,0:T(8,128)(2,1)}), bf16[16,24,256]{2,1,0:T(8,128)(2,1)S(1)}, u32[]{:S(2)}, u32[]{:S(2)}) async-start(bf16[16,24,256]{2,1,0:T(8,128)(2,1)} %bitcast.15), calls=%async_computation.7 | async-start | bytes 393216 | tf_op jit(solution)/shard_map/all_to_all | solution.py:49
  173.2 0.0 copy-done.4
  173.2 0.1 copy.16
  173.2 15.2 %all-to-all-done.7 = bf16[16,24,256]{2,1,0:T(8,128)(2,1)S(1)} async-done(((bf16[16,24,256]{2,1,0:T(8,128)(2,1)}), bf16[16,24,256]{2,1,0:T(8,128)(2,1)S(1)}, u32[]{:S(2)}, u32[]{:S(2)}) %all-to-all-start.7) | async-done | bytes 196640 | tf_op jit(solution)/shard_map/all_to_all | solution.py:49
  188.5 0.9 shard_map.126
  (1 shorter events, 0.0 us)
Async XLA Ops:
  1.4 36.0 %all-to-all-start = ((bf16[16,32,256]{2,1,0:T(8,128)(2,1)}), bf16[16,32,256]{2,1,0:T(8,128)(2,1)S(1)}, u32[]{:S(2)}, u32[]{:S(2)}) async-start(bf16[16,32,256]{2,1,0:T(8,128)(2,1)} %broadcast_in_dim.12), calls=%async_computation | async-start | bytes 524288 | tf_op jit(solution)/shard_map/all_to_all | solution.py:49
  19.0 18.4 %collective-permute-start = (f32[40,256]{1,0:T(8,128)S(1)}, f32[40,256]{1,0:T(8,128)S(1)}, u32[]{:S(2)}, u32[]{:S(2)}) collective-permute-start(f32[40,256]{1,0:T(8,128)S(1)} %select_maximum_fusion), channel_id=1, source_target_pairs={{0,0},{1,16},{2,32},{3,48},{4,64},{5,80},{6,96},{7,112},{8,128},{9... | collective-permute-start | bytes 122888 | tf_op jit(solution)/shard_map/ppermute | solution.py:243
  26.7 12.7 %copy-start.1 = (bf16[256,256]{1,0:T(8,128)(2,1)S(1)}, bf16[256,256]{1,0:T(8,128)(2,1)}, u32[]{:S(2)}) copy-start(bf16[256,256]{1,0:T(8,128)(2,1)} %weight_ref.1) | copy-start | bytes 393220
  26.7 53.2 %copy-start.3 = (f32[4096]{0:T(1024)S(1)}, f32[4096]{0:T(1024)}, u32[]{:S(2)}) copy-start(f32[4096]{0:T(1024)} %param.15) | copy-start | bytes 49156
  30.3 63.6 %copy-start.2 = (bf16[2,96,96]{2,1,0:T(8,128)(2,1)S(1)}, bf16[2,96,96]{2,1,0:T(8,128)(2,1)}, u32[]{:S(2)}) copy-start(bf16[2,96,96]{2,1,0:T(8,128)(2,1)} %constant.37.clone.order_ref) | copy-start | bytes 110596
  37.5 56.4 %collective-permute-start.1 = (bf16[576,4096]{1,0:T(8,128)(2,1)}, bf16[576,4096]{1,0:T(8,128)(2,1)}, u32[]{:S(2)}, u32[]{:S(2)}) collective-permute-start(bf16[576,4096]{1,0:T(8,128)(2,1)} %shard_map.118.own_ref), channel_id=1, source_target_pairs={{0,256},{256,0},{1,257},{257,1},{2,258},{258,2},{3,259},{259,3},{4... | collective-permute-start | bytes 14155784 | tf_op jit(solution)/shard_map/ppermute | solution.py:255
  80.9 13.0 %all-to-all-start.3 = ((bf16[4,24,4096]{2,1,0:T(8,128)(2,1)}), bf16[4,24,4096]{2,1,0:T(8,128)(2,1)S(1)}, u32[]{:S(2)}, u32[]{:S(2)}) async-start(bf16[4,24,4096]{2,1,0:T(8,128)(2,1)} %shard_map.121), calls=%async_computation.3 | async-start | bytes 1572864 | tf_op jit(solution)/shard_map/all_to_all | solution.py:224
  95.9 26.9 %all-to-all-start.4 = ((bf16[4,96,4096]{2,1,0:T(8,128)(2,1)}), bf16[4,96,4096]{2,1,0:T(8,128)(2,1)S(1)}, u32[]{:S(2)}, u32[]{:S(2)}) async-start(bf16[4,96,4096]{2,1,0:T(8,128)(2,1)} %shard_map.122), calls=%async_computation.4 | async-start | bytes 6291456 | tf_op jit(solution)/shard_map/all_to_all | solution.py:224
  102.1 10.7 %collective-permute-start.2 = (f32[32,256]{1,0:T(8,128)S(1)}, f32[32,256]{1,0:T(8,128)S(1)}, u32[]{:S(2)}, u32[]{:S(2)}) collective-permute-start(f32[32,256]{1,0:T(8,128)S(1)} %get-tuple-element.19), channel_id=1, source_target_pairs={{0,0},{1,16},{2,32},{3,48},{4,64},{5,80},{6,96},{7,112},{8,128},{9... | collective-permute-start | bytes 98312 | tf_op jit(solution)/shard_map/ppermute | solution.py:266
  153.6 12.4 %copy-start = (bf16[2,384,384]{2,1,0:T(8,128)(2,1)S(1)}, bf16[2,384,384]{2,1,0:T(8,128)(2,1)}, u32[]{:S(2)}) copy-start(bf16[2,384,384]{2,1,0:T(8,128)(2,1)} %constant.38.clone.order_ref) | copy-start | bytes 1769476
  153.6 19.5 %copy-start.4 = (f32[1,32,8]{1,2,0:T(8,128)S(1)}, f32[1,32,8]{1,2,0:T(8,128)}, u32[]{:S(2)}) copy-start(f32[1,32,8]{1,2,0:T(8,128)} %param.18) | copy-start | bytes 3076
  167.0 21.5 %all-to-all-start.7 = ((bf16[16,24,256]{2,1,0:T(8,128)(2,1)}), bf16[16,24,256]{2,1,0:T(8,128)(2,1)S(1)}, u32[]{:S(2)}, u32[]{:S(2)}) async-start(bf16[16,24,256]{2,1,0:T(8,128)(2,1)} %bitcast.15), calls=%async_computation.7 | async-start | bytes 393216 | tf_op jit(solution)/shard_map/all_to_all | solution.py:49

commit v8 on v7

--- a/solution.py
+++ b/solution.py
@@ -152,12 +152,16 @@
         gate, up = product[:, :UNITS], product[:, COLS:]
         hidden = (gate / (1.0 + jnp.exp(-gate)) * up).astype(BF16)
         loads[3 * number + 2][0].wait()
-        for peer in range(LINE):
-            for sub in range(LINE):
-                block = jnp.where(first, sub * LINE + peer, peer * LINE + sub)
-                at = pl.ds(pl.multiple_of(block * COLS, COLS), COLS)
-                value = jnp.dot(hidden, downs[number, :, at], preferred_element_type=F32)
-                out_ref[peer, sub * 2 + number] = value.astype(BF16)
+        for block in range(HEADS):
+            outer, inner = block // LINE, block % LINE
+            peer = jnp.where(first, inner, outer)
+            sub = jnp.where(first, outer, inner)
+            value = jnp.dot(
+                hidden,
+                downs[number, :, block * COLS : (block + 1) * COLS],
+                preferred_element_type=F32,
+            )
+            out_ref[peer, sub * 2 + number] = value.astype(BF16)
 
 
 def add_kernel(parts_ref, out_ref):

time: 190 us -> 190 us (level)
  the two profiles are of different devices: /device:TPU:8 before, /device:TPU:32 now
where the time goes in v8:
time: 190 us; the launch traced here: 189 us
  blocking collectives  81 us (43%)
  waiting for transfers between devices  51.3 us (27%)
  starting transfers between devices  37.1 us (20%)
  Pallas kernels  15.6 us (8%)
  local copies, waits for them, and re-layouts  3.14 us (2%)
    all_to_all x2, blocking collectives, exchange(): return lax.all_to_all(x, axes, split_axis=0, concat_axis=0, tiled=True)  44.3 us
    all_to_all x2, blocking collectives, exchange_lines(): lax.all_to_all(x, PLANE, split_axis=0, concat_axis=0, tiled=True, axis_in...  36.7 us
    all_to_all x2, waiting for transfers between devices, exchange_lines(): lax.all_to_all(x, PLANE, split_axis=0, concat_axis=0, tiled=True, axis_in...  24.4 us
    all_to_all x2, starting transfers between devices, exchange(): return lax.all_to_all(x, axes, split_axis=0, concat_axis=0, tiled=True)  22.2 us
    all_to_all x2, waiting for transfers between devices, exchange(): return lax.all_to_all(x, axes, split_axis=0, concat_axis=0, tiled=True)  16.6 us
    all_to_all x2, starting transfers between devices, exchange_lines(): lax.all_to_all(x, PLANE, split_axis=0, concat_axis=0, tiled=True, axis_in...  7.2 us
    pallas_call x1, Pallas kernels, on_device(): pl.pallas_call(expert_kernel, out_shape=shape_of(LINE, 2 * LINE, LINE * G...  6.15 us
    ppermute x1, waiting for transfers between devices, on_device(): lax.ppermute(jnp.concatenate([stream[0], routes], axis=0), turned, turn)  6.09 us
  transfers between devices with their start and end apart: 7, of which 6 were waited for; matrix products, arithmetic and copies ran while one was open for 1% of the time, Pallas kernels for 3%

profile of v8, /device:TPU:32, one launch (start us, length us, event | category | flops | bytes accessed | tf_op | source)
XLA Modules:
  0.0 189.1 jit_solution(16414962502041706087)
XLA Ops:
  0.0 1.4 broadcast_in_dim.12
  1.4 15.2 %all-to-all-start = ((bf16[16,32,256]{2,1,0:T(8,128)(2,1)}), bf16[16,32,256]{2,1,0:T(8,128)(2,1)S(1)}, u32[]{:S(2)}, u32[]{:S(2)}) async-start(bf16[16,32,256]{2,1,0:T(8,128)(2,1)} %broadcast_in_dim.12), calls=%async_computation | async-start | bytes 524288 | tf_op jit(solution)/shard_map/all_to_all | solution.py:49
  16.7 0.8 copy.13
  17.4 0.8 copy.14
  18.2 0.1 copy.17
  18.3 0.8 select_maximum_fusion
  19.0 2.9 %collective-permute-start = (f32[40,256]{1,0:T(8,128)S(1)}, f32[40,256]{1,0:T(8,128)S(1)}, u32[]{:S(2)}, u32[]{:S(2)}) collective-permute-start(f32[40,256]{1,0:T(8,128)S(1)} %select_maximum_fusion), channel_id=1, source_target_pairs={{0,0},{1,16},{2,32},{3,48},{4,64},{5,80},{6,96},{7,112},{8,128},{9... | collective-permute-start | bytes 122888 | tf_op jit(solution)/shard_map/ppermute | solution.py:247
  22.0 0.0 copy-start.1
  22.0 0.0 copy-start.3
  22.0 3.6 %shard_map.118.own_ref = bf16[576,4096]{1,0:T(8,128)(2,1)} custom-call(bf16[192,4096]{1,0:T(8,128)(2,1)} %bitcast.60, bf16[192,4096]{1,0:T(8,128)(2,1)} %bitcast.61, bf16[192,4096]{1,0:T(8,128)(2,1)} %bitcast.62), custom_call_target="tpu_custom_call" | custom-call | bytes 9437184 | tf_op jit(solution)/shard_map/pallas_call | solution.py:248
  25.6 0.0 copy-start.2
  25.6 6.1 %collective-permute-done.turned_ref = f32[40,256]{1,0:T(8,128)S(1)} collective-permute-done((f32[40,256]{1,0:T(8,128)S(1)}, f32[40,256]{1,0:T(8,128)S(1)}, u32[]{:S(2)}, u32[]{:S(2)}) %collective-permute-start) | collective-permute-done | bytes 40992 | tf_op jit(solution)/shard_map/ppermute | solution.py:247
  31.7 2.6 %all-to-all-done = bf16[16,32,256]{2,1,0:T(8,128)(2,1)S(1)} async-done(((bf16[16,32,256]{2,1,0:T(8,128)(2,1)}), bf16[16,32,256]{2,1,0:T(8,128)(2,1)S(1)}, u32[]{:S(2)}, u32[]{:S(2)}) %all-to-all-start) | async-done | bytes 262176 | tf_op jit(solution)/shard_map/all_to_all | solution.py:49
  34.4 1.9 %collective-permute-start.1 = (bf16[576,4096]{1,0:T(8,128)(2,1)}, bf16[576,4096]{1,0:T(8,128)(2,1)}, u32[]{:S(2)}, u32[]{:S(2)}) collective-permute-start(bf16[576,4096]{1,0:T(8,128)(2,1)} %shard_map.118.own_ref), channel_id=1, source_target_pairs={{0,256},{256,0},{1,257},{257,1},{2,258},{258,2},{3,259},{259,3},{4... | collective-permute-start | bytes 14155784 | tf_op jit(solution)/shard_map/ppermute | solution.py:259
  36.3 0.0 copy-done.1
  36.3 0.2 shard_map.119
  36.5 19.3 %all_to_all.40.parts_ref = bf16[16,32,256]{2,1,0:T(8,128)(2,1)S(1)} all-to-all(bf16[16,32,256]{2,1,0:T(8,128)(2,1)S(1)} %bitcast.55), channel_id=1, replica_groups=mesh['tok'=2,'head_0'=4,'head_1'=4,'exp'=16] {'head_0','head_1'}, dimensions={0} | all-to-all | bytes 524288 | tf_op jit(solution)/shard_map/all_to_all | solution.py:49
  55.8 0.3 shard_map.120
  56.1 25.0 %all_to_all.41.rows_ref = bf16[16,24,256]{2,1,0:T(8,128)(2,1)S(1)} all-to-all(bf16[16,24,256]{2,1,0:T(8,128)(2,1)S(1)} %bitcast.57), channel_id=1, replica_groups=mesh['tok'=2,'head_0'=4,'head_1'=4,'exp'=16] {'exp'}, dimensions={0} | all-to-all | bytes 393216 | tf_op jit(solution)/shard_map/all_to_all | solution.py:49
  81.1 0.0 copy-done.3
  81.1 1.1 shard_map.121
  82.1 3.5 %all-to-all-start.3 = ((bf16[4,24,4096]{2,1,0:T(8,128)(2,1)}), bf16[4,24,4096]{2,1,0:T(8,128)(2,1)S(1)}, u32[]{:S(2)}, u32[]{:S(2)}) async-start(bf16[4,24,4096]{2,1,0:T(8,128)(2,1)} %shard_map.121), calls=%async_computation.3 | async-start | bytes 1572864 | tf_op jit(solution)/shard_map/all_to_all | solution.py:228
  85.6 9.4 %all-to-all-done.3 = bf16[4,24,4096]{2,1,0:T(8,128)(2,1)S(1)} async-done(((bf16[4,24,4096]{2,1,0:T(8,128)(2,1)}), bf16[4,24,4096]{2,1,0:T(8,128)(2,1)S(1)}, u32[]{:S(2)}, u32[]{:S(2)}) %all-to-all-start.3) | async-done | bytes 786464 | tf_op jit(solution)/shard_map/all_to_all | solution.py:228
  95.1 0.0 collective-permute-done.1.other_ref
  95.1 0.0 copy-done.2
  95.1 2.0 %shard_map.122 = bf16[4,96,4096]{2,1,0:T(8,128)(2,1)} custom-call(s32[1]{0:T(128)} %bitcast.core_ref, bf16[96,4096]{1,0:T(8,128)(2,1)S(1)} %bitcast.52, bf16[2,96,96]{2,1,0:T(8,128)(2,1)S(1)} %copy-done.2), custom_call_target="tpu_custom_call" | custom-call | tf_op jit(solution)/shard_map/pallas_call | solution.py:280
  97.1 3.7 %all-to-all-start.4 = ((bf16[4,96,4096]{2,1,0:T(8,128)(2,1)}), bf16[4,96,4096]{2,1,0:T(8,128)(2,1)S(1)}, u32[]{:S(2)}, u32[]{:S(2)}) async-start(bf16[4,96,4096]{2,1,0:T(8,128)(2,1)} %shard_map.122), calls=%async_computation.4 | async-start | bytes 6291456 | tf_op jit(solution)/shard_map/all_to_all | solution.py:228
  100.8 2.9 %collective-permute-start.2 = (f32[32,256]{1,0:T(8,128)S(1)}, f32[32,256]{1,0:T(8,128)S(1)}, u32[]{:S(2)}, u32[]{:S(2)}) collective-permute-start(f32[32,256]{1,0:T(8,128)S(1)} %get-tuple-element.19), channel_id=1, source_target_pairs={{0,0},{1,16},{2,32},{3,48},{4,64},{5,80},{6,96},{7,112},{8,128},{9... | collective-permute-start | bytes 98312 | tf_op jit(solution)/shard_map/ppermute | solution.py:270
  103.7 4.2 %collective-permute-done.2.resid_ref = f32[32,256]{1,0:T(8,128)S(1)} collective-permute-done((f32[32,256]{1,0:T(8,128)S(1)}, f32[32,256]{1,0:T(8,128)S(1)}, u32[]{:S(2)}, u32[]{:S(2)}) %collective-permute-start.2) | collective-permute-done | bytes 32800 | tf_op jit(solution)/shard_map/ppermute | solution.py:270
  108.0 15.0 %all-to-all-done.4.rows_ref = bf16[4,96,4096]{2,1,0:T(8,128)(2,1)S(1)} async-done(((bf16[4,96,4096]{2,1,0:T(8,128)(2,1)}), bf16[4,96,4096]{2,1,0:T(8,128)(2,1)S(1)}, u32[]{:S(2)}, u32[]{:S(2)}) %all-to-all-start.4) | async-done | bytes 3145760 | tf_op jit(solution)/shard_map/all_to_all | solution.py:228
  122.9 6.1 %shard_map.123 = bf16[4,8,192,256]{3,2,1,0:T(8,128)(2,1)S(1)} custom-call(s32[1]{0:T(128)} %bitcast.core_ref, bf16[4,96,4096]{2,1,0:T(8,128)(2,1)S(1)} %all-to-all-done.4.rows_ref, bf16[576,4096]{1,0:T(8,128)(2,1)} %shard_map.118.own_ref, bf16[576,4096]{1,0:T(8,128)(2,1)} %collective-permute-done.1.other_ref), custom_call_target="tpu_custom_call" | custom-call | flops 2147483648 | bytes 16777216 | tf_op jit(solution)/shard_map/pallas_call | solution.py:293
  129.1 24.6 %all_to_all.42.parts_ref = bf16[4,8,192,256]{3,2,1,0:T(8,128)(2,1)S(1)} all-to-all(bf16[4,8,192,256]{3,2,1,0:T(8,128)(2,1)S(1)} %shard_map.123), channel_id=1, replica_groups={{0,16,32,48},{64,80,96,112},{128,144,160,176},{192,208,224,240},{256,32..., dimensions={0} | all-to-all | bytes 6291456 | tf_op jit(solution)/shard_map/all_to_all | solution.py:228
  153.7 0.0 copy-start
  153.7 0.0 copy-start.4
  153.7 0.4 shard_map.124
  154.1 12.1 %all_to_all.43.parts_ref = bf16[4,384,256]{2,1,0:T(8,128)(2,1)S(1)} all-to-all(bf16[4,384,256]{2,1,0:T(8,128)(2,1)S(1)} %bitcast.53), channel_id=1, replica_groups={{0,64,128,192},{16,80,144,208},{32,96,160,224},{48,112,176,240},{256,27..., dimensions={0} | all-to-all | bytes 1572864 | tf_op jit(solution)/shard_map/all_to_all | solution.py:228
  166.2 0.0 copy-done
  166.2 1.0 shard_map.125
  167.2 7.0 %all-to-all-start.7 = ((bf16[16,24,256]{2,1,0:T(8,128)(2,1)}), bf16[16,24,256]{2,1,0:T(8,128)(2,1)S(1)}, u32[]{:S(2)}, u32[]{:S(2)}) async-start(bf16[16,24,256]{2,1,0:T(8,128)(2,1)} %bitcast.15), calls=%async_computation.7 | async-start | bytes 393216 | tf_op jit(solution)/shard_map/all_to_all | solution.py:49
  174.2 0.0 copy-done.4
  174.2 0.1 copy.16
  174.2 13.9 %all-to-all-done.7 = bf16[16,24,256]{2,1,0:T(8,128)(2,1)S(1)} async-done(((bf16[16,24,256]{2,1,0:T(8,128)(2,1)}), bf16[16,24,256]{2,1,0:T(8,128)(2,1)S(1)}, u32[]{:S(2)}, u32[]{:S(2)}) %all-to-all-start.7) | async-done | bytes 196640 | tf_op jit(solution)/shard_map/all_to_all | solution.py:49
  188.2 0.9 shard_map.126
  (1 shorter events, 0.0 us)
Async XLA Ops:
  1.4 32.9 %all-to-all-start = ((bf16[16,32,256]{2,1,0:T(8,128)(2,1)}), bf16[16,32,256]{2,1,0:T(8,128)(2,1)S(1)}, u32[]{:S(2)}, u32[]{:S(2)}) async-start(bf16[16,32,256]{2,1,0:T(8,128)(2,1)} %broadcast_in_dim.12), calls=%async_computation | async-start | bytes 524288 | tf_op jit(solution)/shard_map/all_to_all | solution.py:49
  19.0 12.7 %collective-permute-start = (f32[40,256]{1,0:T(8,128)S(1)}, f32[40,256]{1,0:T(8,128)S(1)}, u32[]{:S(2)}, u32[]{:S(2)}) collective-permute-start(f32[40,256]{1,0:T(8,128)S(1)} %select_maximum_fusion), channel_id=1, source_target_pairs={{0,0},{1,16},{2,32},{3,48},{4,64},{5,80},{6,96},{7,112},{8,128},{9... | collective-permute-start | bytes 122888 | tf_op jit(solution)/shard_map/ppermute | solution.py:247
  22.0 14.3 %copy-start.1 = (bf16[256,256]{1,0:T(8,128)(2,1)S(1)}, bf16[256,256]{1,0:T(8,128)(2,1)}, u32[]{:S(2)}) copy-start(bf16[256,256]{1,0:T(8,128)(2,1)} %weight_ref.1) | copy-start | bytes 393220
  22.0 59.1 %copy-start.3 = (f32[4096]{0:T(1024)S(1)}, f32[4096]{0:T(1024)}, u32[]{:S(2)}) copy-start(f32[4096]{0:T(1024)} %param.15) | copy-start | bytes 49156
  25.6 69.5 %copy-start.2 = (bf16[2,96,96]{2,1,0:T(8,128)(2,1)S(1)}, bf16[2,96,96]{2,1,0:T(8,128)(2,1)}, u32[]{:S(2)}) copy-start(bf16[2,96,96]{2,1,0:T(8,128)(2,1)} %constant.37.clone.order_ref) | copy-start | bytes 110596
  34.4 60.7 %collective-permute-start.1 = (bf16[576,4096]{1,0:T(8,128)(2,1)}, bf16[576,4096]{1,0:T(8,128)(2,1)}, u32[]{:S(2)}, u32[]{:S(2)}) collective-permute-start(bf16[576,4096]{1,0:T(8,128)(2,1)} %shard_map.118.own_ref), channel_id=1, source_target_pairs={{0,256},{256,0},{1,257},{257,1},{2,258},{258,2},{3,259},{259,3},{4... | collective-permute-start | bytes 14155784 | tf_op jit(solution)/shard_map/ppermute | solution.py:259
  82.1 13.0 %all-to-all-start.3 = ((bf16[4,24,4096]{2,1,0:T(8,128)(2,1)}), bf16[4,24,4096]{2,1,0:T(8,128)(2,1)S(1)}, u32[]{:S(2)}, u32[]{:S(2)}) async-start(bf16[4,24,4096]{2,1,0:T(8,128)(2,1)} %shard_map.121), calls=%async_computation.3 | async-start | bytes 1572864 | tf_op jit(solution)/shard_map/all_to_all | solution.py:228
  97.1 25.8 %all-to-all-start.4 = ((bf16[4,96,4096]{2,1,0:T(8,128)(2,1)}), bf16[4,96,4096]{2,1,0:T(8,128)(2,1)S(1)}, u32[]{:S(2)}, u32[]{:S(2)}) async-start(bf16[4,96,4096]{2,1,0:T(8,128)(2,1)} %shard_map.122), calls=%async_computation.4 | async-start | bytes 6291456 | tf_op jit(solution)/shard_map/all_to_all | solution.py:228
  100.8 7.1 %collective-permute-start.2 = (f32[32,256]{1,0:T(8,128)S(1)}, f32[32,256]{1,0:T(8,128)S(1)}, u32[]{:S(2)}, u32[]{:S(2)}) collective-permute-start(f32[32,256]{1,0:T(8,128)S(1)} %get-tuple-element.19), channel_id=1, source_target_pairs={{0,0},{1,16},{2,32},{3,48},{4,64},{5,80},{6,96},{7,112},{8,128},{9... | collective-permute-start | bytes 98312 | tf_op jit(solution)/shard_map/ppermute | solution.py:270
  153.7 12.5 %copy-start = (bf16[2,384,384]{2,1,0:T(8,128)(2,1)S(1)}, bf16[2,384,384]{2,1,0:T(8,128)(2,1)}, u32[]{:S(2)}) copy-start(bf16[2,384,384]{2,1,0:T(8,128)(2,1)} %constant.38.clone.order_ref) | copy-start | bytes 1769476
  153.7 20.4 %copy-start.4 = (f32[1,32,8]{1,2,0:T(8,128)S(1)}, f32[1,32,8]{1,2,0:T(8,128)}, u32[]{:S(2)}) copy-start(f32[1,32,8]{1,2,0:T(8,128)} %param.18) | copy-start | bytes 3076
  167.2 21.0 %all-to-all-start.7 = ((bf16[16,24,256]{2,1,0:T(8,128)(2,1)}), bf16[16,24,256]{2,1,0:T(8,128)(2,1)S(1)}, u32[]{:S(2)}, u32[]{:S(2)}) async-start(bf16[16,24,256]{2,1,0:T(8,128)(2,1)} %bitcast.15), calls=%async_computation.7 | async-start | bytes 393216 | tf_op jit(solution)/shard_map/all_to_all | solution.py:49
